TPU v7x, 32 devices: a whole 2x2x4 slice. The times are simulated.
32 devices in a mesh: seq: 8 (over z, x), ctx: 4 (over y, core).
Axes of the slice: x: 2, y: 2, z: 4, core: 2. Of those that a mesh axis runs over, the one named last changes fastest.
Arguments:
- tokens: bfloat16 [16, 1024, 768], P('seq', 'ctx'), may hold values from -6 to 6
- prior_logits: bfloat16 [16, 12, 1024, 1024], P('seq', None, 'ctx'), may hold values from -6 to 6
- doc_ids: int32 [16, 1024], P('seq', 'ctx'), may hold values from 0 to 255, as said below
- w_query: bfloat16 [768, 768], P('seq'), may hold values from -0.21875 to 0.21875
- w_key: bfloat16 [768, 768], P('seq'), may hold values from -0.21875 to 0.21875
- w_value: bfloat16 [768, 768], P('seq'), may hold values from -0.21875 to 0.21875
- w_out: bfloat16 [768, 768], P('seq'), may hold values from -0.875 to 0.875
- b_query: bfloat16 [768], P('seq'), may hold values from -3 to 3
- b_value: bfloat16 [768], P('seq'), may hold values from -3 to 3
- b_out: bfloat16 [768], P('seq'), may hold values from -3 to 3
- first_norm_gain: bfloat16 [768], P('seq'), may hold values from 0.5 to 1.5
- norm1_shift: bfloat16 [768], P('seq'), may hold values from -3 to 3
- w_in: bfloat16 [768, 3072], P('seq'), may hold values from -0.21875 to 0.21875
- b_in: bfloat16 [3072], P('seq'), may hold values from -3 to 3
- w_down: bfloat16 [3072, 768], P('seq'), may hold values from -0.109375 to 0.109375
- b_down: bfloat16 [768], P('seq'), may hold values from -3 to 3
- norm2_gain: bfloat16 [768], P('seq'), may hold values from 0.5 to 1.5
- norm2_shift: bfloat16 [768], P('seq'), may hold values from -3 to 3
- cotangent: bfloat16 [16, 1024, 768], P('seq', 'ctx'), may hold values from -6 to 6
Outputs:
- output: bfloat16 [16, 1024, 768], P('seq', 'ctx')
- raw_logits: bfloat16 [16, 12, 1024, 1024], P('seq', None, 'ctx')
- grad_tokens: float32 [16, 1024, 768], P('seq', 'ctx')
- grad_prior: bfloat16 [16, 12, 1024, 1024], P('seq', None, 'ctx')
- grad_w_query: float32 [768, 768], P('seq')
- grad_w_key: float32 [768, 768], P('seq')
- grad_w_value: float32 [768, 768], P('seq')
- grad_w_out: float32 [768, 768], P('seq')
- grad_b_query: float32 [768], P('seq')
- grad_b_value: float32 [768], P('seq')
- grad_b_out: float32 [768], P('seq')
- grad_norm1_gain: float32 [768], P('seq')
- grad_norm1_shift: float32 [768], P('seq')
- grad_w_in: float32 [768, 3072], P('seq')
- grad_b_in: float32 [3072], P('seq')
- grad_w_down: float32 [3072, 768], P('seq')
- grad_b_down: float32 [768], P('seq')
- grad_norm2_gain: float32 [768], P('seq')
- grad_norm2_shift: float32 [768], P('seq')
Inputs may be any that keep to these rules, and one draw needn't show every extreme that they name: `doc_ids`: in every sequence the document numbers start at 0 and rise by 0 or 1 from one token to the next, up to at most 255, which the first sequence reaches. In each aligned group of 2 sequences, one sequence has a document holding a token of its first 256 tokens and one of its last 256 tokens.
All inputs are finite; a program needn't handle non-finite values.
Results may differ from a plain program's by a relative error of at most 0.013.
Values may be sent and summed in bfloat16 or wider, within the bound.
No kernel may reach another device: no remote copies, remote signals or barrier semaphores. Data moves between devices by JAX's collectives and lax.ppermute only.
A program may use at most 256 MiB of HBM per device.

v0:
```python
from functools import partial
import math

import jax
import jax.numpy as jnp
from jax import lax
from jax.sharding import PartitionSpec as P

EPSILON = 1e-05
NEGATIVE = -1e30


def norm_rows(hidden_in, scales, shifts):
    row_mean = jnp.mean(hidden_in, -1, keepdims=True)
    centered = hidden_in - row_mean
    inverse = lax.rsqrt(jnp.mean(centered * centered, -1, keepdims=True) + EPSILON)
    normed = centered * inverse
    return (normed * scales + shifts, normed, inverse)


def norm_back(grad_out, normed, inverse, scales):
    scaled = grad_out * scales
    return inverse * (
        scaled
        - jnp.mean(scaled, -1, keepdims=True)
        - normed * jnp.mean(scaled * normed, -1, keepdims=True)
    )


def matmul(first_op, second_op):
    return jnp.dot(first_op, second_op, preferred_element_type=jnp.float32)


def matmul_tn(first_op, second_op):
    return lax.dot_general(
        first_op, second_op, (((0,), (0,)), ((), ())), preferred_element_type=jnp.float32
    )


def matmul_nt(first_op, second_op):
    return lax.dot_general(
        first_op, second_op, (((1,), (1,)), ((), ())), preferred_element_type=jnp.float32
    )


def score_block(query_heads, key_heads, priors, doc_ids, all_docs, score_scale):
    raw_logits = jnp.einsum(
        "sqhe,skhe->shqk", query_heads, key_heads, preferred_element_type=jnp.float32
    ) * score_scale + priors.astype(jnp.float32)
    same_doc = doc_ids[:, None, :, None] == all_docs[:, None, None, :]
    return (raw_logits, jnp.where(same_doc, raw_logits, NEGATIVE))


def column_sum(grad_rows):
    return jnp.sum(grad_rows.astype(jnp.float32), 0)


def on_device(
    tokens,
    prior_logits,
    doc_ids,
    w_query,
    w_key,
    w_value,
    w_out,
    b_query,
    b_value,
    b_out,
    first_norm_gain,
    norm1_shift,
    w_in,
    b_in,
    w_down,
    b_down,
    norm2_gain,
    norm2_shift,
    cotangent,
):
    seq_dev, shard, width = tokens.shape
    rows_dev = seq_dev * shard
    heads = prior_logits.shape[1]
    head_dim = width // heads
    score_scale = 1.0 / math.sqrt(head_dim)
    full = (
        lax.all_gather(w_query, "seq", axis=0, tiled=True),
        lax.all_gather(w_key, "seq", axis=0, tiled=True),
        lax.all_gather(w_value, "seq", axis=0, tiled=True),
        lax.all_gather(w_out, "seq", axis=0, tiled=True),
        lax.all_gather(w_in, "seq", axis=0, tiled=True),
        lax.all_gather(w_down, "seq", axis=0, tiled=True),
        lax.all_gather(b_query, "seq", axis=0, tiled=True),
        lax.all_gather(b_value, "seq", axis=0, tiled=True),
        lax.all_gather(b_out, "seq", axis=0, tiled=True),
        lax.all_gather(b_in, "seq", axis=0, tiled=True),
        lax.all_gather(b_down, "seq", axis=0, tiled=True),
        lax.all_gather(first_norm_gain, "seq", axis=0, tiled=True),
        lax.all_gather(norm1_shift, "seq", axis=0, tiled=True),
        lax.all_gather(norm2_gain, "seq", axis=0, tiled=True),
        lax.all_gather(norm2_shift, "seq", axis=0, tiled=True),
    )
    weight_q, weight_k, weight_v, weight_o, weight_i, weight_d = (
        full[0],
        full[1],
        full[2],
        full[3],
        full[4],
        full[5],
    )
    bias_q, bias_v, bias_o, bias_i, bias_d, gain_one, shift_one, second_norm_gain, shift_two = [
        vector.astype(jnp.float32) for vector in full[6:]
    ]
    inputs = tokens.reshape(rows_dev, width)
    queries = (matmul(inputs, weight_q) + bias_q).astype(jnp.bfloat16)
    keys_own = matmul(inputs, weight_k).astype(jnp.bfloat16).reshape(seq_dev, shard, width)
    values_own = (
        (matmul(inputs, weight_v) + bias_v).astype(jnp.bfloat16).reshape(seq_dev, shard, width)
    )
    all_docs = lax.all_gather(doc_ids, "ctx", axis=1, tiled=True)
    length = all_docs.shape[1]
    key_value = (
        lax.all_gather(keys_own, "ctx", axis=1, tiled=True),
        lax.all_gather(values_own, "ctx", axis=1, tiled=True),
    )
    query_heads = queries.reshape(seq_dev, shard, heads, head_dim)
    key_heads = key_value[0].reshape(seq_dev, length, heads, head_dim)
    value_heads = key_value[1].reshape(seq_dev, length, heads, head_dim)
    raw_logits, masked = score_block(
        query_heads, key_heads, prior_logits, doc_ids, all_docs, score_scale
    )
    row_max = jnp.max(masked, -1, keepdims=True)
    exp_terms = jnp.exp(masked - row_max)
    row_total = jnp.sum(exp_terms, -1, keepdims=True)
    probs_low = (exp_terms / row_total).astype(jnp.bfloat16)
    log_total = row_max + jnp.log(row_total)
    mixed = jnp.einsum(
        "shqk,skhe->sqhe", probs_low, value_heads, preferred_element_type=jnp.float32
    )
    mixed = mixed.reshape(rows_dev, width).astype(jnp.bfloat16)
    branch = matmul(mixed, weight_o) + bias_o
    first, normed_one, inverse_one = norm_rows(
        inputs.astype(jnp.float32) + branch, gain_one, shift_one
    )
    inner = first.astype(jnp.bfloat16)
    pre_act = matmul(inner, weight_i) + bias_i
    hidden = jax.nn.gelu(pre_act, approximate=False).astype(jnp.bfloat16)
    second = matmul(hidden, weight_d) + bias_d
    output, normed_two, inverse_two = norm_rows(first + second, second_norm_gain, shift_two)
    back = (
        lax.all_gather(w_query, "seq", axis=0, tiled=True),
        lax.all_gather(w_key, "seq", axis=0, tiled=True),
        lax.all_gather(w_value, "seq", axis=0, tiled=True),
        lax.all_gather(w_out, "seq", axis=0, tiled=True),
        lax.all_gather(w_in, "seq", axis=0, tiled=True),
        lax.all_gather(w_down, "seq", axis=0, tiled=True),
    )
    back_q, back_k, back_v, back_o, back_i, back_d = (
        back[0],
        back[1],
        back[2],
        back[3],
        back[4],
        back[5],
    )
    grad_out = cotangent.reshape(rows_dev, width).astype(jnp.float32)
    grad_gain_two = jnp.sum(grad_out * normed_two, 0)
    grad_shift_two = jnp.sum(grad_out, 0)
    grad_sum_two = norm_back(grad_out, normed_two, inverse_two, second_norm_gain)
    grad_second = grad_sum_two.astype(jnp.bfloat16)
    grad_down_bias = column_sum(grad_second)
    grad_weight_d = matmul_tn(hidden, grad_second)
    grad_hidden = matmul_nt(grad_second, back_d)
    gelu_backprop = jax.vjp(partial(jax.nn.gelu, approximate=False), pre_act)[1]
    grad_pre = gelu_backprop(grad_hidden)[0].astype(jnp.bfloat16)
    grad_bias_i = column_sum(grad_pre)
    grad_weight_i = matmul_tn(inner, grad_pre)
    grad_first = grad_sum_two + matmul_nt(grad_pre, back_i)
    grad_gain_one = jnp.sum(grad_first * normed_one, 0)
    grad_shift_one = jnp.sum(grad_first, 0)
    grad_sum_one = norm_back(grad_first, normed_one, inverse_one, gain_one)
    grad_branch = grad_sum_one.astype(jnp.bfloat16)
    grad_bias_o = column_sum(grad_branch)
    grad_weight_o = matmul_tn(mixed, grad_branch)
    grad_mixed = (
        matmul_nt(grad_branch, back_o).astype(jnp.bfloat16).reshape(seq_dev, shard, heads, head_dim)
    )
    key_value_back = (
        lax.all_gather(keys_own, "ctx", axis=1, tiled=True),
        lax.all_gather(values_own, "ctx", axis=1, tiled=True),
    )
    key_back = key_value_back[0].reshape(seq_dev, length, heads, head_dim)
    value_back = key_value_back[1].reshape(seq_dev, length, heads, head_dim)
    raw_again, masked_again = score_block(
        query_heads, key_back, prior_logits, doc_ids, all_docs, score_scale
    )
    probs = jnp.exp(masked_again - log_total)
    probs_back = probs.astype(jnp.bfloat16)
    grad_probs = jnp.einsum(
        "sqhe,skhe->shqk", grad_mixed, value_back, preferred_element_type=jnp.float32
    )
    grad_raw = (probs * (grad_probs - jnp.sum(probs * grad_probs, -1, keepdims=True))).astype(
        jnp.bfloat16
    )
    grad_query = (
        jnp.einsum("shqk,skhe->sqhe", grad_raw, key_back, preferred_element_type=jnp.float32)
        * score_scale
    )
    grad_query = grad_query.reshape(rows_dev, width).astype(jnp.bfloat16)
    key_term = (
        jnp.einsum("shqk,sqhe->skhe", grad_raw, query_heads, preferred_element_type=jnp.float32)
        * score_scale
    )
    value_term = jnp.einsum(
        "shqk,sqhe->skhe", probs_back, grad_mixed, preferred_element_type=jnp.float32
    )
    key_part, value_part = (
        lax.psum_scatter(
            key_term.reshape(seq_dev, length, width), "ctx", scatter_dimension=1, tiled=True
        ),
        lax.psum_scatter(
            value_term.reshape(seq_dev, length, width), "ctx", scatter_dimension=1, tiled=True
        ),
    )
    grad_key = key_part.reshape(rows_dev, width).astype(jnp.bfloat16)
    grad_value = value_part.reshape(rows_dev, width).astype(jnp.bfloat16)
    grad_weight_q = matmul_tn(inputs, grad_query)
    grad_bias_q = column_sum(grad_query)
    grad_weight_k = matmul_tn(inputs, grad_key)
    grad_weight_v = matmul_tn(inputs, grad_value)
    grad_bias_v = column_sum(grad_value)
    grad_inputs = (
        grad_sum_one
        + matmul_nt(grad_query, back_q)
        + matmul_nt(grad_key, back_k)
        + matmul_nt(grad_value, back_v)
    )
    shard_sums = (
        lax.psum_scatter(grad_weight_q, "seq", scatter_dimension=0, tiled=True),
        lax.psum_scatter(grad_weight_k, "seq", scatter_dimension=0, tiled=True),
        lax.psum_scatter(grad_weight_v, "seq", scatter_dimension=0, tiled=True),
        lax.psum_scatter(grad_weight_o, "seq", scatter_dimension=0, tiled=True),
        lax.psum_scatter(grad_bias_q, "seq", scatter_dimension=0, tiled=True),
        lax.psum_scatter(grad_bias_v, "seq", scatter_dimension=0, tiled=True),
        lax.psum_scatter(grad_bias_o, "seq", scatter_dimension=0, tiled=True),
        lax.psum_scatter(grad_gain_one, "seq", scatter_dimension=0, tiled=True),
        lax.psum_scatter(grad_shift_one, "seq", scatter_dimension=0, tiled=True),
        lax.psum_scatter(grad_weight_i, "seq", scatter_dimension=0, tiled=True),
        lax.psum_scatter(grad_bias_i, "seq", scatter_dimension=0, tiled=True),
        lax.psum_scatter(grad_weight_d, "seq", scatter_dimension=0, tiled=True),
        lax.psum_scatter(grad_down_bias, "seq", scatter_dimension=0, tiled=True),
        lax.psum_scatter(grad_gain_two, "seq", scatter_dimension=0, tiled=True),
        lax.psum_scatter(grad_shift_two, "seq", scatter_dimension=0, tiled=True),
    )
    totals = lax.psum(
        (
            shard_sums[0],
            shard_sums[1],
            shard_sums[2],
            shard_sums[3],
            shard_sums[4],
            shard_sums[5],
            shard_sums[6],
            shard_sums[7],
            shard_sums[8],
            shard_sums[9],
            shard_sums[10],
            shard_sums[11],
            shard_sums[12],
            shard_sums[13],
            shard_sums[14],
        ),
        "ctx",
    )
    return (
        output.reshape(seq_dev, shard, width).astype(jnp.bfloat16),
        raw_logits.astype(jnp.bfloat16),
        grad_inputs.reshape(seq_dev, shard, width),
        grad_raw,
        totals[0],
        totals[1],
        totals[2],
        totals[3],
        totals[4],
        totals[5],
        totals[6],
        totals[7],
        totals[8],
        totals[9],
        totals[10],
        totals[11],
        totals[12],
        totals[13],
        totals[14],
    )


def solution(mesh):
    in_specs = (
        P("seq", "ctx", None),
        P("seq", None, "ctx", None),
        P("seq", "ctx"),
        P("seq", None),
        P("seq", None),
        P("seq", None),
        P("seq", None),
        P("seq"),
        P("seq"),
        P("seq"),
        P("seq"),
        P("seq"),
        P("seq", None),
        P("seq"),
        P("seq", None),
        P("seq"),
        P("seq"),
        P("seq"),
        P("seq", "ctx", None),
    )
    out_specs = (
        P("seq", "ctx", None),
        P("seq", None, "ctx", None),
        P("seq", "ctx", None),
        P("seq", None, "ctx", None),
        P("seq", None),
        P("seq", None),
        P("seq", None),
        P("seq", None),
        P("seq"),
        P("seq"),
        P("seq"),
        P("seq"),
        P("seq"),
        P("seq", None),
        P("seq"),
        P("seq", None),
        P("seq"),
        P("seq"),
        P("seq"),
    )
    return jax.shard_map(
        on_device, mesh=mesh, in_specs=in_specs, out_specs=out_specs, check_vma=False
    )
```

profile of v0, /device:TPU:0, one launch (start us, length us, event | category | flops | bytes accessed | tf_op | source)
XLA Modules:
  0.0 1290.1 jit_solution(634227860752482469)
XLA Ops:
  9.6 44.5 %all-gather.16.cloned.1.call-done = bf16[768,768]{1,0:T(8,128)(2,1)} async-done(((bf16[96,768]{1,0:T(8,128)(2,1)}), bf16[768,768]{1,0:T(8,128)(2,1)}) %all-gather.16.cloned.1.call-update) | async-done | bytes 1179664 | tf_op jit(solution)/shard_map/all_gather | solution.py:86
  54.1 3.2 convolution_convert_fusion.1
  60.5 35.5 %all-reduce.20 = (bf16[768]{0:T(1024)(128)(2,1)S(1)}, bf16[768]{0:T(1024)(128)(2,1)S(1)}, bf16[768]{0:T(1024)(128)(2,1)S(1)}, bf16[768]{0:T(1024)(128)(2,1)S(1)}...) all-reduce(bf16[768]{0:T(1024)(128)(2,1)S(1)} %dynamic-update-slice, ...), channel_id=1, replica_groups=mesh['seq'=8,'ctx'=4] {'seq'}, use_global_device_ids=true, to_apply=%add | all-reduce | flops 6144 | bytes 24576
  96.4 2.9 add_convert_fusion.3
  102.5 5.1 all_gather.65
  107.6 26.1 %all-gather = bf16[8,1,384]{2,1,0:T(2,128)(2,1)S(1)} all-gather(bf16[1,1,384]{2,1,0:T(2,128)(2,1)S(1)} %reshape.200), channel_id=1, replica_groups=mesh['seq'=8,'ctx'=4] {'seq'}, dimensions={0}, use_global_device_ids=true | all-gather | bytes 6912 | tf_op jit(solution)/shard_map/all_gather | solution.py:94
  134.9 3.6 all-gather.14.cloned.1.call-done
  138.4 2.0 add_convert_fusion.2
  141.8 25.9 %all-gather.18.cloned.1.call-done = bf16[2,1024,768]{2,1,0:T(8,128)(2,1)} async-done(((bf16[2,256,768]{2,1,0:T(8,128)(2,1)}), bf16[2,1024,768]{2,1,0:T(8,128)(2,1)}) %all-gather.18.cloned.1.call-update) | async-done | bytes 3145744 | tf_op jit(solution)/shard_map/all_gather | solution.py:121
  167.8 3.3 copy.66
  171.1 16.2 %select_reduce_fusion = (f32[2,12,256]{2,1,0:T(8,128)S(1)}, f32[2,12,256,1024]{3,2,1,0:T(8,128)}) fusion(pred[2,256,1024]{2,1,0:T(8,128)(4,1)} %broadcast_compare_fusion, bf16[2,12,256,1024]{3,2,1,0:T(8,128)(2,1)} %param.20, bf16[2,1024,12,64]{1,3,2,0:T(8,128)(2,1)S(1)} %bitcast.105, bf16[2,256,12,64]{1,0,3,2:T(2,128)(2,1)} %reshape.168), kind=kOutput, calls=%fused_computation.7 | convolution fusion | flops 836757504 | bytes 42229760 | tf_op jit(solution)/shard_map/sqhe,skhe->shqk/dot_general | solution.py:47
  187.3 11.5 fusion
  198.9 4.7 copy.64
  203.6 12.3 fusion.24
  216.9 24.5 %all-gather.20.cloned.1.call-done = bf16[768,768]{1,0:T(8,128)(2,1)} async-done(((bf16[96,768]{1,0:T(8,128)(2,1)}), bf16[768,768]{1,0:T(8,128)(2,1)}) %all-gather.20.cloned.1.call-update) | async-done | bytes 1179664 | tf_op jit(solution)/shard_map/all_gather | solution.py:88
  241.4 2.4 fusion.48
  244.2 78.1 %all-gather.22.cloned.1.call-done = bf16[768,3072]{1,0:T(8,128)(2,1)} async-done(((bf16[96,3072]{1,0:T(8,128)(2,1)}), bf16[768,3072]{1,0:T(8,128)(2,1)}) %all-gather.22.cloned.1.call-update) | async-done | bytes 4718608 | tf_op jit(solution)/shard_map/all_gather | solution.py:89
  322.3 19.9 %multiply_convert_fusion.1 = (bf16[512,3072]{1,0:T(8,128)(2,1)}, f32[512,3072]{1,0:T(8,128)}, f32[512,3072]{1,0:T(8,128)}) fusion(f32[3072]{0:T(1024)S(1)} %bitcast.127, bf16[768,3072]{1,0:T(8,128)(2,1)} %all-gather.22.cloned.1.call-done, f32[512,768]{1,0:T(8,128)S(1)} %get-tuple-element.132, f32[768]{0:T(1024)S(1)} %convert_element_type.155, ...), kind=kOutput, calls=%fused_computation.18 | convolution fusion | flops 2521694208 | bytes 22042624 | tf_op jit(solution)/shard_map/dot_general | solution.py:31
  342.2 60.4 %all-gather.24.cloned.1.call-done = bf16[3072,768]{1,0:T(8,128)(2,1)} async-done(((bf16[384,768]{1,0:T(8,128)(2,1)}), bf16[3072,768]{1,0:T(8,128)(2,1)}) %all-gather.24.cloned.1.call-update) | async-done | bytes 4718608 | tf_op jit(solution)/shard_map/all_gather | solution.py:90
  402.5 6.1 fusion.49
  411.3 10.2 convert_reduce_fusion
  421.6 5.0 multiply_reduce_fusion.1
  429.6 12.5 fusion.2
  442.2 6.6 copy.75
  448.8 22.0 %multiply_reduce_fusion = (f32[2,12,256]{2,1,0:T(8,128)S(1)}, f32[2,12,256,1024]{3,2,1,0:T(8,128)}) fusion(f32[2,12,256,1024]{3,2,1,0:T(8,128)} %get-tuple-element.130, f32[2,12,256]{2,1,0:T(8,128)S(1)} %log_add_fusion, pred[2,256,1024]{2,1,0:T(8,128)(4,1)S(1)} %copy-done.4, bf16[2,1024,12,64]{1,3,2,0:T(8,128)(2,1)} %bitcast.109, ...), kind=kOutput, calls=%fused_computation.1 | convolution fusion | flops 830466048 | bytes 54837248 | tf_op jit(solution)/shard_map/sqhe,skhe->shqk/dot_general | solution.py:197
  470.8 31.5 %multiply_convert_fusion = (bf16[2,12,256,1024]{3,2,1,0:T(8,128)(2,1)S(1)}, bf16[2,12,256,1024]{3,2,1,0:T(8,128)(2,1)}) fusion(f32[2,12,256,1024]{3,2,1,0:T(8,128)} %get-tuple-element.138, f32[2,12,256,1024]{3,2,1,0:T(8,128)} %get-tuple-element.130, f32[2,12,256]{2,1,0:T(8,128)S(1)} %get-tuple-element.137, f32[2,12,256]{2,1,0:T(8,128)S(1)} %log_add_fusion, ...), kind=kLoop, calls=%fused_computation | loop fusion | flops 37748736 | bytes 76070912 | tf_op jit(solution)/shard_map/convert_element_type | solution.py:200
  502.3 5.5 broadcast_multiply_fusion
  509.0 6.6 copy.73
  517.4 10.1 convert_reduce_fusion.5
  530.2 2.2 copy.83
  537.8 34.9 %reduce-scatter.15.cloned.1.call-done = f32[2,256,768]{2,1,0:T(8,128)} async-done(((f32[2,1024,768]{2,1,0:T(8,128)}), f32[2,256,768]{2,1,0:T(8,128)}) %reduce-scatter.15.cloned.1.call-update) | async-done | bytes 1572880 | tf_op jit(solution)/shard_map/reduce_scatter | solution.py:216
  575.1 2.2 convolution_bitcast_fusion.1
  577.3 3.3 copy.85
  580.7 3.4 fusion.30
  584.2 7.2 fusion.41
  592.8 8.3 fusion.33
  601.1 44.0 %reduce-scatter.25.cloned.1.call-done = f32[96,768]{1,0:T(8,128)} async-done(((f32[768,768]{1,0:T(8,128)}), f32[96,768]{1,0:T(8,128)}) %reduce-scatter.25.cloned.1.call-update) | async-done | bytes 294928
  647.1 69.6 %reduce-scatter.29.cloned.1.call-done = f32[96,768]{1,0:T(8,128)} async-done(((f32[768,768]{1,0:T(8,128)}), f32[96,768]{1,0:T(8,128)}) %reduce-scatter.29.cloned.1.call-update) | async-done | bytes 294928
  718.6 69.7 %reduce-scatter.27.cloned.1.call-done = f32[96,768]{1,0:T(8,128)} async-done(((f32[768,768]{1,0:T(8,128)}), f32[96,768]{1,0:T(8,128)}) %reduce-scatter.27.cloned.1.call-update) | async-done | bytes 294928
  790.2 69.3 %reduce-scatter.19.cloned.1.call-done = f32[96,768]{1,0:T(8,128)} async-done(((f32[768,768]{1,0:T(8,128)}), f32[96,768]{1,0:T(8,128)}) %reduce-scatter.19.cloned.1.call-update) | async-done | bytes 294928 | tf_op jit(solution)/shard_map/reduce_scatter | solution.py:240
  859.5 166.0 %reduce-scatter.21.cloned.1.call-done = f32[96,3072]{1,0:T(8,128)} async-done(((f32[768,3072]{1,0:T(8,128)}), f32[96,3072]{1,0:T(8,128)}) %reduce-scatter.21.cloned.1.call-update) | async-done | bytes 1179664 | tf_op jit(solution)/shard_map/reduce_scatter | solution.py:246
  1025.5 166.0 %reduce-scatter.23.cloned.1.call-done = f32[384,768]{1,0:T(8,128)} async-done(((f32[3072,768]{1,0:T(8,128)}), f32[384,768]{1,0:T(8,128)}) %reduce-scatter.23.cloned.1.call-update) | async-done | bytes 1179664 | tf_op jit(solution)/shard_map/reduce_scatter | solution.py:248
  1192.9 3.3 fusion.50
  1196.2 35.6 %all-reduce.17 = (f32[768]{0:T(1024)S(1)}, f32[768]{0:T(1024)S(1)}, f32[768]{0:T(1024)S(1)}, f32[768]{0:T(1024)S(1)}, f32[768]{0:T(1024)S(1)}, /*index=5*/f32[30...) all-reduce(f32[768]{0:T(1024)S(1)} %reduce_sum.184, ...), channel_id=8, replica_groups=mesh['seq'=8,'ctx'=4] {'seq'}, use_global_device_ids=true, to_apply=%region_22.23.clone | all-reduce | flops 9216 | bytes 73728
  1232.5 6.3 all-reduce.18
  1238.8 2.6 fusion.51
  1241.4 3.4 add_add_fusion
  1244.9 29.0 %all-reduce.23.cloned.1.call-done = (f32[96,768]{0,1:T(8,128)}, f32[96,768]{0,1:T(8,128)}, f32[96,768]{0,1:T(8,128)}, f32[96,768]{1,0:T(8,128)}, f32[96,3072]{1,0:T(8,128)}, /*index=5*/f32[384,768]{1,0:T(8,128)}) async-done(((f32[96,768]{0,1:T(8,128)}, f32[96,768]{0,1:T(8,128)}, f32[96,768]{0,1:T(8,128)}, f32[96,768]{1,0:T(8,128)}, f32[96,3072]{1,0:T(8,128)}, /*index=5*/f32[384,768]{1,0:T(8,128)}), ...) | async-done | bytes 3538960 | tf_op jit(solution)/shard_map/psum | solution.py:253
  (196 shorter events, 48.7 us)
Async XLA Ops:
  7.2 50.2 %copy-start.27 = (u32[32]{0:T(128)S(1)}, u32[32]{0:T(128)}, u32[]{:S(2)}) copy-start(u32[32]{0:T(128)} %constant.89) | copy-start | bytes 388
  7.2 89.2 %copy-start.23 = (bf16[2,256,768]{2,1,0:T(8,128)(2,1)S(1)}, bf16[2,256,768]{2,1,0:T(8,128)(2,1)}, u32[]{:S(2)}) copy-start(bf16[2,256,768]{2,1,0:T(8,128)(2,1)} %param.19) | copy-start | bytes 2359300
  7.2 51.4 %copy-start.31 = (bf16[96]{0:T(256)(128)(2,1)S(1)}, bf16[96]{0:T(256)(128)(2,1)}, u32[]{:S(2)}) copy-start(bf16[96]{0:T(256)(128)(2,1)} %param.36) | copy-start | bytes 580
  7.2 51.6 %copy-start.32 = (bf16[96]{0:T(256)(128)(2,1)S(1)}, bf16[96]{0:T(256)(128)(2,1)}, u32[]{:S(2)}) copy-start(bf16[96]{0:T(256)(128)(2,1)} %param.34) | copy-start | bytes 580
  7.2 51.9 %copy-start.33 = (bf16[96]{0:T(256)(128)(2,1)S(1)}, bf16[96]{0:T(256)(128)(2,1)}, u32[]{:S(2)}) copy-start(bf16[96]{0:T(256)(128)(2,1)} %param.29) | copy-start | bytes 580
  7.2 52.1 %copy-start.34 = (bf16[96]{0:T(256)(128)(2,1)S(1)}, bf16[96]{0:T(256)(128)(2,1)}, u32[]{:S(2)}) copy-start(bf16[96]{0:T(256)(128)(2,1)} %param.30) | copy-start | bytes 580
  7.3 52.3 %copy-start.35 = (bf16[96]{0:T(256)(128)(2,1)S(1)}, bf16[96]{0:T(256)(128)(2,1)}, u32[]{:S(2)}) copy-start(bf16[96]{0:T(256)(128)(2,1)} %param.28) | copy-start | bytes 580
  7.3 52.5 %copy-start.36 = (bf16[96]{0:T(256)(128)(2,1)S(1)}, bf16[96]{0:T(256)(128)(2,1)}, u32[]{:S(2)}) copy-start(bf16[96]{0:T(256)(128)(2,1)} %param.26) | copy-start | bytes 580
  7.3 52.8 %copy-start.37 = (bf16[96]{0:T(256)(128)(2,1)S(1)}, bf16[96]{0:T(256)(128)(2,1)}, u32[]{:S(2)}) copy-start(bf16[96]{0:T(256)(128)(2,1)} %param.27) | copy-start | bytes 580
  7.3 53.0 %copy-start.38 = (bf16[96]{0:T(256)(128)(2,1)S(1)}, bf16[96]{0:T(256)(128)(2,1)}, u32[]{:S(2)}) copy-start(bf16[96]{0:T(256)(128)(2,1)} %param.35) | copy-start | bytes 580
  7.3 46.8 %all-gather.16.cloned.1.call-start = ((), (), s32[]{:S(2)}) async-start(), calls=%async_computation.11 | async-start | bytes 1327104 | tf_op jit(solution)/shard_map/all_gather | solution.py:86
  8.0 88.3 %all-gather.10.cloned.1.call-start = ((), (), s32[]{:S(2)}) async-start(), calls=%async_computation.8 | async-start | bytes 1327104 | tf_op jit(solution)/shard_map/all_gather | solution.py:87
  8.8 129.6 %all-gather.14.cloned.1.call-start = ((), (), s32[]{:S(2)}) async-start(), calls=%async_computation.10 | async-start | bytes 1327104 | tf_op jit(solution)/shard_map/all_gather | solution.py:85
  9.5 158.2 %all-gather.18.cloned.1.call-start = ((), (), s32[]{:S(2)}) async-start(), calls=%async_computation.12 | async-start | bytes 3932160 | tf_op jit(solution)/shard_map/all_gather | solution.py:121
  57.3 141.6 %all-gather.12.cloned.1.call-start = ((), (), s32[]{:S(2)}) async-start(), calls=%async_computation.9 | async-start | bytes 3932160 | tf_op jit(solution)/shard_map/all_gather | solution.py:122
  96.0 5.5 copy-start.28
  96.0 5.6 copy-start.8
  96.0 6.5 copy-start.26
  99.3 142.1 %all-gather.20.cloned.1.call-start = ((), (), s32[]{:S(2)}) async-start(), calls=%async_computation.13 | async-start | bytes 1327104 | tf_op jit(solution)/shard_map/all_gather | solution.py:88
  99.9 222.4 %all-gather.22.cloned.1.call-start = ((), (), s32[]{:S(2)}) async-start(), calls=%async_computation.14 | async-start | bytes 5308416 | tf_op jit(solution)/shard_map/all_gather | solution.py:89
  100.7 301.9 %all-gather.24.cloned.1.call-start = ((), (), s32[]{:S(2)}) async-start(), calls=%async_computation.15 | async-start | bytes 5308416 | tf_op jit(solution)/shard_map/all_gather | solution.py:90
  101.4 431.1 %reduce-scatter.17.cloned.1.call-start = ((), (), s32[]{:S(2)}) async-start(), calls=%async_computation.17 | async-start | bytes 7864320 | tf_op jit(solution)/shard_map/reduce_scatter | solution.py:219
  171.1 16.2 %copy-start.1 = (bf16[2,1024,768]{1,2,0:T(8,128)(2,1)}, bf16[2,1024,768]{1,2,0:T(8,128)(2,1)S(1)}, u32[]{:S(2)}) copy-start(bf16[2,1024,768]{1,2,0:T(8,128)(2,1)S(1)} %copy.66) | copy-start | bytes 9437188
  171.1 16.2 %copy-start.3 = (pred[2,256,1024]{2,1,0:T(8,128)(4,1)S(1)}, pred[2,256,1024]{2,1,0:T(8,128)(4,1)}, u32[]{:S(2)}) copy-start(pred[2,256,1024]{2,1,0:T(8,128)(4,1)} %broadcast_compare_fusion) | copy-start | bytes 1572868
  198.9 4.8 copy-start.4
  216.9 27.3 %copy-start.14 = (bf16[96,8,2,256]{3,1,2,0:T(8,128)(2,1)}, bf16[96,8,2,256]{3,1,2,0:T(8,128)(2,1)S(1)}, u32[]{:S(2)}) copy-start(bf16[96,8,2,256]{3,1,2,0:T(8,128)(2,1)S(1)} %copy.89) | copy-start | bytes 2359300
  243.8 182.8 %copy-start.12 = (f32[512,768]{1,0:T(8,128)}, f32[512,768]{1,0:T(8,128)S(1)}, u32[]{:S(2)}) copy-start(f32[512,768]{1,0:T(8,128)S(1)} %get-tuple-element.132) | copy-start | bytes 4718596
  402.5 6.4 copy-start.9
  409.7 11.9 slice-start
  411.2 10.3 copy-start.10
  411.3 10.2 slice-start.1
  448.7 124.0 %reduce-scatter.15.cloned.1.call-start = ((), (), s32[]{:S(2)}) async-start(), calls=%async_computation.16 | async-start | bytes 7864320 | tf_op jit(solution)/shard_map/reduce_scatter | solution.py:216
  470.8 31.5 %copy-start.7 = (bf16[2,256,12,64]{1,0,3,2:T(2,128)(2,1)S(1)}, bf16[2,256,12,64]{1,0,3,2:T(2,128)(2,1)}, u32[]{:S(2)}) copy-start(bf16[2,256,12,64]{1,0,3,2:T(2,128)(2,1)} %reshape.168) | copy-start | bytes 2359300
  502.3 6.7 copy-start
  515.6 129.6 %reduce-scatter.25.cloned.1.call-start = ((), (), s32[]{:S(2)}) async-start(), calls=%async_computation.21 | async-start | bytes 2654208
  532.4 184.3 %reduce-scatter.29.cloned.1.call-start = ((), (), s32[]{:S(2)}) async-start(), calls=%async_computation.23 | async-start | bytes 2654208
  537.8 250.5 %reduce-scatter.27.cloned.1.call-start = ((), (), s32[]{:S(2)}) async-start(), calls=%async_computation.22 | async-start | bytes 2654208
  577.3 3.3 copy-start.6
  580.6 3.6 copy-start.13
  580.6 278.9 %reduce-scatter.19.cloned.1.call-start = ((), (), s32[]{:S(2)}) async-start(), calls=%async_computation.18 | async-start | bytes 2654208 | tf_op jit(solution)/shard_map/reduce_scatter | solution.py:240
  584.1 441.4 %reduce-scatter.21.cloned.1.call-start = ((), (), s32[]{:S(2)}) async-start(), calls=%async_computation.19 | async-start | bytes 10616832 | tf_op jit(solution)/shard_map/reduce_scatter | solution.py:246
  591.4 600.1 %reduce-scatter.23.cloned.1.call-start = ((), (), s32[]{:S(2)}) async-start(), calls=%async_computation.20 | async-start | bytes 10616832 | tf_op jit(solution)/shard_map/reduce_scatter | solution.py:248
  601.1 591.8 %copy-start.16 = (bf16[96,8,2,256]{3,1,2,0:T(8,128)(2,1)S(1)}, bf16[96,8,2,256]{3,1,2,0:T(8,128)(2,1)}, u32[]{:S(2)}) copy-start(bf16[96,8,2,256]{3,1,2,0:T(8,128)(2,1)} %copy-done.15) | copy-start | bytes 2359300
  601.1 672.8 %all-reduce.23.cloned.1.call-start = ((), (), s32[]{:S(2)}) async-start(), calls=%async_computation.24 | async-start | bytes 7667712 | tf_op jit(solution)/shard_map/psum | solution.py:253
  1191.5 4.7 copy-start.25
  1192.9 48.5 %copy-start.18 = (bf16[2,256,768]{2,1,0:T(8,128)(2,1)S(1)}, bf16[2,256,768]{2,1,0:T(8,128)(2,1)}, u32[]{:S(2)}) copy-start(bf16[2,256,768]{2,1,0:T(8,128)(2,1)} %copy-done.17) | copy-start | bytes 2359300
  1273.9 7.5 copy-start.21
  1273.9 8.5 copy-start.20
  (10 other events, 15.7 us)
Sparse Core Ops, SparseCore 0:
  10.3 43.7 all-gather.15
  56.3 40.0 all-gather.9
  98.6 39.8 all-gather.13
  140.4 27.2 all-gather.17
  169.7 28.5 all-gather.11
  200.4 41.0 all-gather.19
  243.6 78.6 all-gather.21
  324.5 78.0 all-gather.23
  448.9 56.4 reduce-scatter.16
  515.7 56.9 reduce-scatter.14
  576.2 68.9 reduce-scatter.24
  648.5 68.0 reduce-scatter.28
  720.2 68.0 reduce-scatter.26
  791.6 67.8 reduce-scatter.18
  862.9 162.5 reduce-scatter.20
  1028.9 162.5 reduce-scatter.22
  1194.2 79.6 all-reduce.22
where the time goes:
time: 1300 us; the launch traced here: 1290 us
  waiting for transfers between devices  890 us (68%)
  matrix products  163 us (13%)
  blocking collectives  109 us (8%)
  local copies, waits for them, and re-layouts  59.1 us (5%)
  other arithmetic  51.6 us (4%)
  between operations  16.8 us (1%)
    unnamed x20, waiting for transfers between devices  188 us
    reduce_scatter x1, waiting for transfers between devices, on_device(): lax.psum_scatter(grad_weight_d, 'seq', scatter_dimension=0, tiled=True)  166 us
    reduce_scatter x1, waiting for transfers between devices, on_device(): lax.psum_scatter(grad_weight_i, 'seq', scatter_dimension=0, tiled=True)  166 us
    all_gather x1, waiting for transfers between devices, on_device(): lax.all_gather(w_in, 'seq', axis=0, tiled=True)  78.1 us
    unnamed x2, blocking collectives  71 us
    reduce_scatter x1, waiting for transfers between devices, on_device(): lax.psum_scatter(grad_weight_o, 'seq', scatter_dimension=0, tiled=True)  69.3 us
    all_gather x1, waiting for transfers between devices, on_device(): lax.all_gather(w_down, 'seq', axis=0, tiled=True)  60.4 us
    all_gather x1, waiting for transfers between devices, on_device(): lax.all_gather(w_key, 'seq', axis=0, tiled=True)  44.5 us
  transfers between devices with their start and end apart: 17, of which 15 were waited for; matrix products, arithmetic and copies ran while one was open for 16% of the time, Pallas kernels for 0%

commit v1 on v0

v1 whole, which is shorter than its diff:
```python
import functools
import math

import jax
import jax.numpy as jnp
from jax import lax
from jax.experimental import pallas as pl
from jax.experimental.pallas import tpu as pltpu
from jax.sharding import PartitionSpec as P

EPSILON = 1e-05
NEGATIVE = -1e30
BF = jnp.bfloat16
F32 = jnp.float32
VM = pltpu.VMEM
ANY = pl.ANY
VMEM_LIMIT = 60 * 1024 * 1024
GROUPS = 3


def dot(a, b):
    return lax.dot_general(a, b, (((1,), (0,)), ((), ())), preferred_element_type=F32)


def dot_nt(a, b):
    return lax.dot_general(a, b, (((1,), (1,)), ((), ())), preferred_element_type=F32)


def dot_tn(a, b):
    return lax.dot_general(a, b, (((0,), (0,)), ((), ())), preferred_element_type=F32)


def vmem(shape=None, index=None):
    if shape is None:
        return pl.BlockSpec(memory_space=VM)
    return pl.BlockSpec(shape, index)


def params(n_grid=0):
    return pltpu.CompilerParams(
        vmem_limit_bytes=VMEM_LIMIT,
        dimension_semantics=("arbitrary",) * n_grid if n_grid else None,
    )


def smem():
    return pl.BlockSpec(memory_space=pltpu.SMEM)


def swap(value, axis, size, bit):
    step = 1 << bit
    return lax.ppermute(value, axis, [(i, i ^ step) for i in range(size)])


def gather_seq(block, size, order):
    held = block[None]
    for bit in order:
        held = jnp.concatenate([held, swap(held, "seq", size, bit)], 0)
    return held


def reduce_seq(held, size, order):
    for bit in reversed(order):
        half = held.shape[0] // 2
        got = swap(held[half:], "seq", size, bit)
        held = (held[:half].astype(F32) + got.astype(F32)).astype(held.dtype)
    return held


def place(index, order):
    out = 0
    for step, bit in enumerate(order):
        out = out | (((index >> bit) & 1) << step)
    return out


def turn_kernel(scal, t0, t1, t2, t3, out_ref):
    mc = scal[1]
    seqs, _, width = t0.shape
    shard = out_ref.shape[2] // 4
    for j, tok in enumerate((t0, t1, t2, t3)):
        where = pl.multiple_of((mc ^ j) * shard, shard)
        for s in range(seqs):
            out_ref[s, :, pl.ds(where, shard)] = tok[s, :shard, :].T


def attend_kernel(
    order, shards, aliased,
    scal, t0, t1, t2, t3, doc_ref, w_own, w_got, bias_ref, prior_ref, *rest,
):
    if aliased:
        rest = rest[1:]
    raw_ref, e_ref, q_ref, k_ref, v_ref, o_ref, inv_ref, w_s, kt_s, mask_s = rest
    s, h = pl.program_id(0), pl.program_id(1)
    pm, mc, core = scal[0], scal[1], scal[2]
    rows = w_own.shape[1]
    half = w_own.shape[2]
    cols = q_ref.shape[2]
    shard = q_ref.shape[1]
    head = cols // 4

    @pl.when((s == 0) & (h == 0))
    def _():
        for i in range(shards):
            at = place(i, order) ^ pm
            mine, other = w_own[at], w_got[at]
            first = core == 0
            w_s[i * rows:(i + 1) * rows, :half] = jnp.where(first, mine, other)
            w_s[i * rows:(i + 1) * rows, half:] = jnp.where(first, other, mine)

    @pl.when(h == 0)
    def _():
        q = dot(t0[s, :shard, :], w_s[:, :cols]) + bias_ref[0:1, :]
        q_ref[0] = (q.astype(BF).astype(F32) * (1.0 / math.sqrt(head))).astype(BF)
        mine = doc_ref[0]
        for j, tok in enumerate((t0, t1, t2, t3)):
            where = pl.multiple_of((mc ^ j) * shard, shard)
            kv = dot(tok[s, :shard, :], w_s[:, cols:])
            k_ref[0, pl.ds(where, shard), :] = kv[:, :cols].astype(BF)
            v_ref[0, pl.ds(where, shard), :] = (kv[:, cols:] + bias_ref[1:2, :]).astype(BF)
            docs = tok[s, shard:shard + 1, :shard].astype(F32)
            mask_s[:, pl.ds(where, shard)] = jnp.where(mine == docs, 0.0, NEGATIVE)
        kt_s[...] = k_ref[0].T

    lane = lax.broadcasted_iota(jnp.int32, (shard, cols), 1) // head
    this = lane == h
    qm = jnp.where(this, q_ref[0].astype(F32), 0.0).astype(BF)
    length = k_ref.shape[1]
    lane_k = lax.broadcasted_iota(jnp.int32, (length, cols), 1) // head
    v_one = jnp.where(lane_k == h, v_ref[0].astype(F32), 1.0).astype(BF)
    step = 64
    for r in range(0, shard, step):
        logits = dot(qm[r:r + step], kt_s[...]) + prior_ref[0, 0, r:r + step, :].astype(F32)
        raw_ref[0, 0, r:r + step, :] = logits.astype(BF)
        masked = logits + mask_s[r:r + step, :]
        top = jnp.max(masked, -1, keepdims=True)
        e_ref[0, 0, r:r + step, :] = jnp.exp(masked - top).astype(BF)
    o = dot(e_ref[0, 0], v_one)
    total = jnp.max(jnp.where(lane == (h + 1) % 4, o, 0.0), -1, keepdims=True)
    inv = 1.0 / total
    o_ref[0] = jnp.where(this, o * inv, o_ref[0])
    inv_ref[0] = jnp.where(this, inv, inv_ref[0])


def gelu_parts(x):
    z = jnp.abs(x) * 0.7071067811865476
    t = 1.0 / (1.0 + 0.3275911 * z)
    e = jnp.exp(-0.5 * x * x)
    poly = t * (0.254829592 + t * (-0.284496736 + t * (1.421413741 + t * (-1.453152027 + t * 1.061405429))))
    tail = 0.5 * poly * e
    phi = jnp.where(x >= 0, 1.0 - tail, tail)
    return x * phi, phi + x * (e * 0.3989422804014327)


def moments(x):
    mean = jnp.mean(x, -1, keepdims=True)
    centered = x - mean
    inverse = lax.rsqrt(jnp.mean(centered * centered, -1, keepdims=True) + EPSILON)
    return centered * inverse, inverse


def norm_back(grad, normed, inverse, gain):
    scaled = grad * gain
    return inverse * (
        scaled - jnp.mean(scaled, -1, keepdims=True)
        - normed * jnp.mean(scaled * normed, -1, keepdims=True)
    )


def copies_of(pairs, sem, base):
    return [pltpu.make_async_copy(src, dst, sem.at[base + i]) for i, (src, dst) in enumerate(pairs)]


def forward_kernel(
    oi, oo, od, shards,
    scal, o0, o1, o2, tok_ref, cot_ref, vec_ref, bin_ref,
    wo_own, wo_got, i0, i1, i2, i3, d_own, d_got,
    out_ref, first_n_ref, inv1_ref, inner_ref, hid_ref, dg_ref, dsum2_ref, dsec_ref, vg_ref,
    wo_s, wi_s, wd_s, first_s, acc_s, sem,
):
    mc, core = scal[1], scal[2]
    p_o, p_i, p_d = scal[3], scal[4], scal[5]
    my_y = mc >> 1
    rows = wo_own.shape[1]
    half = wo_own.shape[2]
    sub = d_own.shape[2]
    seqs, shard, width = tok_ref.shape
    n_rows = seqs * shard
    base = 0
    in_copies, down_copies = [], []
    for j, ref in enumerate((i0, i1, i2, i3)):
        in_copies.append(copies_of(
            [(ref.at[place(s, oi) ^ p_i], wi_s.at[j, pl.ds(s * rows, rows)]) for s in range(shards)], sem, base))
        base += shards
        src = d_own if j % 2 == 0 else d_got
        down_copies.append(copies_of(
            [(src.at[place(s, od) ^ p_d, my_y ^ (j >> 1)], wd_s.at[j, pl.ds(s * sub, sub)]) for s in range(shards)], sem, base))
        base += shards
    for j in range(4):
        for c in in_copies[j] + down_copies[j]:
            c.start()
    first_core = core == 0
    for i in range(shards):
        at = place(i, oo) ^ p_o
        mine, other = wo_own[at], wo_got[at]
        wo_s[i * rows:(i + 1) * rows, :half] = jnp.where(first_core, mine, other)
        wo_s[i * rows:(i + 1) * rows, half:] = jnp.where(first_core, other, mine)
    mixed = jnp.concatenate([r[...].reshape(n_rows, -1).astype(BF) for r in (o0, o1, o2)], 1)
    tokens = tok_ref[...].reshape(n_rows, width).astype(F32)
    normed, inverse = moments(tokens + (dot(mixed, wo_s[...]) + vec_ref[0:1, :]))
    first_n_ref[...] = normed
    inv1_ref[...] = inverse
    first = normed * vec_ref[1:2, :] + vec_ref[2:3, :]
    first_s[...] = first
    inner_ref[...] = first.astype(BF)
    for j in range(4):
        for c in in_copies[j]:
            c.wait()
        for r in range(0, n_rows, 128):
            pre = dot(inner_ref[r:r + 128, :], wi_s[j]) + bin_ref[mc ^ j]
            hid, dg = gelu_parts(pre)
            hid_ref[j, r:r + 128, :] = hid.astype(BF)
            dg_ref[j, r:r + 128, :] = dg.astype(BF)
        for c in down_copies[j]:
            c.wait()
        part = dot(hid_ref[j], wd_s[j])
        acc_s[...] = part if j == 0 else acc_s[...] + part
    normed, inverse = moments(first_s[...] + (acc_s[...] + vec_ref[3:4, :]))
    gain = vec_ref[4:5, :]
    out_ref[...] = (normed * gain + vec_ref[5:6, :]).astype(BF).reshape(seqs, shard, width)
    dy = cot_ref[...].reshape(n_rows, width).astype(F32)
    dsum2 = norm_back(dy, normed, inverse, gain)
    dsum2_ref[...] = dsum2
    dsec = dsum2.astype(BF)
    dsec_ref[...] = dsec
    vg_ref[0:1, :] = jnp.sum(dy * normed, 0, keepdims=True)
    vg_ref[1:2, :] = jnp.sum(dy, 0, keepdims=True)
    vg_ref[2:3, :] = jnp.sum(dsec.astype(F32), 0, keepdims=True)


def backward_kernel(
    oi, oo, od, shards,
    scal, o0, o1, o2, first_n, inv1, inner, hid, dg, dsum2, dsec, vec_ref,
    wo_own, wo_got, i0, i1, i2, i3, d_own, d_got,
    gi0, gi1, gi2, gi3, gd_keep, gd_send, go_keep, go_send, dsum1_ref, dmix_ref, vg_ref, gbin_ref,
    wo_s, wi_s, wd_s, acc_s, sem,
):
    mc, core = scal[1], scal[2]
    p_o, p_i, p_d = scal[3], scal[4], scal[5]
    my_y = mc >> 1
    rows = wo_own.shape[1]
    half = wo_own.shape[2]
    sub = d_own.shape[2]
    n_rows, width = dsec.shape
    base = 0
    in_copies, down_copies = [], []
    for j, ref in enumerate((i0, i1, i2, i3)):
        src = d_own if j % 2 == 0 else d_got
        down_copies.append(copies_of(
            [(src.at[place(s, od) ^ p_d, my_y ^ (j >> 1)], wd_s.at[j, pl.ds(s * sub, sub)]) for s in range(shards)], sem, base))
        base += shards
        in_copies.append(copies_of(
            [(ref.at[place(s, oi) ^ p_i], wi_s.at[j, pl.ds(s * rows, rows)]) for s in range(shards)], sem, base))
        base += shards
    for j in range(4):
        for c in down_copies[j] + in_copies[j]:
            c.start()
    first_core = core == 0
    for i in range(shards):
        at = place(i, oo) ^ p_o
        mine, other = wo_own[at], wo_got[at]
        wo_s[i * rows:(i + 1) * rows, :half] = jnp.where(first_core, mine, other)
        wo_s[i * rows:(i + 1) * rows, half:] = jnp.where(first_core, other, mine)
    for j, gi in enumerate((gi0, gi1, gi2, gi3)):
        gd = gd_keep if j % 2 == 0 else gd_send
        grad_d = dot_tn(hid[j], dsec[...]).astype(BF)
        for s in range(shards):
            gd[place(s, od) ^ p_d, my_y ^ (j >> 1)] = grad_d[s * sub:(s + 1) * sub]
        for c in down_copies[j]:
            c.wait()
        dpre = (dot_nt(dsec[...], wd_s[j]) * dg[j].astype(F32)).astype(BF)
        gbin_ref[mc ^ j] = jnp.sum(dpre.astype(F32), 0, keepdims=True)
        grad_i = dot_tn(inner[...], dpre).astype(BF)
        for s in range(shards):
            gi[place(s, oi) ^ p_i] = grad_i[s * rows:(s + 1) * rows]
        for c in in_copies[j]:
            c.wait()
        part = dot_nt(dpre, wi_s[j])
        acc_s[...] = (dsum2[...] if j == 0 else acc_s[...]) + part
    dfirst = acc_s[...]
    normed = first_n[...]
    dsum1 = norm_back(dfirst, normed, inv1[...], vec_ref[1:2, :])
    dsum1_ref[...] = dsum1
    dbranch = dsum1.astype(BF)
    vg_ref[0:1, :] = jnp.sum(dfirst * normed, 0, keepdims=True)
    vg_ref[1:2, :] = jnp.sum(dfirst, 0, keepdims=True)
    vg_ref[2:3, :] = jnp.sum(dbranch.astype(F32), 0, keepdims=True)
    dmix_ref[...] = dot_nt(dbranch, wo_s[...]).astype(BF).reshape(dmix_ref.shape)
    mixed = jnp.concatenate([r[...].reshape(n_rows, -1).astype(BF) for r in (o0, o1, o2)], 1)
    grad_o = dot_tn(mixed, dbranch).astype(BF)
    for s in range(shards):
        block = grad_o[s * rows:(s + 1) * rows]
        at = place(s, oo) ^ p_o
        go_keep[at] = jnp.where(first_core, block[:, :half], block[:, half:])
        go_send[at] = jnp.where(first_core, block[:, half:], block[:, :half])


def attend_back_kernel(
    order, shards, aliased,
    scal, e_ref, dm_ref, q_ref, k_ref, v_ref, o_ref, inv_ref, xt_ref, *rest,
):
    if aliased:
        rest = rest[1:]
    (gp_ref, g_keep, g_send, dq_ref, dkv_ref, vg_ref,
     vt_s, qt_s, dmt_s, dmi_s, dl_s, dkt_s, dvt_s, dq_s) = rest
    s, h = pl.program_id(0), pl.program_id(1)
    pm, mc, core = scal[0], scal[1], scal[2]
    shard, cols = q_ref.shape[1:]
    length = k_ref.shape[1]
    head = cols // 4
    seqs = dq_ref.shape[0]

    @pl.when(h == 0)
    def _():
        vt_s[...] = v_ref[0].T
        dmi = (dm_ref[0].astype(F32) * inv_ref[0]).astype(BF)
        dmi_s[...] = dmi
        dl_s[...] = dmi.astype(F32) * o_ref[0]
        qt_s[...] = q_ref[0].T
        dmt_s[...] = dmi.T

    lane = lax.broadcasted_iota(jnp.int32, (shard, cols), 1) // head
    this = lane == h
    dmm = jnp.where(this, dmi_s[...].astype(F32), 0.0).astype(BF)
    delta = jnp.sum(jnp.where(this, dl_s[...], 0.0), -1, keepdims=True)
    step = 64
    for r in range(0, shard, step):
        dp = dot(dmm[r:r + step], vt_s[...])
        gp_ref[0, 0, r:r + step, :] = (
            e_ref[0, 0, r:r + step, :].astype(F32) * (dp - delta[r:r + step])
        ).astype(BF)
    g = gp_ref[0, 0]
    dq = dot(g, k_ref[0]) * (1.0 / math.sqrt(head))
    dq_s[s] = jnp.where(this, dq, dq_s[s])
    at = pl.multiple_of(h * head, head)
    dkt_s[pl.ds(at, head), :] = dot(qt_s[pl.ds(at, head), :], g).astype(BF)
    dvt_s[pl.ds(at, head), :] = dot(dmt_s[pl.ds(at, head), :], e_ref[0, 0]).astype(BF)

    @pl.when(h == 3)
    def _():
        dq_ref[s] = dq_s[s].astype(BF)
        dkv_ref[s, :, :cols] = dkt_s[...].T
        dkv_ref[s, :, cols:] = dvt_s[...].T

    @pl.when((h == 3) & (s == seqs - 1))
    def _():
        grad_kv = None
        grad_q = None
        ones = jnp.ones((8, length), BF)
        sum_v = None
        sum_q = None
        for i in range(seqs):
            part = dot(xt_ref[i], dkv_ref[i])
            grad_kv = part if i == 0 else grad_kv + part
            mine = pl.multiple_of(mc * shard, shard)
            part = dot(xt_ref[i, :, pl.ds(mine, shard)], dq_ref[i])
            grad_q = part if i == 0 else grad_q + part
            part = dot(ones, dkv_ref[i, :, cols:])
            sum_v = part if i == 0 else sum_v + part
            part = dot(ones[:, :shard], dq_ref[i])
            sum_q = part if i == 0 else sum_q + part
        vg_ref[0:1, :] = sum_q[0:1]
        vg_ref[1:2, :] = sum_v[0:1]
        grad = jnp.concatenate([grad_q.astype(BF), grad_kv.astype(BF)], 1)
        rows = g_keep.shape[1]
        half = g_keep.shape[2]
        first_core = core == 0
        for i in range(shards):
            block = grad[i * rows:(i + 1) * rows]
            to = place(i, order) ^ pm
            g_keep[to] = jnp.where(first_core, block[:, :half], block[:, half:])
            g_send[to] = jnp.where(first_core, block[:, half:], block[:, :half])


def token_kernel(
    order, shards,
    scal, dq0, dq1, dq2, dkv0, dkv1, dkv2, own0, got0, own1, got1, own2, got2, dsum1,
    p0, p1, p2, p3, w_s,
):
    pms, mc, core = scal[0], scal[1], scal[2]
    rows, half = own0.shape[1:]
    seqs, shard, cols = dq0.shape
    first_core = core == 0
    for g, (own, got) in enumerate(((own0, got0), (own1, got1), (own2, got2))):
        for i in range(shards):
            at = place(i, order) ^ pms
            mine, other = own[at, :, :half], got[at, :, :half]
            w_s[g, i * rows:(i + 1) * rows, :half] = jnp.where(first_core, mine, other)
            w_s[g, i * rows:(i + 1) * rows, half:] = jnp.where(first_core, other, mine)
    for j, out in reversed(list(enumerate((p0, p1, p2, p3)))):
        where = pl.multiple_of((mc ^ j) * shard, shard)
        for s in range(seqs):
            total = None
            for g, (dq, dkv) in enumerate(((dq0, dkv0), (dq1, dkv1), (dq2, dkv2))):
                part = dot_nt(dkv[s, pl.ds(where, shard), :], w_s[g, :, cols:])
                if j == 0:
                    part = part + dot_nt(dq[s], w_s[g, :, :cols])
                total = part if total is None else total + part
            if j == 0:
                total = total + dsum1[s * shard:(s + 1) * shard, :]
            out[s] = total.astype(out.dtype)


def on_device(
    n, order,
    tokens, prior_logits, doc_ids, w_query, w_key, w_value, w_out, b_query, b_value, b_out,
    first_norm_gain, norm1_shift, w_in, b_in, w_down, b_down, norm2_gain, norm2_shift, cotangent,
):
    seqs, shard, width = tokens.shape
    heads, length = prior_logits.shape[1], prior_logits.shape[3]
    ctx = length // shard
    head = width // heads
    rows = w_query.shape[0]
    ff = w_in.shape[1]
    sub = w_down.shape[0] // 4
    cols = width // GROUPS
    per = heads // GROUPS
    half = (3 * cols) // 2
    n_rows = seqs * shard
    me_s = lax.axis_index("seq")
    me_c = lax.axis_index("ctx")
    core, my_y = me_c & 1, me_c >> 1
    pm = place(me_s, order)
    scal = jnp.stack([pm, me_c, core, pm, pm, pm]).astype(jnp.int32)
    own_core = core == 0

    docs = jnp.pad(doc_ids.astype(BF)[:, None, :], ((0, 0), (0, 15), (0, width - shard)))
    tok0 = jnp.concatenate([tokens, docs], 1)
    tok2 = swap(tok0, "ctx", ctx, 1)
    both = swap(jnp.stack([tok0, tok2]), "ctx", ctx, 0)
    tok = (tok0, both[0], tok2, both[1])
    doc_col = doc_ids.astype(F32)[:, :, None]

    vec = jnp.concatenate(
        [b_query, b_value, b_out, first_norm_gain, norm1_shift, b_down, norm2_gain, norm2_shift, b_in])[None]
    vec = gather_seq(vec, n, order)[:, 0]
    spots = place(jnp.arange(n), order) ^ pm
    vec = jnp.take(vec, spots, axis=0).astype(F32)
    small = vec[:, :8 * rows].reshape(n, 8, rows).transpose(1, 0, 2).reshape(8, width)
    bin_all = vec[:, 8 * rows:].reshape(n, 2, 2, sub).transpose(2, 1, 0, 3).reshape(4, 1, n * sub)
    vecs = small[2:8]

    def tile(g):
        cut = slice(g * cols, (g + 1) * cols)
        parts = [w_query[:, cut], w_key[:, cut], w_value[:, cut]]
        whole = jnp.concatenate(parts, 1)
        return jnp.where(own_core, whole[:, :half], whole[:, half:])

    def o_tile():
        return jnp.where(own_core, w_out[:, :half], w_out[:, half:])

    tiles = [tile(g) for g in range(GROUPS)] + [o_tile()]
    own = [gather_seq(t, n, order) for t in tiles]
    got = [swap(o, "ctx", ctx, 0) for o in own]

    in_part = w_in.reshape(rows, n, 2, 2, sub)
    in_part = lax.dynamic_slice(in_part, (0, 0, core, my_y, 0), (rows, n, 1, 1, sub)).reshape(rows, n * sub)
    in0 = gather_seq(in_part, n, order)
    in2 = swap(in0, "ctx", ctx, 1)
    in1 = swap(in0, "ctx", ctx, 0)
    in3 = swap(in2, "ctx", ctx, 0)
    down_part = lax.dynamic_slice(w_down.reshape(2, 2 * sub, width), (core, 0, 0), (1, 2 * sub, width))[0]
    d_own = gather_seq(down_part, n, order)
    d_got = swap(d_own, "ctx", ctx, 0).reshape(n, 2, sub, width)
    d_own = d_own.reshape(n, 2, sub, width)

    sds = jax.ShapeDtypeStruct
    x_t = pl.pallas_call(
        turn_kernel,
        out_shape=sds((seqs, width, length), BF),
        in_specs=[smem()] + [vmem()] * 4,
        out_specs=vmem(),
        compiler_params=params(),
        name="turn",
    )(scal, *tok)

    def per_seq(rows_, cols_):
        return pl.BlockSpec((1, rows_, cols_), lambda s, h: (s, 0, 0))

    def big(g):
        return pl.BlockSpec((1, 1, shard, length), lambda s, h: (s, g * per + h, 0, 0))

    local_big = pl.BlockSpec((1, 1, shard, length), lambda s, h: (s, h, 0, 0))
    raw = None
    kept = []
    for g in range(GROUPS):
        bias = jnp.zeros((8, cols), F32).at[0].set(small[0, g * cols:(g + 1) * cols]).at[1].set(
            small[1, g * cols:(g + 1) * cols])
        args = [scal, *tok, doc_col, own[g], got[g], bias, prior_logits]
        specs = [smem()] + [vmem()] * 4 + [per_seq(shard, 1), vmem(), vmem(), vmem(), big(g)]
        alias = {}
        if raw is not None:
            alias = {len(args): 0}
            args.append(raw)
            specs.append(pl.BlockSpec(memory_space=ANY))
        raw, *rest = pl.pallas_call(
            functools.partial(attend_kernel, order, n, raw is not None),
            grid=(seqs, per),
            out_shape=[
                sds(prior_logits.shape, BF),
                sds((seqs, per, shard, length), BF),
                sds((seqs, shard, cols), BF),
                sds((seqs, length, cols), BF),
                sds((seqs, length, cols), BF),
                sds((seqs, shard, cols), F32),
                sds((seqs, shard, cols), F32),
            ],
            in_specs=specs,
            out_specs=[big(g), local_big, per_seq(shard, cols), per_seq(length, cols), per_seq(length, cols),
                       per_seq(shard, cols), per_seq(shard, cols)],
            scratch_shapes=[VM((width, 3 * cols), BF), VM((cols, length), BF), VM((shard, length), F32)],
            input_output_aliases=alias,
            compiler_params=params(2),
            name=f"attend{g}",
        )(*args)
        kept.append(rest)

    weights = [own[3], got[3], in0, in1, in2, in3, d_own, d_got]
    weight_specs = [vmem(), vmem()] + [pl.BlockSpec(memory_space=ANY)] * 6
    weight_scratch = [VM((width, width), BF), VM((4, width, n * sub), BF), VM((4, n * sub, width), BF)]
    o_parts = [k[4] for k in kept]
    output, first_n, inv1, inner, hid, dg, dsum2, dsec, vg2 = pl.pallas_call(
        functools.partial(forward_kernel, order, order, order, n),
        out_shape=[
            sds((seqs, shard, width), BF), sds((n_rows, width), F32), sds((n_rows, 1), F32), sds((n_rows, width), BF),
            sds((4, n_rows, n * sub), BF), sds((4, n_rows, n * sub), BF), sds((n_rows, width), F32),
            sds((n_rows, width), BF), sds((8, width), F32),
        ],
        in_specs=[smem()] + [vmem()] * 7 + weight_specs,
        out_specs=[vmem()] * 9,
        scratch_shapes=weight_scratch + [VM((n_rows, width), F32), VM((n_rows, width), F32),
                                         pltpu.SemaphoreType.DMA((8 * n,))],
        compiler_params=params(),
        name="ff_fwd",
    )(scal, *o_parts, tokens, cotangent, vecs, bin_all, *weights)

    gi0, gi1, gi2, gi3, gd_keep, gd_send, go_keep, go_send, dsum1, dmix, vg1, gbin = pl.pallas_call(
        functools.partial(backward_kernel, order, order, order, n),
        out_shape=[sds((n, rows, n * sub), BF)] * 4 + [sds((n, 2, sub, width), BF)] * 2
        + [sds((n, rows, half), BF)] * 2 + [
            sds((n_rows, width), F32), sds((seqs, shard, width), BF), sds((8, width), F32), sds((4, 1, n * sub), F32)],
        in_specs=[smem()] + [vmem()] * 11 + weight_specs,
        out_specs=[vmem()] * 12,
        scratch_shapes=weight_scratch + [VM((n_rows, width), F32), pltpu.SemaphoreType.DMA((8 * n,))],
        compiler_params=params(),
        name="ff_bwd",
    )(scal, *o_parts, first_n, inv1, inner, hid, dg, dsum2, dsec, vecs, *weights)

    def add(a, b):
        return (a.astype(F32) + b.astype(F32)).astype(BF)

    gd = add(gd_keep, swap(gd_send, "ctx", ctx, 0)).reshape(n, 2 * sub, width)
    gd = reduce_seq(gd, n, order)[0]
    gd = add(gd, swap(gd, "ctx", ctx, 1))
    gd_other = swap(gd, "ctx", ctx, 0)
    grad_w_down = jnp.where(own_core, jnp.concatenate([gd, gd_other]), jnp.concatenate([gd_other, gd])).astype(F32)

    gi_a = add(gi0, swap(gi1, "ctx", ctx, 0))
    gi_b = add(gi2, swap(gi3, "ctx", ctx, 0))
    gi = add(gi_a, swap(gi_b, "ctx", ctx, 1))
    gi = reduce_seq(gi, n, order)[0]
    gi_y = swap(gi, "ctx", ctx, 1)
    pair = jnp.where(my_y == 0, jnp.stack([gi, gi_y]), jnp.stack([gi_y, gi]))
    pair_other = swap(pair, "ctx", ctx, 0)
    quad = jnp.where(own_core, jnp.stack([pair, pair_other]), jnp.stack([pair_other, pair]))
    grad_w_in = quad.reshape(2, 2, rows, n, sub).transpose(2, 3, 0, 1, 4).reshape(rows, ff).astype(F32)

    def finish(keep, send):
        held = add(keep, swap(send, "ctx", ctx, 0))
        held = reduce_seq(held, n, order)[0]
        held = add(held, swap(held, "ctx", ctx, 1))
        other = swap(held, "ctx", ctx, 0)
        lo = jnp.where(own_core, held, other)
        hi = jnp.where(own_core, other, held)
        return jnp.concatenate([lo, hi], 1).astype(F32)

    grad_w_out = finish(go_keep, go_send)

    gp = None
    grads, dqs, dkvs, vgs = [], [], [], []
    for g in range(GROUPS):
        e, q, k, v, o, inv = kept[g]
        args = [scal, e, dmix, q, k, v, o, inv, x_t]
        specs = [smem(), local_big, pl.BlockSpec((1, shard, cols), lambda s, h, g=g: (s, 0, g)),
                 per_seq(shard, cols), per_seq(length, cols), per_seq(length, cols), per_seq(shard, cols),
                 per_seq(shard, cols), vmem()]
        alias = {}
        if gp is not None:
            alias = {len(args): 0}
            args.append(gp)
            specs.append(pl.BlockSpec(memory_space=ANY))
        gp, keep, send, dq, dkv, vg = pl.pallas_call(
            functools.partial(attend_back_kernel, order, n, gp is not None),
            grid=(seqs, per),
            out_shape=[
                sds(prior_logits.shape, BF), sds((n, rows, half), BF), sds((n, rows, half), BF),
                sds((seqs, shard, cols), BF), sds((seqs, length, 2 * cols), BF), sds((8, cols), F32),
            ],
            in_specs=specs,
            out_specs=[big(g)] + [vmem()] * 5,
            scratch_shapes=[
                VM((cols, length), BF), VM((cols, shard), BF), VM((cols, shard), BF), VM((shard, cols), BF),
                VM((shard, cols), F32), VM((cols, length), BF), VM((cols, length), BF), VM((seqs, shard, cols), F32),
            ],
            input_output_aliases=alias,
            compiler_params=params(2),
            name=f"attend_back{g}",
        )(*args)
        grads.append(finish(keep, send))
        dqs.append(dq)
        dkvs.append(dkv)
        vgs.append(vg)

    pieces = pl.pallas_call(
        functools.partial(token_kernel, order, n),
        out_shape=[sds((seqs, shard, width), F32)] + [sds((seqs, shard, width), BF)] * 3,
        in_specs=[smem()] + [vmem()] * 13,
        out_specs=[vmem()] * 4,
        scratch_shapes=[VM((GROUPS, width, 3 * cols), BF)],
        compiler_params=params(),
        name="token_grad",
    )(scal, *dqs, *dkvs, own[0], got[0], own[1], got[1], own[2], got[2], dsum1)
    from_core = swap(jnp.stack([pieces[1], pieces[3]]), "ctx", ctx, 0)
    across = add(pieces[2], from_core[1])
    grad_tokens = pieces[0] + from_core[0].astype(F32) + swap(across, "ctx", ctx, 1).astype(F32)

    def by_shard(row):
        return row.reshape(n, rows)

    sums = [
        jnp.concatenate([vg[0] for vg in vgs]), jnp.concatenate([vg[1] for vg in vgs]),
        vg1[2], vg1[0], vg1[1], vg2[2], vg2[0], vg2[1],
    ]
    bin_nat = gbin.reshape(2, 2, n, sub).transpose(2, 1, 0, 3).reshape(n, 4 * sub)
    table = jnp.concatenate([by_shard(v) for v in sums] + [bin_nat], 1)
    back = place(jnp.arange(n), order)
    inverse_spots = [0] * n
    for i in range(n):
        inverse_spots[place(i, order)] = i
    table = jnp.take(table, jnp.array(inverse_spots) ^ me_s, axis=0)
    del back
    table = reduce_seq(table, n, order)[0]
    table = table + swap(table, "ctx", ctx, 1)
    table = table + swap(table, "ctx", ctx, 0)
    cut = [table[i * rows:(i + 1) * rows] for i in range(8)]
    g_bq, g_bv, g_bo, g_g1, g_s1, g_bd, g_g2, g_s2 = cut
    g_bin = table[8 * rows:]

    def columns(i):
        return jnp.concatenate([gr[:, i * cols:(i + 1) * cols] for gr in grads], 1)

    return (
        output, raw, grad_tokens, gp,
        columns(0), columns(1), columns(2), grad_w_out,
        g_bq, g_bv, g_bo, g_g1, g_s1, grad_w_in, g_bin, grad_w_down, g_bd, g_g2, g_s2,
    )


def solution(mesh):
    n = mesh.shape["seq"]
    order = tuple(reversed(range(n.bit_length() - 1)))
    in_specs = (
        P("seq", "ctx", None), P("seq", None, "ctx", None), P("seq", "ctx"),
        P("seq", None), P("seq", None), P("seq", None), P("seq", None),
        P("seq"), P("seq"), P("seq"), P("seq"), P("seq"),
        P("seq", None), P("seq"), P("seq", None), P("seq"), P("seq"), P("seq"),
        P("seq", "ctx", None),
    )
    out_specs = (
        P("seq", "ctx", None), P("seq", None, "ctx", None), P("seq", "ctx", None), P("seq", None, "ctx", None),
        P("seq", None), P("seq", None), P("seq", None), P("seq", None),
        P("seq"), P("seq"), P("seq"), P("seq"), P("seq"),
        P("seq", None), P("seq"), P("seq", None), P("seq"), P("seq"), P("seq"),
    )
    return jax.shard_map(
        functools.partial(on_device, n, order),
        mesh=mesh, in_specs=in_specs, out_specs=out_specs, check_vma=False,
    )
```

time: 1300 us -> 546 us (0.42)
  waiting for transfers between devices: 890 us -> 220 us
  matrix products: 163 us -> 0 us
  Pallas kernels: 0 us -> 156 us
  blocking collectives: 109 us -> 0 us
  starting transfers between devices: 0.68 us -> 70.6 us
  between operations: 16.8 us -> 2.14 us
  other arithmetic: 51.6 us -> 37.4 us
    reduce_scatter x5 -> x0, waiting for transfers between devices: 436 us -> none  [the longest x1 166 us: on_device(): lax.psum_scatter(grad_weight_d, 'seq', scatter_dimension=0, tiled=True)]
    all_gather x8 -> x0, waiting for transfers between devices: 237 us -> none  [the longest x1 78.1 us: on_device(): lax.all_gather(w_in, 'seq', axis=0, tiled=True)]
    ppermute x0 -> x76, waiting for transfers between devices: none -> 220 us  [swap(): return lax.ppermute(value, axis, [(i, i ^ step) for i in range(size)])]
    unnamed x20 -> x0, waiting for transfers between devices: 188 us -> none
    dot_general x24 -> x0, matrix products: 163 us -> none  [the longest x6 36.5 us: matmul(): return jnp.dot(first_op, second_op, preferred_element_type=jnp.float32)]
    pallas_call x0 -> x10, Pallas kernels: none -> 156 us  [the longest x3 50.2 us: on_device(): pl.pallas_call(functools.partial(attend_back_kernel, order, n, gp is not...]
    unnamed x2 -> x0, blocking collectives: 71 us -> none
    ppermute x0 -> x76, starting transfers between devices: none -> 70.6 us  [swap(): return lax.ppermute(value, axis, [(i, i ^ step) for i in range(size)])]
  transfers between devices with their start and end apart: 17 -> 76, of which waited for: 15 -> 37; matrix products, arithmetic and copies ran while one was open for 16% -> 14% of each run, Pallas kernels for 0% -> 12%
where the time goes in v1:
time: 546 us; the launch traced here: 538 us
  waiting for transfers between devices  220 us (40%)
  Pallas kernels  156 us (29%)
  starting transfers between devices  70.6 us (13%)
  local copies, waits for them, and re-layouts  51.8 us (9%)
  other arithmetic  37.4 us (7%)
    ppermute x76, waiting for transfers between devices, swap(): return lax.ppermute(value, axis, [(i, i ^ step) for i in range(size)])  220 us
    ppermute x76, starting transfers between devices, swap(): return lax.ppermute(value, axis, [(i, i ^ step) for i in range(size)])  70.6 us
    pallas_call x3, Pallas kernels, on_device(): pl.pallas_call(functools.partial(attend_back_kernel, order, n, gp is not...  50.2 us
    pallas_call x3, Pallas kernels, on_device(): pl.pallas_call(functools.partial(attend_kernel, order, n, raw is not None...  46.5 us
    pallas_call x1, Pallas kernels, on_device(): pl.pallas_call(functools.partial(backward_kernel, order, order, order, n)...  23.8 us
    pallas_call x1, Pallas kernels, on_device(): pl.pallas_call(functools.partial(forward_kernel, order, order, order, n),...  19.2 us
    concatenate x19, other arithmetic, gather_seq(): held = jnp.concatenate([held, swap(held, 'seq', size, bit)], 0)  16 us
    pallas_call x1, Pallas kernels, on_device(): pl.pallas_call(functools.partial(token_kernel, order, n), out_shape=[sds(...  11.4 us
  transfers between devices with their start and end apart: 76, of which 37 were waited for; matrix products, arithmetic and copies ran while one was open for 14% of the time, Pallas kernels for 12%

profile of v1, /device:TPU:0, one launch (start us, length us, event | category | flops | bytes accessed | tf_op | source)
XLA Modules:
  0.0 537.8 jit_solution(16298546022883754577)
XLA Ops:
  0.7 6.2 %concatenate.176 = bf16[1152]{0:T(1024)(128)(2,1)S(1)} concatenate(bf16[96]{0:T(256)(128)(2,1)} %param.39, bf16[96]{0:T(256)(128)(2,1)} %param.40, bf16[96]{0:T(256)(128)(2,1)} %param.41, bf16[96]{0:T(256)(128)(2,1)} %param.42, bf16[96]{0:T(256)(128)(2,1)} %param.43, bf16[96]{0:T(256)(128)(2,1)} %param.47, bf16[96]{0:T(256)(128)(2,1)} %param.48, bf16[96]{0:T(256)(128)(2,1)} %param.49, ...), dimensions={0} | concatenate | bytes 4608 | tf_op jit(solution)/shard_map/concatenate | solution.py:444
  6.9 4.1 collective-permute-start.6
  17.1 2.9 collective-permute-start.2
  22.4 3.0 collective-permute-start.21
  28.8 11.2 %collective-permute-done.27 = bf16[1,192,768]{2,1,0:T(8,128)(2,1)S(1)} collective-permute-done((bf16[1,192,768]{2,1,0:T(8,128)(2,1)S(1)}, bf16[1,192,768]{2,1,0:T(8,128)(2,1)S(1)}, u32[]{:S(2)}, u32[]{:S(2)}) %collective-permute-start.27) | collective-permute-done | bytes 294944 | tf_op jit(solution)/shard_map/ppermute | solution.py:52
  43.1 12.6 %collective-permute-done.7 = bf16[2,1,1152]{2,0,1:T(2,128)(2,1)S(1)} collective-permute-done((bf16[2,1,1152]{2,0,1:T(2,128)(2,1)S(1)}, bf16[2,1,1152]{2,0,1:T(2,128)(2,1)S(1)}, u32[]{:S(2)}, u32[]{:S(2)}) %collective-permute-start.7) | collective-permute-done | bytes 4640 | tf_op jit(solution)/shard_map/ppermute | solution.py:52
  55.8 2.4 collective-permute-start.13
  83.4 20.3 %collective-permute-done.23 = bf16[4,96,768]{2,1,0:T(8,128)(2,1)S(1)} collective-permute-done((bf16[4,96,768]{2,1,0:T(8,128)(2,1)S(1)}, bf16[4,96,768]{2,1,0:T(8,128)(2,1)S(1)}, u32[]{:S(2)}, u32[]{:S(2)}) %collective-permute-start.23) | collective-permute-done | bytes 589856 | tf_op jit(solution)/shard_map/ppermute | solution.py:52
  109.0 5.4 %collective-permute-done.11 = bf16[4,96,384]{2,1,0:T(8,128)(2,1)S(1)} collective-permute-done((bf16[4,96,384]{2,1,0:T(8,128)(2,1)S(1)}, bf16[4,96,384]{2,1,0:T(8,128)(2,1)S(1)}, u32[]{:S(2)}, u32[]{:S(2)}) %collective-permute-start.11) | collective-permute-done | bytes 294944 | tf_op jit(solution)/shard_map/ppermute | solution.py:52
  122.2 4.8 collective-permute-done.15
  156.6 2.7 slice_bitcast_fusion
  159.4 4.5 turn.1.xt_ref
  163.8 15.3 %attend0.1 = (bf16[2,12,256,1024]{3,2,1,0:T(8,128)(2,1)}, bf16[2,4,256,1024]{3,2,1,0:T(8,128)(2,1)}, bf16[2,256,256]{2,1,0:T(8,128)(2,1)}, bf16[2,1024,256]{2,1,...) custom-call(s32[6]{0:T(128)} %stack.66.scal, ...), custom_call_target="tpu_custom_call" | custom-call | tf_op jit(solution)/shard_map/attend0/pallas_call | solution.py:506
  179.2 15.4 %attend1.1 = (bf16[2,12,256,1024]{3,2,1,0:T(8,128)(2,1)}, bf16[2,4,256,1024]{3,2,1,0:T(8,128)(2,1)}, bf16[2,256,256]{2,1,0:T(8,128)(2,1)}, bf16[2,1024,256]{2,1,...) custom-call(s32[6]{0:T(128)} %stack.66.scal, ...), custom_call_target="tpu_custom_call", output_to_operand_aliasing={{0}: (10, {})} | custom-call | tf_op jit(solution)/shard_map/attend1/pallas_call | solution.py:506
  194.5 15.9 %attend2.1 = (bf16[2,12,256,1024]{3,2,1,0:T(8,128)(2,1)}, bf16[2,4,256,1024]{3,2,1,0:T(8,128)(2,1)}, bf16[2,256,256]{2,1,0:T(8,128)(2,1)}, bf16[2,1024,256]{2,1,...) custom-call(s32[6]{0:T(128)} %stack.66.scal, ...), custom_call_target="tpu_custom_call", output_to_operand_aliasing={{0}: (10, {})} | custom-call | tf_op jit(solution)/shard_map/attend2/pallas_call | solution.py:506
  210.4 19.2 %ff_fwd.1 = (bf16[2,256,768]{2,1,0:T(8,128)(2,1)}, f32[512,768]{1,0:T(8,128)}, f32[512,1]{1,0:T(8,128)}, bf16[512,768]{1,0:T(8,128)(2,1)}, bf16[4,512,768]{2,1,0...) custom-call(s32[6]{0:T(128)} %stack.66.scal, ...), custom_call_target="tpu_custom_call" | custom-call | tf_op jit(solution)/shard_map/ff_fwd/pallas_call | solution.py:532
  230.7 23.8 %ff_bwd.1 = (bf16[8,96,768]{2,1,0:T(8,128)(2,1)}, bf16[8,96,768]{2,1,0:T(8,128)(2,1)}, bf16[8,96,768]{2,1,0:T(8,128)(2,1)}, bf16[8,96,768]{2,1,0:T(8,128)(2,1)},...) custom-call(s32[6]{0:T(128)} %stack.66.scal, ...), custom_call_target="tpu_custom_call" | custom-call | tf_op jit(solution)/shard_map/ff_bwd/pallas_call | solution.py:547
  256.6 16.7 %attend_back0.1 = (bf16[2,12,256,1024]{3,2,1,0:T(8,128)(2,1)}, bf16[8,96,384]{2,1,0:T(8,128)(2,1)}, bf16[8,96,384]{2,1,0:T(8,128)(2,1)}, bf16[2,256,256]{2,1,0:T...) custom-call(s32[6]{0:T(128)} %stack.66.scal, bf16[2,4,256,1024]{3,2,1,0:T(8,128)(2,1)} %get-tuple-element.162.e_ref, ...), custom_call_target="tpu_custom_call" | custom-call | tf_op jit(solution)/shard_map/attend_back0/pallas_call | solution.py:602
  274.1 16.5 %attend_back1.1 = (bf16[2,12,256,1024]{3,2,1,0:T(8,128)(2,1)}, bf16[8,96,384]{2,1,0:T(8,128)(2,1)}, bf16[8,96,384]{2,1,0:T(8,128)(2,1)}, bf16[2,256,256]{2,1,0:T...) custom-call(s32[6]{0:T(128)} %stack.66.scal, ...), custom_call_target="tpu_custom_call", output_to_operand_aliasing={{0}: (9, {})} | custom-call | tf_op jit(solution)/shard_map/attend_back1/pallas_call | solution.py:602
  291.4 16.9 %attend_back2.1 = (bf16[2,12,256,1024]{3,2,1,0:T(8,128)(2,1)}, bf16[8,96,384]{2,1,0:T(8,128)(2,1)}, bf16[8,96,384]{2,1,0:T(8,128)(2,1)}, bf16[2,256,256]{2,1,0:T...) custom-call(s32[6]{0:T(128)} %stack.66.scal, ...), custom_call_target="tpu_custom_call", output_to_operand_aliasing={{0}: (9, {})} | custom-call | tf_op jit(solution)/shard_map/attend_back2/pallas_call | solution.py:602
  314.8 2.9 collective-permute-done.58
  317.7 2.7 collective-permute-start.59
  323.6 11.4 %token_grad.1 = (f32[2,256,768]{2,1,0:T(8,128)}, bf16[2,256,768]{2,1,0:T(8,128)(2,1)}, bf16[2,256,768]{2,1,0:T(8,128)(2,1)}, bf16[2,256,768]{2,1,0:T(8,128)(2,1)}) custom-call(s32[6]{0:T(128)} %stack.66.scal, bf16[2,256,256]{2,1,0:T(8,128)(2,1)} %get-tuple-element.175.dq0, bf16[2,256,256]{2,1,0:T(8,128)(2,1)} %get-tuple-element.182.dq1, ...), custom_call_target="tpu_custom_call" | custom-call | tf_op jit(solution)/shard_map/token_grad/pallas_call | solution.py:624
  342.5 7.0 %collective-permute-done.52 = bf16[4,96,384]{2,1,0:T(8,128)(2,1)S(1)} collective-permute-done((bf16[4,96,384]{2,1,0:T(8,128)(2,1)S(1)}, bf16[4,96,384]{2,1,0:T(8,128)(2,1)S(1)}, u32[]{:S(2)}, u32[]{:S(2)}) %collective-permute-start.52) | collective-permute-done | bytes 294944 | tf_op jit(solution)/shard_map/ppermute | solution.py:52
  351.1 4.8 collective-permute-done.34
  357.4 4.7 collective-permute-done.40
  362.2 5.8 %collective-permute-done.46 = bf16[4,96,384]{2,1,0:T(8,128)(2,1)S(1)} collective-permute-done((bf16[4,96,384]{2,1,0:T(8,128)(2,1)S(1)}, bf16[4,96,384]{2,1,0:T(8,128)(2,1)S(1)}, u32[]{:S(2)}, u32[]{:S(2)}) %collective-permute-start.46) | collective-permute-done | bytes 294944 | tf_op jit(solution)/shard_map/ppermute | solution.py:52
  370.2 3.6 collective-permute-done.53
  375.6 3.3 collective-permute-done.35
  380.7 3.9 collective-permute-done.41
  386.8 3.9 collective-permute-done.47
  390.7 2.7 collective-permute-start.54
  393.4 4.0 collective-permute-done.54
  398.6 5.9 %collective-permute-done.36 = bf16[1,96,384]{2,1,0:T(8,128)(2,1)S(1)} collective-permute-done((bf16[1,96,384]{2,1,0:T(8,128)(2,1)S(1)}, bf16[1,96,384]{2,1,0:T(8,128)(2,1)S(1)}, u32[]{:S(2)}, u32[]{:S(2)}) %collective-permute-start.36) | collective-permute-done | bytes 73760 | tf_op jit(solution)/shard_map/ppermute | solution.py:52
  404.5 5.7 %collective-permute-done.42 = bf16[1,96,384]{2,1,0:T(8,128)(2,1)S(1)} collective-permute-done((bf16[1,96,384]{2,1,0:T(8,128)(2,1)S(1)}, bf16[1,96,384]{2,1,0:T(8,128)(2,1)S(1)}, u32[]{:S(2)}, u32[]{:S(2)}) %collective-permute-start.42) | collective-permute-done | bytes 73760 | tf_op jit(solution)/shard_map/ppermute | solution.py:52
  410.3 5.3 collective-permute-done.48
  416.1 3.8 collective-permute-done.55
  420.4 3.8 collective-permute-done.37
  424.8 3.8 collective-permute-done.43
  429.1 3.8 collective-permute-done.49
  437.7 25.0 %collective-permute-done.64 = bf16[8,96,768]{2,1,0:T(8,128)(2,1)S(1)} collective-permute-done((bf16[8,96,768]{2,1,0:T(8,128)(2,1)S(1)}, bf16[8,96,768]{2,1,0:T(8,128)(2,1)S(1)}, u32[]{:S(2)}, u32[]{:S(2)}) %collective-permute-start.64) | collective-permute-done | bytes 1179680 | tf_op jit(solution)/shard_map/ppermute | solution.py:52
  464.9 13.2 %collective-permute-done.65 = bf16[4,96,768]{2,1,0:T(8,128)(2,1)S(1)} collective-permute-done((bf16[4,96,768]{2,1,0:T(8,128)(2,1)S(1)}, bf16[4,96,768]{2,1,0:T(8,128)(2,1)S(1)}, u32[]{:S(2)}, u32[]{:S(2)}) %collective-permute-start.65) | collective-permute-done | bytes 589856 | tf_op jit(solution)/shard_map/ppermute | solution.py:52
  482.4 7.5 %collective-permute-done.66 = bf16[2,96,768]{2,1,0:T(8,128)(2,1)S(1)} collective-permute-done((bf16[2,96,768]{2,1,0:T(8,128)(2,1)S(1)}, bf16[2,96,768]{2,1,0:T(8,128)(2,1)S(1)}, u32[]{:S(2)}, u32[]{:S(2)}) %collective-permute-start.66) | collective-permute-done | bytes 294944 | tf_op jit(solution)/shard_map/ppermute | solution.py:52
  490.2 11.5 %collective-permute-done.72 = bf16[2,192,768]{2,1,0:T(8,128)(2,1)S(1)} collective-permute-done((bf16[2,192,768]{2,1,0:T(8,128)(2,1)S(1)}, bf16[2,192,768]{2,1,0:T(8,128)(2,1)S(1)}, u32[]{:S(2)}, u32[]{:S(2)}) %collective-permute-start.72) | collective-permute-done | bytes 589856 | tf_op jit(solution)/shard_map/ppermute | solution.py:52
  504.7 10.7 %collective-permute-done.73 = bf16[1,192,768]{2,1,0:T(8,128)(2,1)S(1)} collective-permute-done((bf16[1,192,768]{2,1,0:T(8,128)(2,1)S(1)}, bf16[1,192,768]{2,1,0:T(8,128)(2,1)S(1)}, u32[]{:S(2)}, u32[]{:S(2)}) %collective-permute-start.73) | collective-permute-done | bytes 294944 | tf_op jit(solution)/shard_map/ppermute | solution.py:52
  517.8 8.1 %collective-permute-done.68 = bf16[96,768]{1,0:T(8,128)(2,1)S(1)} collective-permute-done((bf16[96,768]{1,0:T(8,128)(2,1)S(1)}, bf16[96,768]{1,0:T(8,128)(2,1)S(1)}, u32[]{:S(2)}, u32[]{:S(2)}) %collective-permute-start.68) | collective-permute-done | bytes 147488 | tf_op jit(solution)/shard_map/ppermute | solution.py:52
  526.0 3.0 collective-permute-done.74
  533.3 3.2 reshape.379
  (392 shorter events, 140.6 us)
Async XLA Ops:
  6.9 34.2 %collective-permute-start.6 = (bf16[1,1,1152]{2,0,1:T(2,128)(2,1)S(1)}, bf16[1,1,1152]{2,0,1:T(2,128)(2,1)S(1)}, u32[]{:S(2)}, u32[]{:S(2)}) collective-permute-start(bf16[1,1,1152]{2,0,1:T(2,128)(2,1)S(1)} %broadcast_in_dim_broadcast_in_dim.3), channel_id=1, source_target_pairs={{0,16},{4,20},{8,24},{12,28},{16,0},{20,4},{24,8},{28,12},{1,17},{... | collective-permute-start | bytes 6920 | tf_op jit(solution)/shard_map/ppermute | solution.py:52
  11.9 46.3 %collective-permute-start.17 = (bf16[1,96,384]{2,1,0:T(8,128)(2,1)S(1)}, bf16[1,96,384]{2,1,0:T(8,128)(2,1)}, u32[]{:S(2)}, u32[]{:S(2)}) collective-permute-start(bf16[1,96,384]{2,1,0:T(8,128)(2,1)S(1)} %select_bitcast_fusion), channel_id=1, source_target_pairs={{0,16},{4,20},{8,24},{12,28},{16,0},{20,4},{24,8},{28,12},{1,17},{... | collective-permute-start | bytes 221192 | tf_op jit(solution)/shard_map/ppermute | solution.py:52
  17.1 50.9 %collective-permute-start.2 = (bf16[1,96,384]{2,1,0:T(8,128)(2,1)}, bf16[1,96,384]{2,1,0:T(8,128)(2,1)}, u32[]{:S(2)}, u32[]{:S(2)}) collective-permute-start(bf16[1,96,384]{2,1,0:T(8,128)(2,1)} %fusion.16), channel_id=1, source_target_pairs={{0,16},{4,20},{8,24},{12,28},{16,0},{20,4},{24,8},{28,12},{1,17},{... | collective-permute-start | bytes 221192 | tf_op jit(solution)/shard_map/ppermute | solution.py:52
  20.1 20.0 %collective-permute-start.27 = (bf16[1,192,768]{2,1,0:T(8,128)(2,1)S(1)}, bf16[1,192,768]{2,1,0:T(8,128)(2,1)S(1)}, u32[]{:S(2)}, u32[]{:S(2)}) collective-permute-start(bf16[1,192,768]{2,1,0:T(8,128)(2,1)S(1)} %constant_dynamic-slice_fusion), channel_id=1, source_target_pairs={{0,16},{4,20},{8,24},{12,28},{16,0},{20,4},{24,8},{28,12},{1,17},{... | collective-permute-start | bytes 884744 | tf_op jit(solution)/shard_map/ppermute | solution.py:52
  22.4 37.3 %collective-permute-start.21 = (bf16[1,96,768]{2,1,0:T(8,128)(2,1)S(1)}, bf16[1,96,768]{2,1,0:T(8,128)(2,1)}, u32[]{:S(2)}, u32[]{:S(2)}) collective-permute-start(bf16[1,96,768]{2,1,0:T(8,128)(2,1)S(1)} %broadcast_in_dim_reshape.3), channel_id=1, source_target_pairs={{0,16},{4,20},{8,24},{12,28},{16,0},{20,4},{24,8},{28,12},{1,17},{... | collective-permute-start | bytes 442376 | tf_op jit(solution)/shard_map/ppermute | solution.py:52
  40.9 21.3 %collective-permute-start.28 = (bf16[2,192,768]{2,1,0:T(8,128)(2,1)}, bf16[2,192,768]{2,1,0:T(8,128)(2,1)S(1)}, u32[]{:S(2)}, u32[]{:S(2)}) collective-permute-start(bf16[2,192,768]{2,1,0:T(8,128)(2,1)} %pad_maximum_fusion.9), channel_id=1, source_target_pairs={{0,8},{4,12},{8,0},{12,4},{16,24},{20,28},{24,16},{28,20},{1,9},{5... | collective-permute-start | bytes 1769480 | tf_op jit(solution)/shard_map/ppermute | solution.py:52
  41.1 14.7 %collective-permute-start.7 = (bf16[2,1,1152]{2,0,1:T(2,128)(2,1)S(1)}, bf16[2,1,1152]{2,0,1:T(2,128)(2,1)S(1)}, u32[]{:S(2)}, u32[]{:S(2)}) collective-permute-start(bf16[2,1,1152]{2,0,1:T(2,128)(2,1)S(1)} %pad_maximum_fusion.29), channel_id=1, source_target_pairs={{0,8},{4,12},{8,0},{12,4},{16,24},{20,28},{24,16},{28,20},{1,9},{5... | collective-permute-start | bytes 13832 | tf_op jit(solution)/shard_map/ppermute | solution.py:52
  59.7 21.0 %collective-permute-start = (bf16[2,272,768]{2,1,0:T(8,128)(2,1)S(1)}, bf16[2,272,768]{2,1,0:T(8,128)(2,1)S(1)}, u32[]{:S(2)}, u32[]{:S(2)}) collective-permute-start(bf16[2,272,768]{2,1,0:T(8,128)(2,1)S(1)} %get-tuple-element.232.t0), channel_id=1, source_target_pairs={{0,2},{1,3},{2,0},{3,1},{4,6},{5,7},{6,4},{7,5},{8,10},{9,11},{10,... | collective-permute-start | bytes 2506760 | tf_op jit(solution)/shard_map/ppermute | solution.py:52
  62.3 10.0 %collective-permute-start.22 = (bf16[2,96,768]{2,1,0:T(8,128)(2,1)S(1)}, bf16[2,96,768]{2,1,0:T(8,128)(2,1)S(1)}, u32[]{:S(2)}, u32[]{:S(2)}) collective-permute-start(bf16[2,96,768]{2,1,0:T(8,128)(2,1)S(1)} %pad_maximum_fusion.14), channel_id=1, source_target_pairs={{0,8},{4,12},{8,0},{12,4},{16,24},{20,28},{24,16},{28,20},{1,9},{5... | collective-permute-start | bytes 884744 | tf_op jit(solution)/shard_map/ppermute | solution.py:52
  64.8 41.3 %collective-permute-start.29 = (bf16[4,192,768]{2,1,0:T(8,128)(2,1)S(1)}, bf16[4,192,768]{2,1,0:T(8,128)(2,1)S(1)}, u32[]{:S(2)}, u32[]{:S(2)}) collective-permute-start(bf16[4,192,768]{2,1,0:T(8,128)(2,1)S(1)} %pad_maximum_fusion.3), channel_id=1, source_target_pairs={{0,4},{4,0},{8,12},{12,8},{16,20},{20,16},{24,28},{28,24},{1,5},{5... | collective-permute-start | bytes 3538952 | tf_op jit(solution)/shard_map/ppermute | solution.py:52
  66.4 12.8 %collective-permute-start.14 = (bf16[2,96,384]{2,1,0:T(8,128)(2,1)S(1)}, bf16[2,96,384]{2,1,0:T(8,128)(2,1)S(1)}, u32[]{:S(2)}, u32[]{:S(2)}) collective-permute-start(bf16[2,96,384]{2,1,0:T(8,128)(2,1)S(1)} %pad_maximum_fusion.20), channel_id=1, source_target_pairs={{0,8},{4,12},{8,0},{12,4},{16,24},{20,28},{24,16},{28,20},{1,9},{5... | collective-permute-start | bytes 442376 | tf_op jit(solution)/shard_map/ppermute | solution.py:52
  73.3 30.4 %collective-permute-start.23 = (bf16[4,96,768]{2,1,0:T(8,128)(2,1)S(1)}, bf16[4,96,768]{2,1,0:T(8,128)(2,1)S(1)}, u32[]{:S(2)}, u32[]{:S(2)}) collective-permute-start(bf16[4,96,768]{2,1,0:T(8,128)(2,1)S(1)} %pad_maximum_fusion.8), channel_id=1, source_target_pairs={{0,4},{4,0},{8,12},{12,8},{16,20},{20,16},{24,28},{28,24},{1,5},{5... | collective-permute-start | bytes 1769480 | tf_op jit(solution)/shard_map/ppermute | solution.py:52
  76.8 27.7 %collective-permute-start.8 = (bf16[4,1,1152]{2,0,1:T(4,128)(2,1)S(1)}, bf16[4,1,1152]{2,0,1:T(4,128)(2,1)S(1)}, u32[]{:S(2)}, u32[]{:S(2)}) collective-permute-start(bf16[4,1,1152]{2,0,1:T(4,128)(2,1)S(1)} %pad_maximum_fusion.28), channel_id=1, source_target_pairs={{0,4},{4,0},{8,12},{12,8},{16,20},{20,16},{24,28},{28,24},{1,5},{5... | collective-permute-start | bytes 27656 | tf_op jit(solution)/shard_map/ppermute | solution.py:52
  79.2 27.6 %collective-permute-start.3 = (bf16[2,96,384]{2,1,0:T(8,128)(2,1)S(1)}, bf16[2,96,384]{2,1,0:T(8,128)(2,1)S(1)}, u32[]{:S(2)}, u32[]{:S(2)}) collective-permute-start(bf16[2,96,384]{2,1,0:T(8,128)(2,1)S(1)} %pad_maximum_fusion.18), channel_id=1, source_target_pairs={{0,8},{4,12},{8,0},{12,4},{16,24},{20,28},{24,16},{28,20},{1,9},{5... | collective-permute-start | bytes 442376 | tf_op jit(solution)/shard_map/ppermute | solution.py:52
  80.7 27.4 %collective-permute-start.18 = (bf16[2,96,384]{2,1,0:T(8,128)(2,1)S(1)}, bf16[2,96,384]{2,1,0:T(8,128)(2,1)S(1)}, u32[]{:S(2)}, u32[]{:S(2)}) collective-permute-start(bf16[2,96,384]{2,1,0:T(8,128)(2,1)S(1)} %pad_maximum_fusion.21), channel_id=1, source_target_pairs={{0,8},{4,12},{8,0},{12,4},{16,24},{20,28},{24,16},{28,20},{1,9},{5... | collective-permute-start | bytes 442376 | tf_op jit(solution)/shard_map/ppermute | solution.py:52
  103.7 37.5 %collective-permute-start.1 = (bf16[2,2,272,768]{3,2,1,0:T(8,128)(2,1)}, bf16[2,2,272,768]{3,2,1,0:T(8,128)(2,1)}, u32[]{:S(2)}, u32[]{:S(2)}) collective-permute-start(bf16[2,2,272,768]{3,2,1,0:T(8,128)(2,1)} %pad_maximum_fusion.1), channel_id=1, source_target_pairs={{0,1},{1,0},{2,3},{3,2},{4,5},{5,4},{6,7},{7,6},{8,9},{9,8},{10,11... | collective-permute-start | bytes 5013512 | tf_op jit(solution)/shard_map/ppermute | solution.py:52
  106.1 31.4 %collective-permute-start.25 = (bf16[8,96,768]{2,1,0:T(8,128)(2,1)}, bf16[8,96,768]{2,1,0:T(8,128)(2,1)}, u32[]{:S(2)}, u32[]{:S(2)}) collective-permute-start(bf16[8,96,768]{2,1,0:T(8,128)(2,1)} %constant_dynamic-update-slice_fusion.i0), channel_id=1, source_target_pairs={{0,2},{1,3},{2,0},{3,1},{4,6},{5,7},{6,4},{7,5},{8,10},{9,11},{10,... | collective-permute-start | bytes 3538952 | tf_op jit(solution)/shard_map/ppermute | solution.py:52
  106.9 103.6 %collective-permute-start.30 = (bf16[8,192,768]{2,1,0:T(8,128)(2,1)S(1)}, bf16[8,192,768]{2,1,0:T(8,128)(2,1)}, u32[]{:S(2)}, u32[]{:S(2)}) collective-permute-start(bf16[8,192,768]{2,1,0:T(8,128)(2,1)S(1)} %pad_maximum_fusion), channel_id=1, source_target_pairs={{0,1},{1,0},{2,3},{3,2},{4,5},{5,4},{6,7},{7,6},{8,9},{9,8},{10,11... | collective-permute-start | bytes 7077896 | tf_op jit(solution)/shard_map/ppermute | solution.py:52
  108.1 12.6 %collective-permute-start.4 = (bf16[4,96,384]{2,1,0:T(8,128)(2,1)S(1)}, bf16[4,96,384]{2,1,0:T(8,128)(2,1)S(1)}, u32[]{:S(2)}, u32[]{:S(2)}) collective-permute-start(bf16[4,96,384]{2,1,0:T(8,128)(2,1)S(1)} %pad_maximum_fusion.10), channel_id=1, source_target_pairs={{0,4},{4,0},{8,12},{12,8},{16,20},{20,16},{24,28},{28,24},{1,5},{5... | collective-permute-start | bytes 884744 | tf_op jit(solution)/shard_map/ppermute | solution.py:52
  114.4 12.6 %collective-permute-start.15 = (bf16[4,96,384]{2,1,0:T(8,128)(2,1)S(1)}, bf16[4,96,384]{2,1,0:T(8,128)(2,1)S(1)}, u32[]{:S(2)}, u32[]{:S(2)}) collective-permute-start(bf16[4,96,384]{2,1,0:T(8,128)(2,1)S(1)} %pad_maximum_fusion.12), channel_id=1, source_target_pairs={{0,4},{4,0},{8,12},{12,8},{16,20},{20,16},{24,28},{28,24},{1,5},{5... | collective-permute-start | bytes 884744 | tf_op jit(solution)/shard_map/ppermute | solution.py:52
  120.7 12.4 %collective-permute-start.19 = (bf16[4,96,384]{2,1,0:T(8,128)(2,1)}, bf16[4,96,384]{2,1,0:T(8,128)(2,1)}, u32[]{:S(2)}, u32[]{:S(2)}) collective-permute-start(bf16[4,96,384]{2,1,0:T(8,128)(2,1)} %pad_maximum_fusion.13), channel_id=1, source_target_pairs={{0,4},{4,0},{8,12},{12,8},{16,20},{20,16},{24,28},{28,24},{1,5},{5... | collective-permute-start | bytes 884744 | tf_op jit(solution)/shard_map/ppermute | solution.py:52
  127.0 10.0 %collective-permute-start.12 = (bf16[8,96,384]{2,1,0:T(8,128)(2,1)S(1)}, bf16[8,96,384]{2,1,0:T(8,128)(2,1)}, u32[]{:S(2)}, u32[]{:S(2)}) collective-permute-start(bf16[8,96,384]{2,1,0:T(8,128)(2,1)S(1)} %pad_maximum_fusion.5.w_own.own1), channel_id=1, source_target_pairs={{0,1},{1,0},{2,3},{3,2},{4,5},{5,4},{6,7},{7,6},{8,9},{9,8},{10,11... | collective-permute-start | bytes 1769480 | tf_op jit(solution)/shard_map/ppermute | solution.py:52
  137.0 73.5 %collective-permute-start.24 = (bf16[8,96,768]{2,1,0:T(8,128)(2,1)}, bf16[8,96,768]{2,1,0:T(8,128)(2,1)}, u32[]{:S(2)}, u32[]{:S(2)}) collective-permute-start(bf16[8,96,768]{2,1,0:T(8,128)(2,1)} %constant_dynamic-update-slice_fusion.i0), channel_id=1, source_target_pairs={{0,1},{1,0},{2,3},{3,2},{4,5},{5,4},{6,7},{7,6},{8,9},{9,8},{10,11... | collective-permute-start | bytes 3538952 | tf_op jit(solution)/shard_map/ppermute | solution.py:52
  137.5 73.0 %collective-permute-start.26 = (bf16[8,96,768]{2,1,0:T(8,128)(2,1)}, bf16[8,96,768]{2,1,0:T(8,128)(2,1)}, u32[]{:S(2)}, u32[]{:S(2)}) collective-permute-start(bf16[8,96,768]{2,1,0:T(8,128)(2,1)} %collective-permute-done.25.i2), channel_id=1, source_target_pairs={{0,1},{1,0},{2,3},{3,2},{4,5},{5,4},{6,7},{7,6},{8,9},{9,8},{10,11... | collective-permute-start | bytes 3538952 | tf_op jit(solution)/shard_map/ppermute | solution.py:52
  140.7 69.7 %collective-permute-start.20 = (bf16[8,96,384]{2,1,0:T(8,128)(2,1)S(1)}, bf16[8,96,384]{2,1,0:T(8,128)(2,1)}, u32[]{:S(2)}, u32[]{:S(2)}) collective-permute-start(bf16[8,96,384]{2,1,0:T(8,128)(2,1)S(1)} %pad_maximum_fusion.7.wo_own), channel_id=1, source_target_pairs={{0,1},{1,0},{2,3},{3,2},{4,5},{5,4},{6,7},{7,6},{8,9},{9,8},{10,11... | collective-permute-start | bytes 1769480 | tf_op jit(solution)/shard_map/ppermute | solution.py:52
  141.2 53.3 %collective-permute-start.16 = (bf16[8,96,384]{2,1,0:T(8,128)(2,1)}, bf16[8,96,384]{2,1,0:T(8,128)(2,1)}, u32[]{:S(2)}, u32[]{:S(2)}) collective-permute-start(bf16[8,96,384]{2,1,0:T(8,128)(2,1)} %pad_maximum_fusion.6.w_own.own2), channel_id=1, source_target_pairs={{0,1},{1,0},{2,3},{3,2},{4,5},{5,4},{6,7},{7,6},{8,9},{9,8},{10,11... | collective-permute-start | bytes 1769480 | tf_op jit(solution)/shard_map/ppermute | solution.py:52
  314.8 23.9 %collective-permute-start.51 = (bf16[8,96,384]{2,1,0:T(8,128)(2,1)}, bf16[8,96,384]{2,1,0:T(8,128)(2,1)S(1)}, u32[]{:S(2)}, u32[]{:S(2)}) collective-permute-start(bf16[8,96,384]{2,1,0:T(8,128)(2,1)} %get-tuple-element.206), channel_id=1, source_target_pairs={{0,1},{1,0},{2,3},{3,2},{4,5},{5,4},{6,7},{7,6},{8,9},{9,8},{10,11... | collective-permute-start | bytes 1769480 | tf_op jit(solution)/shard_map/ppermute | solution.py:52
  322.3 12.7 %collective-permute-start.60 = (f32[1152]{0:T(1024)S(1)}, f32[1152]{0:T(1024)S(1)}, u32[]{:S(2)}, u32[]{:S(2)}) collective-permute-start(f32[1152]{0:T(1024)S(1)} %fusion.17), channel_id=1, source_target_pairs={{0,2},{1,3},{2,0},{3,1},{4,6},{5,7},{6,4},{7,5},{8,10},{9,11},{10,... | collective-permute-start | bytes 13832 | tf_op jit(solution)/shard_map/ppermute | solution.py:52
  323.1 113.0 %collective-permute-start.62 = (bf16[8,96,768]{2,1,0:T(8,128)(2,1)}, bf16[8,96,768]{2,1,0:T(8,128)(2,1)S(1)}, u32[]{:S(2)}, u32[]{:S(2)}) collective-permute-start(bf16[8,96,768]{2,1,0:T(8,128)(2,1)} %get-tuple-element.214), channel_id=1, source_target_pairs={{0,1},{1,0},{2,3},{3,2},{4,5},{5,4},{6,7},{7,6},{8,9},{9,8},{10,11... | collective-permute-start | bytes 3538952 | tf_op jit(solution)/shard_map/ppermute | solution.py:52
  323.1 109.9 %collective-permute-start.63 = (bf16[8,96,768]{2,1,0:T(8,128)(2,1)}, bf16[8,96,768]{2,1,0:T(8,128)(2,1)S(1)}, u32[]{:S(2)}, u32[]{:S(2)}) collective-permute-start(bf16[8,96,768]{2,1,0:T(8,128)(2,1)} %get-tuple-element.216), channel_id=1, source_target_pairs={{0,1},{1,0},{2,3},{3,2},{4,5},{5,4},{6,7},{7,6},{8,9},{9,8},{10,11... | collective-permute-start | bytes 3538952 | tf_op jit(solution)/shard_map/ppermute | solution.py:52
  323.6 15.7 %collective-permute-start.33 = (bf16[8,96,384]{2,1,0:T(8,128)(2,1)}, bf16[8,96,384]{2,1,0:T(8,128)(2,1)S(1)}, u32[]{:S(2)}, u32[]{:S(2)}) collective-permute-start(bf16[8,96,384]{2,1,0:T(8,128)(2,1)} %get-tuple-element.200), channel_id=1, source_target_pairs={{0,1},{1,0},{2,3},{3,2},{4,5},{5,4},{6,7},{7,6},{8,9},{9,8},{10,11... | collective-permute-start | bytes 1769480 | tf_op jit(solution)/shard_map/ppermute | solution.py:52
  339.3 95.8 %collective-permute-start.70 = (bf16[8,2,96,768]{3,2,1,0:T(8,128)(2,1)S(1)}, bf16[8,2,96,768]{3,2,1,0:T(8,128)(2,1)S(1)}, u32[]{:S(2)}, u32[]{:S(2)}) collective-permute-start(bf16[8,2,96,768]{3,2,1,0:T(8,128)(2,1)S(1)} %copy-done.50), channel_id=1, source_target_pairs={{0,1},{1,0},{2,3},{3,2},{4,5},{5,4},{6,7},{7,6},{8,9},{9,8},{10,11... | collective-permute-start | bytes 7077896 | tf_op jit(solution)/shard_map/ppermute | solution.py:52
  341.4 14.4 %collective-permute-start.34 = (bf16[4,96,384]{2,1,0:T(8,128)(2,1)S(1)}, bf16[4,96,384]{2,1,0:T(8,128)(2,1)S(1)}, u32[]{:S(2)}, u32[]{:S(2)}) collective-permute-start(bf16[4,96,384]{2,1,0:T(8,128)(2,1)S(1)} %slice.528), channel_id=1, source_target_pairs={{0,4},{4,0},{8,12},{12,8},{16,20},{20,16},{24,28},{28,24},{1,5},{5... | collective-permute-start | bytes 884744 | tf_op jit(solution)/shard_map/ppermute | solution.py:52
  349.5 12.6 %collective-permute-start.40 = (bf16[4,96,384]{2,1,0:T(8,128)(2,1)S(1)}, bf16[4,96,384]{2,1,0:T(8,128)(2,1)S(1)}, u32[]{:S(2)}, u32[]{:S(2)}) collective-permute-start(bf16[4,96,384]{2,1,0:T(8,128)(2,1)S(1)} %slice.535), channel_id=1, source_target_pairs={{0,4},{4,0},{8,12},{12,8},{16,20},{20,16},{24,28},{28,24},{1,5},{5... | collective-permute-start | bytes 884744 | tf_op jit(solution)/shard_map/ppermute | solution.py:52
  355.8 12.2 %collective-permute-start.46 = (bf16[4,96,384]{2,1,0:T(8,128)(2,1)S(1)}, bf16[4,96,384]{2,1,0:T(8,128)(2,1)S(1)}, u32[]{:S(2)}, u32[]{:S(2)}) collective-permute-start(bf16[4,96,384]{2,1,0:T(8,128)(2,1)S(1)} %slice.542), channel_id=1, source_target_pairs={{0,4},{4,0},{8,12},{12,8},{16,20},{20,16},{24,28},{28,24},{1,5},{5... | collective-permute-start | bytes 884744 | tf_op jit(solution)/shard_map/ppermute | solution.py:52
  362.1 140.1 %collective-permute-start.31 = (bf16[2,2,256,768]{3,2,1,0:T(8,128)(2,1)S(1)}, bf16[2,2,256,768]{3,2,1,0:T(8,128)(2,1)S(1)}, u32[]{:S(2)}, u32[]{:S(2)}) collective-permute-start(bf16[2,2,256,768]{3,2,1,0:T(8,128)(2,1)S(1)} %pad_maximum_fusion.2), channel_id=1, source_target_pairs={{0,1},{1,0},{2,3},{3,2},{4,5},{5,4},{6,7},{7,6},{8,9},{9,8},{10,11... | collective-permute-start | bytes 4718600 | tf_op jit(solution)/shard_map/ppermute | solution.py:52
  434.2 30.6 %collective-permute-start.56 = (bf16[96,384]{1,0:T(8,128)(2,1)S(1)}, bf16[96,384]{1,0:T(8,128)(2,1)S(1)}, u32[]{:S(2)}, u32[]{:S(2)}) collective-permute-start(bf16[96,384]{1,0:T(8,128)(2,1)S(1)} %add_convert_fusion.22), channel_id=1, source_target_pairs={{0,1},{1,0},{2,3},{3,2},{4,5},{5,4},{6,7},{7,6},{8,9},{9,8},{10,11... | collective-permute-start | bytes 221192 | tf_op jit(solution)/shard_map/ppermute | solution.py:52
  434.5 28.2 %collective-permute-start.64 = (bf16[8,96,768]{2,1,0:T(8,128)(2,1)S(1)}, bf16[8,96,768]{2,1,0:T(8,128)(2,1)S(1)}, u32[]{:S(2)}, u32[]{:S(2)}) collective-permute-start(bf16[8,96,768]{2,1,0:T(8,128)(2,1)S(1)} %add_convert_fusion.2), channel_id=1, source_target_pairs={{0,2},{1,3},{2,0},{3,1},{4,6},{5,7},{6,4},{7,5},{8,10},{9,11},{10,... | collective-permute-start | bytes 3538952 | tf_op jit(solution)/shard_map/ppermute | solution.py:52
  435.1 29.7 %collective-permute-start.50 = (bf16[96,384]{1,0:T(8,128)(2,1)S(1)}, bf16[96,384]{1,0:T(8,128)(2,1)S(1)}, u32[]{:S(2)}, u32[]{:S(2)}) collective-permute-start(bf16[96,384]{1,0:T(8,128)(2,1)S(1)} %add_convert_fusion.24), channel_id=1, source_target_pairs={{0,1},{1,0},{2,3},{3,2},{4,5},{5,4},{6,7},{7,6},{8,9},{9,8},{10,11... | collective-permute-start | bytes 221192 | tf_op jit(solution)/shard_map/ppermute | solution.py:52
  436.2 42.2 %collective-permute-start.71 = (bf16[4,192,768]{2,1,0:T(8,128)(2,1)S(1)}, bf16[4,192,768]{2,1,0:T(8,128)(2,1)S(1)}, u32[]{:S(2)}, u32[]{:S(2)}) collective-permute-start(bf16[4,192,768]{2,1,0:T(8,128)(2,1)S(1)} %bitcast.79), channel_id=1, source_target_pairs={{0,4},{4,0},{8,12},{12,8},{16,20},{20,16},{24,28},{28,24},{1,5},{5... | collective-permute-start | bytes 3538952 | tf_op jit(solution)/shard_map/ppermute | solution.py:52
  463.3 14.8 %collective-permute-start.65 = (bf16[4,96,768]{2,1,0:T(8,128)(2,1)S(1)}, bf16[4,96,768]{2,1,0:T(8,128)(2,1)S(1)}, u32[]{:S(2)}, u32[]{:S(2)}) collective-permute-start(bf16[4,96,768]{2,1,0:T(8,128)(2,1)S(1)} %slice.572), channel_id=1, source_target_pairs={{0,4},{4,0},{8,12},{12,8},{16,20},{20,16},{24,28},{28,24},{1,5},{5... | collective-permute-start | bytes 1769480 | tf_op jit(solution)/shard_map/ppermute | solution.py:52
  478.3 11.6 %collective-permute-start.66 = (bf16[2,96,768]{2,1,0:T(8,128)(2,1)S(1)}, bf16[2,96,768]{2,1,0:T(8,128)(2,1)S(1)}, u32[]{:S(2)}, u32[]{:S(2)}) collective-permute-start(bf16[2,96,768]{2,1,0:T(8,128)(2,1)S(1)} %slice.574), channel_id=1, source_target_pairs={{0,8},{4,12},{8,0},{12,4},{16,24},{20,28},{24,16},{28,20},{1,9},{5... | collective-permute-start | bytes 884744 | tf_op jit(solution)/shard_map/ppermute | solution.py:52
  478.8 22.9 %collective-permute-start.72 = (bf16[2,192,768]{2,1,0:T(8,128)(2,1)S(1)}, bf16[2,192,768]{2,1,0:T(8,128)(2,1)S(1)}, u32[]{:S(2)}, u32[]{:S(2)}) collective-permute-start(bf16[2,192,768]{2,1,0:T(8,128)(2,1)S(1)} %slice.581), channel_id=1, source_target_pairs={{0,8},{4,12},{8,0},{12,4},{16,24},{20,28},{24,16},{28,20},{1,9},{5... | collective-permute-start | bytes 1769480 | tf_op jit(solution)/shard_map/ppermute | solution.py:52
  490.0 13.2 %collective-permute-start.67 = (bf16[1,96,768]{2,1,0:T(8,128)(2,1)S(1)}, bf16[1,96,768]{2,1,0:T(8,128)(2,1)S(1)}, u32[]{:S(2)}, u32[]{:S(2)}) collective-permute-start(bf16[1,96,768]{2,1,0:T(8,128)(2,1)S(1)} %slice.576), channel_id=1, source_target_pairs={{0,16},{4,20},{8,24},{12,28},{16,0},{20,4},{24,8},{28,12},{1,17},{... | collective-permute-start | bytes 442376 | tf_op jit(solution)/shard_map/ppermute | solution.py:52
  502.0 13.4 %collective-permute-start.73 = (bf16[1,192,768]{2,1,0:T(8,128)(2,1)S(1)}, bf16[1,192,768]{2,1,0:T(8,128)(2,1)S(1)}, u32[]{:S(2)}, u32[]{:S(2)}) collective-permute-start(bf16[1,192,768]{2,1,0:T(8,128)(2,1)S(1)} %slice.583), channel_id=1, source_target_pairs={{0,16},{4,20},{8,24},{12,28},{16,0},{20,4},{24,8},{28,12},{1,17},{... | collective-permute-start | bytes 884744 | tf_op jit(solution)/shard_map/ppermute | solution.py:52
  502.5 26.7 %collective-permute-start.32 = (bf16[2,256,768]{2,1,0:T(8,128)(2,1)S(1)}, bf16[2,256,768]{2,1,0:T(8,128)(2,1)S(1)}, u32[]{:S(2)}, u32[]{:S(2)}) collective-permute-start(bf16[2,256,768]{2,1,0:T(8,128)(2,1)S(1)} %fusion.2), channel_id=1, source_target_pairs={{0,2},{1,3},{2,0},{3,1},{4,6},{5,7},{6,4},{7,5},{8,10},{9,11},{10,... | collective-permute-start | bytes 2359304 | tf_op jit(solution)/shard_map/ppermute | solution.py:52
  503.3 22.6 %collective-permute-start.68 = (bf16[96,768]{1,0:T(8,128)(2,1)S(1)}, bf16[96,768]{1,0:T(8,128)(2,1)S(1)}, u32[]{:S(2)}, u32[]{:S(2)}) collective-permute-start(bf16[96,768]{1,0:T(8,128)(2,1)S(1)} %bitcast.78), channel_id=1, source_target_pairs={{0,2},{1,3},{2,0},{3,1},{4,6},{5,7},{6,4},{7,5},{8,10},{9,11},{10,... | collective-permute-start | bytes 442376 | tf_op jit(solution)/shard_map/ppermute | solution.py:52
  515.5 13.6 %collective-permute-start.74 = (bf16[192,768]{1,0:T(8,128)(2,1)S(1)}, bf16[192,768]{1,0:T(8,128)(2,1)S(1)}, u32[]{:S(2)}, u32[]{:S(2)}) collective-permute-start(bf16[192,768]{1,0:T(8,128)(2,1)S(1)} %fusion.6), channel_id=1, source_target_pairs={{0,2},{1,3},{2,0},{3,1},{4,6},{5,7},{6,4},{7,5},{8,10},{9,11},{10,... | collective-permute-start | bytes 884744 | tf_op jit(solution)/shard_map/ppermute | solution.py:52
  (81 other events, 905.4 us)

commit v2 on v1

v2 whole, which is shorter than its diff:
```python
import functools
import math

import jax
import jax.numpy as jnp
from jax import lax
from jax.experimental import pallas as pl
from jax.experimental.pallas import tpu as pltpu
from jax.sharding import PartitionSpec as P

EPSILON = 1e-05
NEGATIVE = -1e30
BF = jnp.bfloat16
F32 = jnp.float32
VM = pltpu.VMEM
ANY = pl.ANY
VMEM_LIMIT = 60 * 1024 * 1024
GROUPS = 3


def dot(a, b):
    return lax.dot_general(a, b, (((1,), (0,)), ((), ())), preferred_element_type=F32)


def dot_nt(a, b):
    return lax.dot_general(a, b, (((1,), (1,)), ((), ())), preferred_element_type=F32)


def dot_tn(a, b):
    return lax.dot_general(a, b, (((0,), (0,)), ((), ())), preferred_element_type=F32)


def vmem(shape=None, index=None):
    if shape is None:
        return pl.BlockSpec(memory_space=VM)
    return pl.BlockSpec(shape, index)


def params(n_grid=0):
    return pltpu.CompilerParams(
        vmem_limit_bytes=VMEM_LIMIT,
        dimension_semantics=("arbitrary",) * n_grid if n_grid else None,
    )


def smem():
    return pl.BlockSpec(memory_space=pltpu.SMEM)


def after(value, *marks):
    return lax.optimization_barrier((value, *marks))[0]


def swap_by(value, axis, size, step):
    return lax.ppermute(value, axis, [(i, i ^ step) for i in range(size)])


def swap(value, axis, size, bit):
    return swap_by(value, axis, size, 1 << bit)


def far_steps(far):
    a, b = 1 << far[0], 1 << far[1]
    return (a, b, a | b)


def add(*parts):
    total = parts[0].astype(F32)
    for part in parts[1:]:
        total = total + part.astype(F32)
    return total.astype(BF)


def place(index, order):
    out = 0
    for step, bit in enumerate(order):
        out = out | (((index >> bit) & 1) << step)
    return out


def prep_kernel(scal, tok, docs, wq, wk, wv, wo, wi, wd, *rest):
    vecs, (a0, rest_w, ffq, tok_ref) = rest[:9], rest[9:]
    mc, core = scal[1], scal[2]
    my_y = mc >> 1
    rows, width = wq.shape
    half = a0.shape[1]
    cols = (2 * half) // 3
    cut = half - cols
    low = core == 0
    sub = ffq.shape[1]
    seqs, shard = tok.shape[:2]

    def pick(g):
        at = g * cols
        first = jnp.concatenate([wq[:, at:at + cols], wk[:, at:at + cut]], 1)
        second = jnp.concatenate([wk[:, at + cut:at + cols], wv[:, at:at + cols]], 1)
        return jnp.where(low, first, second)

    a0[:rows] = pick(0)
    a0[rows:] = jnp.zeros_like(a0[rows:])
    table = jnp.zeros((16, half), F32)
    p = 0
    lines = []
    line = []
    for v in vecs:
        step = rows if v.shape[1] == rows else v.shape[1] // 4
        for i in range(v.shape[1] // step):
            line.append(v[:, i * step:(i + 1) * step].astype(F32))
            p += step
            if p % half == 0:
                lines.append(jnp.concatenate(line, 1))
                line = []
    if line:
        line.append(jnp.zeros((1, half - p % half), F32))
        lines.append(jnp.concatenate(line, 1))
    lines.append(jnp.zeros((16 - len(lines), half), F32))
    a0[rows:] = jnp.concatenate(lines, 0).astype(BF)
    del table
    rest_w[:, :half] = pick(1)
    rest_w[:, half:2 * half] = pick(2)
    rest_w[:, 2 * half:] = jnp.where(low, wo[:, :half], wo[:, half:])
    block = 2 * core + my_y
    ffq[1] = wd[pl.ds(pl.multiple_of(block * sub, sub), sub), :]
    for s in range(width // sub):
        got = [wi[:, (4 * s + b) * sub:(4 * s + b + 1) * sub] for b in range(4)]
        near = jnp.where(my_y == 0, got[0], got[1])
        far = jnp.where(my_y == 0, got[2], got[3])
        ffq[0, :, s * sub:(s + 1) * sub] = jnp.where(low, near, far)
    for s in range(seqs):
        tok_ref[s, :shard, :] = tok[s]
        tok_ref[s, shard:, :] = jnp.zeros_like(tok_ref[s, shard:, :])
        tok_ref[s, shard:shard + 1, :shard] = docs[s:s + 1, :].astype(F32).astype(BF)


def join_kernel(a, b, c, d, out):
    lead = out.ndim == 4
    for i, ref in enumerate((a, b, c, d)):
        if lead:
            out[:, i] = ref[...]
        else:
            out[i] = ref[...]


def fetch(lo, hi, at):
    m = lo.shape[0]
    return jnp.where(at < m, lo[at & (m - 1)], hi[at & (m - 1)])


def weights_in(out, order, pm, core, rows, shards, own, got, at_col, half):
    first = core == 0
    for i in range(shards):
        at = place(i, order) ^ pm
        m = own[0].shape[0]
        pick = lambda ref: ref[at & (m - 1), :rows, at_col:at_col + half]
        in_lo = at < m
        mine = jnp.where(in_lo, pick(own[0]), pick(own[1]))
        other = jnp.where(in_lo, pick(got[0]), pick(got[1]))
        out[i * rows:(i + 1) * rows, :half] = jnp.where(first, mine, other)
        out[i * rows:(i + 1) * rows, half:2 * half] = jnp.where(first, other, mine)


def vector_kernel(order, shards, rows, sub, scal, lo, hi, vec_ref, bin_ref):
    pm = scal[0]
    half = lo.shape[2]
    m = lo.shape[0]
    for s in range(shards):
        at = place(s, order) ^ pm
        block = jnp.where(at < m, lo[at & (m - 1), rows:, :], hi[at & (m - 1), rows:, :]).astype(F32)
        for i in range(8):
            p = i * rows
            vec_ref[i:i + 1, s * rows:(s + 1) * rows] = block[p // half:p // half + 1, p % half:p % half + rows]
        for b in range(4):
            p = 8 * rows + b * sub
            c = 2 * (b & 1) + (b >> 1)
            bin_ref[c, :, s * sub:(s + 1) * sub] = block[p // half:p // half + 1, p % half:p % half + sub]


def turn_kernel(scal, t0, t1, t2, t3, out_ref):
    mc = scal[1]
    seqs, _, width = t0.shape
    shard = out_ref.shape[2] // 4
    for j, tok in enumerate((t0, t1, t2, t3)):
        where = pl.multiple_of((mc ^ j) * shard, shard)
        for s in range(seqs):
            out_ref[s, :, pl.ds(where, shard)] = tok[s, :shard, :].T


def attend_kernel(
    order, shards, seq, group, aliased,
    scal, t0, t1, t2, t3, doc_ref, own_lo, own_hi, got_lo, got_hi, bias_ref, prior_ref, *rest,
):
    if aliased:
        rest = rest[1:]
    raw_ref, e_ref, q_ref, k_ref, v_ref, o_ref, inv_ref, w_s, kt_s, mask_s, vx_s = rest
    h = pl.program_id(0)
    pm, mc, core = scal[0], scal[1], scal[2]
    rows = w_s.shape[0] // shards
    half = w_s.shape[1] // 2
    shard, cols = q_ref.shape
    head = cols // 4

    @pl.when(h == 0)
    def _():
        weights_in(w_s, order, pm, core, rows, shards, (own_lo, own_hi), (got_lo, got_hi), 0, half)
        q = dot(t0[0, :shard, :], w_s[:, :cols]) + bias_ref[0:1, :]
        q_ref[...] = (q.astype(BF).astype(F32) * (1.0 / math.sqrt(head))).astype(BF)
        mine = jnp.broadcast_to(doc_ref[seq:seq + 1, :].astype(F32), (128, shard)).T[:, :1]
        for j, tok in enumerate((t0, t1, t2, t3)):
            where = pl.multiple_of((mc ^ j) * shard, shard)
            kv = dot(tok[0, :shard, :], w_s[:, cols:])
            k_ref[pl.ds(where, shard), :] = kv[:, :cols].astype(BF)
            v = kv[:, cols:] + bias_ref[1:2, :]
            v_ref[pl.ds(where, shard), :] = v.astype(BF)
            even = (lax.broadcasted_iota(jnp.int32, (shard, cols), 1) // head) % 2 == 0
            vx_s[0, pl.ds(where, shard), :] = jnp.where(even, v, 1.0).astype(BF)
            vx_s[1, pl.ds(where, shard), :] = jnp.where(even, 1.0, v).astype(BF)
            docs = tok[0, shard:shard + 1, :shard].astype(F32)
            mask_s[:, pl.ds(where, shard)] = jnp.where(mine == docs, 0.0, NEGATIVE)
        kt_s[...] = k_ref[...].T

    lane = lax.broadcasted_iota(jnp.int32, (shard, cols), 1) // head
    this = lane == h
    qm = jnp.where(this, q_ref[...].astype(F32), 0.0).astype(BF)
    step = 64
    for r in range(0, shard, step):
        logits = dot(qm[r:r + step], kt_s[...]) + prior_ref[0, 0, r:r + step, :].astype(F32)
        raw_ref[0, 0, r:r + step, :] = logits.astype(BF)
        masked = logits + mask_s[r:r + step, :]
        top = jnp.max(masked, -1, keepdims=True)
        e_ref[0, r:r + step, :] = jnp.exp(masked - top).astype(BF)
    o = dot(e_ref[0], vx_s[h & 1])
    total = jnp.max(jnp.where(lane == (h ^ 1), o, 0.0), -1, keepdims=True)
    inv = 1.0 / total
    o_ref[...] = jnp.where(this, o * inv, o_ref[...])
    inv_ref[...] = jnp.where(this, inv, inv_ref[...])


def gelu_parts(x):
    z = jnp.abs(x) * 0.7071067811865476
    t = 1.0 / (1.0 + 0.3275911 * z)
    e = jnp.exp(-0.5 * x * x)
    poly = t * (0.254829592 + t * (-0.284496736 + t * (1.421413741 + t * (-1.453152027 + t * 1.061405429))))
    tail = 0.5 * poly * e
    phi = jnp.where(x >= 0, 1.0 - tail, tail)
    return x * phi, phi + x * (e * 0.3989422804014327)


def moments(x):
    mean = jnp.mean(x, -1, keepdims=True)
    centered = x - mean
    inverse = lax.rsqrt(jnp.mean(centered * centered, -1, keepdims=True) + EPSILON)
    return centered * inverse, inverse


def norm_back(grad, normed, inverse, gain):
    scaled = grad * gain
    return inverse * (
        scaled - jnp.mean(scaled, -1, keepdims=True)
        - normed * jnp.mean(scaled * normed, -1, keepdims=True)
    )


def block_copy(lo, hi, at, dst, sem):
    m = lo.shape[0]
    spot = at & (m - 1)

    @pl.when(at < m)
    def _():
        pltpu.make_async_copy(lo.at[spot], dst, sem).start()

    @pl.when(at >= m)
    def _():
        pltpu.make_async_copy(hi.at[spot], dst, sem).start()

    return pltpu.make_async_copy(lo.at[spot], dst, sem)


def ff_sources(f, which):
    lo, hi, ylo, yhi_i, yhi_d, clo, chi, cylo, cyhi_i, cyhi_d = f
    yhi, cyhi = (yhi_i, cyhi_i) if which == 0 else (yhi_d, cyhi_d)
    return [(lo.at[which], hi.at[which]), (clo.at[which], chi.at[which]),
            (ylo.at[which], yhi), (cylo.at[which], cyhi)]


def ff_copies(f, which, dst, order, pm, shards, rows, sem):
    out = []
    for j, (lo, hi) in enumerate(ff_sources(f, which)):
        out.append([block_copy(lo, hi, place(s, order) ^ pm, dst.at[j, pl.ds(s * rows, rows)], sem.at[j * shards + s])
                    for s in range(shards)])
    return out


def forward_kernel(
    order, shards,
    scal, o00, o01, o10, o11, o20, o21, tok_ref, cot_ref, vec_ref, bin_ref, wl, wh, wgl, wgh, *rest,
):
    f, rest = rest[:10], rest[10:]
    (out_ref, mix_ref, first_n_ref, inv1_ref, inner_ref, hid_ref, dg_ref, dsum2_ref, dsec_ref, vg_ref,
     wo_s, wi_s, wd_s, first_s, acc_s, isem, dsem) = rest
    pm, mc, core = scal[0], scal[1], scal[2]
    seqs, shard, width = tok_ref.shape
    rows = width // shards
    n_rows = seqs * shard
    in_copies = ff_copies(f, 0, wi_s, order, pm, shards, rows, isem)
    down_copies = ff_copies(f, 1, wd_s, order, pm, shards, rows, dsem)
    weights_in(wo_s, order, pm, core, rows, shards, (wl, wh), (wgl, wgh), 0, width // 2)
    mixed = jnp.concatenate(
        [jnp.concatenate([a[...].astype(BF), b[...].astype(BF)], 0) for a, b in ((o00, o01), (o10, o11), (o20, o21))], 1)
    mix_ref[...] = mixed
    tokens = tok_ref[...].reshape(n_rows, width).astype(F32)
    normed, inverse = moments(tokens + (dot(mixed, wo_s[...]) + vec_ref[2:3, :]))
    first_n_ref[...] = normed
    inv1_ref[...] = inverse
    first = normed * vec_ref[3:4, :] + vec_ref[4:5, :]
    first_s[...] = first
    inner_ref[...] = first.astype(BF)
    for j in range(4):
        for c in in_copies[j]:
            c.wait()
        for r in range(0, n_rows, 128):
            pre = dot(inner_ref[r:r + 128, :], wi_s[j]) + bin_ref[mc ^ j]
            hid, dg = gelu_parts(pre)
            hid_ref[j, r:r + 128, :] = hid.astype(BF)
            dg_ref[j, r:r + 128, :] = dg.astype(BF)
        for c in down_copies[j]:
            c.wait()
        part = dot(hid_ref[j], wd_s[j])
        acc_s[...] = part if j == 0 else acc_s[...] + part
    normed, inverse = moments(first_s[...] + (acc_s[...] + vec_ref[5:6, :]))
    gain = vec_ref[6:7, :]
    out_ref[...] = (normed * gain + vec_ref[7:8, :]).astype(BF).reshape(seqs, shard, width)
    dy = cot_ref[...].reshape(n_rows, width).astype(F32)
    dsum2 = norm_back(dy, normed, inverse, gain)
    dsum2_ref[...] = dsum2
    dsec = dsum2.astype(BF)
    dsec_ref[...] = dsec
    vg_ref[0:1, :] = jnp.sum(dy * normed, 0, keepdims=True)
    vg_ref[1:2, :] = jnp.sum(dy, 0, keepdims=True)
    vg_ref[2:3, :] = jnp.sum(dsec.astype(F32), 0, keepdims=True)


def down_grad_kernel(order, shards, scal, hid, dsec, keep, send):
    pm = scal[0]
    sub = keep.shape[2]
    for j in (1, 3, 0, 2):
        out = keep if j % 2 == 0 else send
        grad = dot_tn(hid[j], dsec[...]).astype(BF)
        for s in range(shards):
            out[j >> 1, place(s, order) ^ pm] = grad[s * sub:(s + 1) * sub]


def in_grad_kernel(order, shards, scal, inner, dg, dsec, *rest):
    f, (keep, send, dpre_ref, gbin_ref, wd_s, sem) = rest[:10], rest[10:]
    pm, mc = scal[0], scal[1]
    rows = keep.shape[2]
    down_copies = ff_copies(f, 1, wd_s, order, pm, shards, rows, sem)
    for j in (1, 3, 0, 2):
        out = keep if j % 2 == 0 else send
        for c in down_copies[j]:
            c.wait()
        dpre = (dot_nt(dsec[...], wd_s[j]) * dg[j].astype(F32)).astype(BF)
        dpre_ref[j] = dpre
        gbin_ref[mc ^ j] = jnp.sum(dpre.astype(F32), 0, keepdims=True)
        grad = dot_tn(inner[...], dpre).astype(BF)
        for s in range(shards):
            out[j >> 1, place(s, order) ^ pm] = grad[s * rows:(s + 1) * rows]


def first_grad_kernel(
    order, shards, scal, mix_ref, first_n, inv1, dpre, dsum2, vec_ref, wl, wh, wgl, wgh, *rest,
):
    f, (go_keep, go_send, dsum1_ref, dmix_ref, vg_ref, wo_s, wi_s, sem) = rest[:10], rest[10:]
    pm, core = scal[0], scal[2]
    n_rows, width = dsum2.shape
    rows = width // shards
    half = width // 2
    in_copies = ff_copies(f, 0, wi_s, order, pm, shards, rows, sem)
    weights_in(wo_s, order, pm, core, rows, shards, (wl, wh), (wgl, wgh), 0, half)
    dfirst = dsum2[...]
    for j in range(4):
        for c in in_copies[j]:
            c.wait()
        dfirst = dfirst + dot_nt(dpre[j], wi_s[j])
    normed = first_n[...]
    dsum1 = norm_back(dfirst, normed, inv1[...], vec_ref[3:4, :])
    dsum1_ref[...] = dsum1
    dbranch = dsum1.astype(BF)
    vg_ref[0:1, :] = jnp.sum(dfirst * normed, 0, keepdims=True)
    vg_ref[1:2, :] = jnp.sum(dfirst, 0, keepdims=True)
    vg_ref[2:3, :] = jnp.sum(dbranch.astype(F32), 0, keepdims=True)
    dmix_ref[...] = dot_nt(dbranch, wo_s[...]).astype(BF)
    grad_o = dot_tn(mix_ref[...], dbranch).astype(BF)
    first_core = core == 0
    for s in range(shards):
        block = grad_o[s * rows:(s + 1) * rows]
        at = place(s, order) ^ pm
        go_keep[at] = jnp.where(first_core, block[:, :half], block[:, half:])
        go_send[at] = jnp.where(first_core, block[:, half:], block[:, :half])


def attend_back_kernel(
    aliased,
    scal, e_ref, dm_ref, q_ref, k_ref, v_ref, o_ref, inv_ref, *rest,
):
    if aliased:
        rest = rest[1:]
    gp_ref, dq_ref, dkv_ref, vt_s, qt_s, dmt_s, dmi_s, dl_s, dkt_s, dvt_s, dq_s = rest
    h = pl.program_id(0)
    shard, cols = q_ref.shape
    head = cols // 4

    @pl.when(h == 0)
    def _():
        vt_s[...] = v_ref[...].T
        dmi = (dm_ref[...].astype(F32) * inv_ref[...]).astype(BF)
        dmi_s[...] = dmi
        dl_s[...] = dmi.astype(F32) * o_ref[...]
        qt_s[...] = q_ref[...].T
        dmt_s[...] = dmi.T

    lane = lax.broadcasted_iota(jnp.int32, (shard, cols), 1) // head
    this = lane == h
    dmm = jnp.where(this, dmi_s[...].astype(F32), 0.0).astype(BF)
    delta = jnp.sum(jnp.where(this, dl_s[...], 0.0), -1, keepdims=True)
    step = 64
    for r in range(0, shard, step):
        dp = dot(dmm[r:r + step], vt_s[...])
        gp_ref[0, 0, r:r + step, :] = (
            e_ref[0, r:r + step, :].astype(F32) * (dp - delta[r:r + step])
        ).astype(BF)
    g = gp_ref[0, 0]
    dq = dot(g, k_ref[...]) * (1.0 / math.sqrt(head))
    dq_s[...] = jnp.where(this, dq, dq_s[...])
    at = pl.multiple_of(h * head, head)
    dkt_s[pl.ds(at, head), :] = dot(qt_s[pl.ds(at, head), :], g).astype(BF)
    dvt_s[pl.ds(at, head), :] = dot(dmt_s[pl.ds(at, head), :], e_ref[0]).astype(BF)

    @pl.when(h == 3)
    def _():
        dq_ref[...] = dq_s[...].astype(BF)
        dkv_ref[:, :cols] = dkt_s[...].T
        dkv_ref[:, cols:] = dvt_s[...].T


def table_rows(s, sums, gbin, rows, sub, half):
    pieces = [v[:, s * rows:(s + 1) * rows] for v in sums]
    for b in range(4):
        pieces.append(gbin[2 * (b & 1) + (b >> 1), :, s * sub:(s + 1) * sub])
    lines, line, p = [], [], 0
    for piece in pieces:
        line.append(piece)
        p += piece.shape[1]
        if p % half == 0:
            lines.append(jnp.concatenate(line, 1))
            line = []
    if line:
        line.append(jnp.zeros((1, half - p % half), F32))
        lines.append(jnp.concatenate(line, 1))
    lines.append(jnp.zeros((8 - len(lines), half), F32))
    value = jnp.concatenate(lines, 0)
    high = value.astype(BF)
    return jnp.concatenate([high.astype(F32), value - high.astype(F32)], 0).astype(BF)


def weight_grad_kernel(order, shards, kind, sub, scal, xt_ref, dq0, dq1, dkv0, dkv1, *rest):
    pm, mc, core = scal[0], scal[1], scal[2]
    shard, cols = dq0.shape
    length = dkv0.shape[0]
    extra, (g_keep, g_send, vg_ref) = rest[:-3], rest[-3:]
    mine = pl.multiple_of(mc * shard, shard)
    ones = jnp.ones((8, length), BF)
    grad_kv = dot(xt_ref[0], dkv0[...]) + dot(xt_ref[1], dkv1[...])
    grad_q = dot(xt_ref[0, :, pl.ds(mine, shard)], dq0[...]) + dot(xt_ref[1, :, pl.ds(mine, shard)], dq1[...])
    vg_ref[1:2, :] = (dot(ones, dkv0[:, cols:]) + dot(ones, dkv1[:, cols:]))[0:1]
    vg_ref[0:1, :] = (dot(ones[:, :shard], dq0[...]) + dot(ones[:, :shard], dq1[...]))[0:1]
    grad = jnp.concatenate([grad_q.astype(BF), grad_kv.astype(BF)], 1)
    rows = grad.shape[0] // shards
    half = grad.shape[1] // 2
    first_core = core == 0
    if kind == 2:
        vg0, vg1, ff1, ff2, gbin = extra
        sums = [
            jnp.concatenate([vg0[i:i + 1, :], vg1[i:i + 1, :], vg_ref[i:i + 1, :]], 1) for i in range(2)
        ] + [ff1[2:3, :], ff1[0:1, :], ff1[1:2, :], ff2[2:3, :], ff2[0:1, :], ff2[1:2, :]]
    for i in range(shards):
        block = grad[i * rows:(i + 1) * rows]
        to = place(i, order) ^ pm
        g_keep[to, :rows, :half] = jnp.where(first_core, block[:, :half], block[:, half:])
        g_send[to, :rows, :half] = jnp.where(first_core, block[:, half:], block[:, :half])
        if kind == 0:
            go_keep, go_send = extra
            g_keep[to, :, half:] = go_keep[to]
            g_send[to, :, half:] = go_send[to]
        if kind == 2:
            table = table_rows(i, sums, gbin, rows, sub, half)
            g_keep[to, rows:, :] = table
            g_send[to, rows:, :] = table


def sum_kernel(rows, *refs):
    parts, out = refs[:-1], refs[-1]
    for i in range(out.shape[0]):
        total = parts[0][i].astype(F32)
        for part in parts[1:]:
            total = total + part[i].astype(F32)
        out[i, :rows] = total[:rows].astype(BF)
        value = total[rows:rows + 8] + total[rows + 8:]
        high = value.astype(BF).astype(F32)
        out[i, rows:] = jnp.concatenate([high, value - high], 0).astype(BF)


def token_kernel(
    order, shards,
    scal, dq00, dq01, dq10, dq11, dq20, dq21, dkv00, dkv01, dkv10, dkv11, dkv20, dkv21,
    a_lo, a_hi, ag_lo, ag_hi, b_lo, b_hi, bg_lo, bg_hi, dsum1,
    p0, p1, p2, p3, w_s,
):
    pm, mc, core = scal[0], scal[1], scal[2]
    rows = w_s.shape[1] // shards
    half = w_s.shape[2] // 2
    shard, cols = dq00.shape
    weights_in(w_s.at[0], order, pm, core, rows, shards, (a_lo, a_hi), (ag_lo, ag_hi), 0, half)
    weights_in(w_s.at[1], order, pm, core, rows, shards, (b_lo, b_hi), (bg_lo, bg_hi), 0, half)
    weights_in(w_s.at[2], order, pm, core, rows, shards, (b_lo, b_hi), (bg_lo, bg_hi), half, half)
    dqs = ((dq00, dq10, dq20), (dq01, dq11, dq21))
    dkvs = ((dkv00, dkv10, dkv20), (dkv01, dkv11, dkv21))
    for j, out in reversed(list(enumerate((p0, p1, p2, p3)))):
        where = pl.multiple_of((mc ^ j) * shard, shard)
        for s in range(2):
            total = None
            for g in range(3):
                part = dot_nt(dkvs[s][g][pl.ds(where, shard), :], w_s[g, :, cols:])
                if j == 0:
                    part = part + dot_nt(dqs[s][g][...], w_s[g, :, :cols])
                total = part if total is None else total + part
            if j == 0:
                total = total + dsum1[s * shard:(s + 1) * shard, :]
            out[s] = total.astype(out.dtype)


def finish_kernel(rows, sub, shards, scal, g0, g0c, g1, g1c, g2, g2c, ff, ffc, wq, wk, wv, wo, wi, wd, tab):
    mc, core = scal[1], scal[2]
    low = core == 0
    my_y = mc >> 1
    half = g1.shape[1]
    cols = wq.shape[1] // 3
    cut = half - cols

    def both(mine, other):
        mine, other = mine.astype(F32), other.astype(F32)
        return jnp.where(low, mine, other), jnp.where(low, other, mine)

    groups = [both(g0[:, :half], g0c[:, :half]), both(g1[...], g1c[...]), both(g2[:rows], g2c[:rows])]
    for g, (first, second) in enumerate(groups):
        at = g * cols
        wq[:, at:at + cols] = first[:, :cols]
        wk[:, at:at + cut] = first[:, cols:]
        wk[:, at + cut:at + cols] = second[:, :cols - cut]
        wv[:, at:at + cols] = second[:, cols - cut:]
    first, second = both(g0[:, half:], g0c[:, half:])
    wo[:, :half] = first
    wo[:, half:] = second
    tab[...] = g2[rows:rows + 8, :].astype(F32) + g2[rows + 8:, :].astype(F32)
    quads = []
    for i in range(2):
        a0, a1 = both(ff[0, i], ffc[0, i])
        b0, b1 = both(ff[1, i], ffc[1, i])
        near = my_y == 0
        quads.append([jnp.where(near, a0, b0), jnp.where(near, b0, a0), jnp.where(near, a1, b1), jnp.where(near, b1, a1)])
    for b in range(4):
        wd[b * sub:(b + 1) * sub, :] = quads[1][b]
        for s in range(shards):
            at = (4 * s + b) * sub
            wi[:, at:at + sub] = quads[0][b][:, s * sub:(s + 1) * sub]


def on_device(
    n, far, near,
    tokens, prior_logits, doc_ids, w_query, w_key, w_value, w_out, b_query, b_value, b_out,
    first_norm_gain, norm1_shift, w_in, b_in, w_down, b_down, norm2_gain, norm2_shift, cotangent,
):
    seqs, shard, width = tokens.shape
    heads, length = prior_logits.shape[1], prior_logits.shape[3]
    ctx = length // shard
    rows = w_query.shape[0]
    sub = w_down.shape[0] // 4
    cols = width // GROUPS
    per = heads // GROUPS
    half = (3 * cols) // 2
    n_rows = seqs * shard
    m = n // 2
    order = far + near
    me_s = lax.axis_index("seq")
    me_c = lax.axis_index("ctx")
    core = me_c & 1
    pm = place(me_s, order)
    scal = jnp.stack([pm, me_c, core]).astype(jnp.int32)
    sds = jax.ShapeDtypeStruct
    hbm = pl.BlockSpec(memory_space=ANY)

    def kernel(body, outs, ins, args, scratch=(), grid=None, alias=None, flops=0, moved=0, exps=0, name=None):
        return pl.pallas_call(
            body,
            out_shape=outs,
            in_specs=ins[0],
            out_specs=ins[1],
            scratch_shapes=scratch,
            input_output_aliases=alias or {},
            compiler_params=params(len(grid) if grid else 0),
            cost_estimate=pl.CostEstimate(flops=flops, bytes_accessed=moved, transcendentals=exps),
            name=name,
            **({"grid": grid} if grid else {}),
        )(*args)

    def by_core(value):
        return swap(value, "ctx", ctx, 0)

    def by_y(value):
        return swap(value, "ctx", ctx, 1)

    def by_x(value):
        return swap(value, "seq", n, near[-1])

    def whole(*shape):
        return pl.BlockSpec(shape, lambda *i: (0,) * len(shape))

    vectors = [b_query, b_value, b_out, first_norm_gain, norm1_shift, b_down, norm2_gain, norm2_shift, b_in]
    a0, b0, ffq, tok0 = kernel(
        prep_kernel,
        [sds((rows + 16, half), BF), sds((rows, 3 * half), BF), sds((2, rows, width), BF),
         sds((seqs, shard + 16, width), BF)],
        ([smem()] + [vmem()] * 17, [vmem()] * 4),
        (scal, tokens, doc_ids, w_query, w_key, w_value, w_out, w_in, w_down, *[v.reshape(1, -1) for v in vectors]),
        moved=6 * 10**6, name="prep",
    )

    def spread(held, name):
        parts = [held] + [swap_by(held, "seq", n, step) for step in far_steps(far)]
        lead = held.ndim == 3
        shape = (2, 4, *held.shape[1:]) if lead else (4, *held.shape)
        out, = kernel(join_kernel, [sds(shape, BF)], ([vmem()] * 4, [vmem()]), parts, moved=10**6, name=name)
        for bit in near[:-1]:
            out = jnp.concatenate([out, swap(out, "seq", n, bit)], 1 if lead else 0)
        return out

    a_lo = spread(a0, "join_a")
    tok2 = by_y(tok0)
    tok1 = by_core(tok0)
    ag_lo = by_core(a_lo)
    a_hi = by_x(a_lo)
    b_lo = spread(after(b0, a_lo), "join_b")
    ag_hi = by_core(a_hi)
    tok3 = by_core(tok2)
    tok = (tok0, tok1, tok2, tok3)
    b_hi = by_x(b_lo)
    bg_lo = by_core(b_lo)
    f_lo = spread(after(ffq, b_lo), "join_f")
    vecs, bin_all = kernel(
        functools.partial(vector_kernel, order, n, rows, sub),
        [sds((8, width), F32), sds((4, 1, width), F32)],
        ([smem()] + [vmem()] * 2, [vmem()] * 2), (scal, a_lo, a_hi), moved=10**6, name="vectors",
    )

    raw = None
    kept = []

    def attend(g, s, scal, arrays):
        nonlocal raw
        big = pl.BlockSpec((1, 1, shard, length), lambda h: (s, g * per + h, 0, 0))
        tok_spec = pl.BlockSpec((1, shard + 16, width), lambda h: (s, 0, 0))
        block = max(g - 1, 0)
        w_spec = pl.BlockSpec((m, arrays[0].shape[1], half), lambda h: (0, 0, block))
        args = [scal, *tok, doc_ids, *arrays, vecs, prior_logits]
        specs = [smem()] + [tok_spec] * 4 + [vmem()] + [w_spec] * 4 + [pl.BlockSpec((8, cols), lambda h: (0, g)), big]
        alias = {}
        if raw is not None:
            alias = {len(args): 0}
            args.append(raw)
            specs.append(hbm)
        raw, *rest = kernel(
            functools.partial(attend_kernel, order, n, s, g, raw is not None),
            [sds(prior_logits.shape, BF), sds((per, shard, length), BF), sds((shard, cols), BF),
             sds((length, cols), BF), sds((length, cols), BF), sds((shard, cols), F32), sds((shard, cols), F32)],
            (specs, [big, pl.BlockSpec((1, shard, length), lambda h: (h, 0, 0)), whole(shard, cols), whole(length, cols),
                     whole(length, cols), whole(shard, cols), whole(shard, cols)]),
            args, [VM((width, 3 * cols), BF), VM((cols, length), BF), VM((shard, length), F32), VM((2, length, cols), BF)],
            grid=(per,), alias=alias, flops=5 * 10**9, moved=10 * 10**6, exps=10**6, name=f"attend{g}{s}",
        )
        kept.append(rest)
        return rest[2]

    a_set = (a_lo, a_hi, ag_lo, ag_hi)
    mark = attend(0, 0, after(scal, b_lo), a_set)
    bg_hi = by_core(b_hi)
    b_set = (b_lo, b_hi, bg_lo, bg_hi)
    attend(0, 1, after(scal, f_lo), a_set)
    f_hi, f_ylo = by_x(f_lo), by_y(f_lo)
    fc_lo = by_core(f_lo)
    attend(1, 0, scal, b_set)
    x_t, = kernel(turn_kernel, [sds((seqs, width, length), BF)], ([smem()] + [vmem()] * 4, [vmem()]),
                  (scal, *tok), moved=12 * 10**6, name="turn")
    attend(1, 1, after(scal, kept[-1][4], f_hi, f_ylo), b_set)
    f_yhi_i, f_yhi_d = by_y(f_hi[0]), by_x(f_ylo[1])
    fc_hi, fc_ylo = by_core(f_hi), by_core(f_ylo)
    attend(2, 0, after(scal, x_t), b_set)
    attend(2, 1, after(scal, f_yhi_i, f_yhi_d), b_set)
    fc_yhi_i, fc_yhi_d = by_core(f_yhi_i), by_core(f_yhi_d)
    f = (f_lo, f_hi, f_ylo, f_yhi_i, f_yhi_d, fc_lo, fc_hi, fc_ylo, fc_yhi_i, fc_yhi_d)

    o_spec = pl.BlockSpec((m, rows, half), lambda i: (0, 0, 2))
    w_scratch = VM((4, width, width), BF)
    sems = pltpu.SemaphoreType.DMA((4 * n,))
    output, mixed, first_n, inv1, inner, hid, dg, dsum2, dsec, ff2 = kernel(
        functools.partial(forward_kernel, order, n),
        [
            sds((seqs, shard, width), BF), sds((n_rows, width), BF), sds((n_rows, width), F32), sds((n_rows, 1), F32),
            sds((n_rows, width), BF), sds((4, n_rows, width), BF), sds((4, n_rows, width), BF),
            sds((n_rows, width), F32), sds((n_rows, width), BF), sds((8, width), F32),
        ],
        ([smem()] + [vmem()] * 10 + [o_spec] * 4 + [hbm] * 10, [vmem()] * 10),
        (scal, *[k[4] for k in kept], tokens, cotangent, vecs, bin_all, *b_set, *f),
        [VM((width, width), BF), w_scratch, w_scratch, VM((n_rows, width), F32), VM((n_rows, width), F32), sems, sems],
        grid=(1,), flops=6 * 10**9, moved=25 * 10**6, exps=2 * 10**6, name="ff_fwd",
    )
    pair = [sds((2, n, rows, width), BF)] * 2
    d_keep, d_send = kernel(
        functools.partial(down_grad_kernel, order, n), pair,
        ([smem()] + [vmem()] * 2, [vmem()] * 2), (scal, hid, dsec), flops=3 * 10**9, moved=8 * 10**6, name="down_grad",
    )
    d_got = by_core(d_send)
    i_keep, i_send, dpre, gbin = kernel(
        functools.partial(in_grad_kernel, order, n),
        pair + [sds((4, n_rows, width), BF), sds((4, 1, width), F32)],
        ([smem()] + [vmem()] * 3 + [hbm] * 10, [vmem()] * 4),
        (after(scal, d_keep), inner, dg, dsec, *f), [w_scratch, sems], flops=6 * 10**9, moved=20 * 10**6, name="in_grad",
    )
    i_got = by_core(i_send)
    go_keep, go_send, dsum1, dmix, ff1 = kernel(
        functools.partial(first_grad_kernel, order, n),
        [sds((n, rows, half), BF)] * 2 + [sds((n_rows, width), F32), sds((n_rows, width), BF), sds((8, width), F32)],
        ([smem()] + [vmem()] * 6 + [o_spec] * 4 + [hbm] * 10, [vmem()] * 5),
        (scal, mixed, first_n, inv1, dpre, dsum2, vecs, *b_set, *f), [VM((width, width), BF), w_scratch, sems],
        grid=(1,), flops=4 * 10**9, moved=15 * 10**6, name="first_grad",
    )

    gp = None
    dqs, dkvs, vgs = [], [], []

    def back(g, s, scal):
        nonlocal gp
        e, q, k, v, o, inv = kept[g * seqs + s]
        big = pl.BlockSpec((1, 1, shard, length), lambda h: (s, g * per + h, 0, 0))
        args = [scal, e, dmix, q, k, v, o, inv]
        specs = [smem(), pl.BlockSpec((1, shard, length), lambda h: (h, 0, 0)),
                 pl.BlockSpec((shard, cols), lambda h: (s, g)),
                 whole(shard, cols), whole(length, cols), whole(length, cols), whole(shard, cols), whole(shard, cols)]
        alias = {}
        if gp is not None:
            alias = {len(args): 0}
            args.append(gp)
            specs.append(hbm)
        gp, dq, dkv = kernel(
            functools.partial(attend_back_kernel, gp is not None),
            [sds(prior_logits.shape, BF), sds((shard, cols), BF), sds((length, 2 * cols), BF)],
            (specs, [big, whole(shard, cols), whole(length, 2 * cols)]),
            args,
            [VM((cols, length), BF), VM((cols, shard), BF), VM((cols, shard), BF), VM((shard, cols), BF),
             VM((shard, cols), F32), VM((cols, length), BF), VM((cols, length), BF), VM((shard, cols), F32)],
            grid=(per,), alias=alias, flops=5 * 10**9, moved=10 * 10**6, name=f"back{g}{s}",
        )
        dqs.append(dq)
        dkvs.append(dkv)
        return dq

    def weight_grad(g, scal):
        extra = ([go_keep, go_send], [], vgs + [ff1, ff2, gbin])[g]
        shape = ((n, rows, 2 * half), (n, rows, half), (n, rows + 16, half))[g]
        keep, send, vg = kernel(
            functools.partial(weight_grad_kernel, order, n, g, sub),
            [sds(shape, BF)] * 2 + [sds((8, cols), F32)],
            ([smem()] + [vmem()] * (5 + len(extra)), [vmem()] * 3),
            (scal, x_t, *dqs[-2:], *dkvs[-2:], *extra),
            flops=2 * 10**9, moved=8 * 10**6, name=f"weight_grad{g}",
        )
        vgs.append(vg)
        return keep, send, vg

    def rest_near(held, axis, plus):
        for bit in reversed(near[:-1]):
            k = held.shape[axis] // 2
            keep = lax.slice_in_dim(held, 0, k, axis=axis)
            held = plus(keep, swap(lax.slice_in_dim(held, k, 2 * k, axis=axis), "seq", n, bit))
        return held

    def far_sum(blocks, plus):
        got = [swap_by(b, "seq", n, step) for b, step in zip(blocks[1:], far_steps(far))]
        return plus(blocks[0], *got)

    q_i = by_y(add(i_keep[1, m:], i_got[1, m:]))
    q_d = by_x(add(d_keep[1, m:], d_got[1, m:]))
    back(0, 0, scal)
    mark = back(0, 1, scal)
    hi = jnp.stack([add(i_keep[0, m:], i_got[0, m:], q_i), add(d_keep[0, m:], d_got[0, m:])])
    ylo = jnp.stack([add(i_keep[1, :m], i_got[1, :m]), add(d_keep[1, :m], d_got[1, :m], q_d)])
    x_got, y_got = by_x(hi), by_y(ylo)
    keep, send, vg = weight_grad(0, after(scal, hi, ylo))
    g0_got = by_core(send)
    mark = back(1, 0, after(scal, vg))
    g0_keep = keep
    mark = back(1, 1, after(scal, g0_got))
    lo = jnp.stack([add(i_keep[0, :m], i_got[0, :m], x_got[0], y_got[0]), add(d_keep[0, :m], d_got[0, :m], x_got[1], y_got[1])], 1)
    lo = rest_near(lo, 0, add)
    g0_x = by_x(after(add(g0_keep[m:], g0_got[m:]), mark))
    ff = far_sum([lo[i] for i in range(4)], add)
    g1_keep, g1_send, vg = weight_grad(1, after(scal, lo))
    g1_got = by_core(g1_send)
    mark = back(2, 0, after(scal, vg))
    g0 = rest_near(add(g0_keep[:m], g0_got[:m], g0_x), 0, add)
    g1_x = by_x(add(g1_keep[m:], g1_got[m:]))
    mark = back(2, 1, after(scal, g0))
    g0 = far_sum([g0[i] for i in range(4)], add)
    ff_y = by_y(ff)
    g2_keep, g2_send, _ = weight_grad(2, after(scal, ff))
    g2_got = by_core(g2_send)
    g1 = rest_near(add(g1_keep[:m], g1_got[:m], g1_x), 0, add)

    def plus_table(*parts):
        flat = parts[0].ndim == 2
        parts = [p[None] if flat else p for p in parts]
        out, = kernel(functools.partial(sum_kernel, rows), [sds(parts[0].shape, BF)],
                      ([vmem()] * len(parts), [vmem()]), parts, moved=10**6, name="sum_table")
        return out[0] if flat else out

    g2_x = by_x(plus_table(g2_keep[m:], g2_got[m:]))
    g1 = far_sum([g1[i] for i in range(4)], add)
    pieces = kernel(
        functools.partial(token_kernel, order, n),
        [sds((seqs, shard, width), F32)] + [sds((seqs, shard, width), BF)] * 3,
        ([smem()] + [vmem()] * 12 + [whole(m, a.shape[1], half) for a in a_set]
         + [whole(m, rows, 2 * half)] * 4 + [vmem()], [vmem()] * 4),
        (after(scal, g2_got), *dqs, *dkvs, *a_set, *b_set, dsum1),
        [VM((GROUPS, width, 3 * cols), BF)], grid=(1,), flops=10 * 10**9, moved=15 * 10**6, name="token_grad",
    )
    from_core = (by_core(pieces[1]), by_core(pieces[3]))
    across = by_y(add(pieces[2], from_core[1]))
    g2 = rest_near(plus_table(g2_keep[:m], g2_got[:m], g2_x), 0, plus_table)
    g2 = far_sum([g2[i] for i in range(4)], plus_table)
    g0 = add(g0, by_y(g0))
    g1 = add(g1, by_y(g1))
    g2 = plus_table(g2, by_y(g2))
    ff = jnp.stack([ff, ff_y])
    grad_tokens = pieces[0] + from_core[0].astype(F32) + across.astype(F32)
    g_wq, g_wk, g_wv, g_wo, g_wi, g_wd, table = kernel(
        functools.partial(finish_kernel, rows, sub, n),
        [sds(w.shape, F32) for w in (w_query, w_key, w_value, w_out, w_in, w_down)] + [sds((8, half), F32)],
        ([smem()] + [vmem()] * 8, [vmem()] * 7),
        (scal, g0, by_core(g0), g1, by_core(g1), g2, by_core(g2), ff, by_core(ff)),
        moved=6 * 10**6, name="finish",
    )
    table = table.reshape(-1)
    cut = [table[i * rows:(i + 1) * rows] for i in range(8)]
    g_bq, g_bv, g_bo, g_g1, g_s1, g_bd, g_g2, g_s2 = cut
    g_bin = table[8 * rows:8 * rows + 4 * sub]
    return (
        output, raw, grad_tokens, gp, g_wq, g_wk, g_wv, g_wo,
        g_bq, g_bv, g_bo, g_g1, g_s1, g_wi, g_bin, g_wd, g_bd, g_g2, g_s2,
    )


def solution(mesh):
    n = mesh.shape["seq"]
    top = n.bit_length() - 1
    far, near = (top - 2, top - 1), tuple(reversed(range(top - 2)))
    in_specs = (
        P("seq", "ctx", None), P("seq", None, "ctx", None), P("seq", "ctx"),
        P("seq", None), P("seq", None), P("seq", None), P("seq", None),
        P("seq"), P("seq"), P("seq"), P("seq"), P("seq"),
        P("seq", None), P("seq"), P("seq", None), P("seq"), P("seq"), P("seq"),
        P("seq", "ctx", None),
    )
    out_specs = (
        P("seq", "ctx", None), P("seq", None, "ctx", None), P("seq", "ctx", None), P("seq", None, "ctx", None),
        P("seq", None), P("seq", None), P("seq", None), P("seq", None),
        P("seq"), P("seq"), P("seq"), P("seq"), P("seq"),
        P("seq", None), P("seq"), P("seq", None), P("seq"), P("seq"), P("seq"),
    )
    return jax.shard_map(
        functools.partial(on_device, n, far, near),
        mesh=mesh, in_specs=in_specs, out_specs=out_specs, check_vma=False,
    )
```

time: 546 us -> 395 us (0.72)
  waiting for transfers between devices: 220 us -> 75.6 us
  Pallas kernels: 156 us -> 205 us
  local copies, waits for them, and re-layouts: 51.8 us -> 21.9 us
  other arithmetic: 37.4 us -> 21.7 us
    ppermute x76 -> x62, waiting for transfers between devices: 220 us -> 75.6 us  [swap_by(): return lax.ppermute(value, axis, [(i, i ^ step) for i in range(size)])]
    pallas_call x10 -> x31, Pallas kernels: 156 us -> 205 us  [kernel(): pl.pallas_call(body, out_shape=outs, in_specs=ins[0], out_specs=ins[1], s...]
    concatenate x24 -> x0, other arithmetic: 18.2 us -> none  [the longest x19 16 us: gather_seq(): held = jnp.concatenate([held, swap(held, 'seq', size, bit)], 0)]
    slice x38 -> x3, local copies, waits for them, and re-layouts: 14.3 us -> 4.3 us  [the longest x2 3 us: on_device(): g2_x = by_x(plus_table(g2_keep[m:], g2_got[m:]))]
    concatenate x3 -> x0, local copies, waits for them, and re-layouts: 7.14 us -> none  [the longest x1 6.2 us: on_device(): jnp.concatenate([b_query, b_value, b_out, first_norm_gain, norm1_shift, b...]
    unnamed x109 -> x74, local copies, waits for them, and re-layouts: 4.55 us -> 10.3 us
    convert_element_type x33 -> x12, other arithmetic: 6.15 us -> 11.7 us  [add(): return total.astype(BF)]
    reshape x11 -> x2, local copies, waits for them, and re-layouts: 7.5 us -> 1.95 us  [the longest x1 1.24 us: on_device(): v.reshape(1, -1)]
  transfers between devices with their start and end apart: 76 -> 62, of which waited for: 37 -> 19; matrix products, arithmetic and copies ran while one was open for 14% -> 8% of each run, Pallas kernels for 12% -> 42%
where the time goes in v2:
time: 395 us; the launch traced here: 391 us
  Pallas kernels  205 us (52%)
  waiting for transfers between devices  75.6 us (19%)
  starting transfers between devices  65.3 us (17%)
  local copies, waits for them, and re-layouts  21.9 us (6%)
  other arithmetic  21.7 us (5%)
    pallas_call x31, Pallas kernels, kernel(): pl.pallas_call(body, out_shape=outs, in_specs=ins[0], out_specs=ins[1], s...  205 us
    ppermute x62, waiting for transfers between devices, swap_by(): return lax.ppermute(value, axis, [(i, i ^ step) for i in range(size)])  75.6 us
    ppermute x62, starting transfers between devices, swap_by(): return lax.ppermute(value, axis, [(i, i ^ step) for i in range(size)])  65.3 us
    convert_element_type x12, other arithmetic, add(): return total.astype(BF)  11.7 us
    unnamed x74, local copies, waits for them, and re-layouts  10.3 us
  transfers between devices with their start and end apart: 62, of which 19 were waited for; matrix products, arithmetic and copies ran while one was open for 8% of the time, Pallas kernels for 42%

profile of v2, /device:TPU:0, one launch (start us, length us, event | category | flops | bytes accessed | tf_op | source)
XLA Modules:
  0.0 390.6 jit_solution(3743849748799674465)
XLA Ops:
  2.5 3.8 prep.1
  6.3 3.0 collective-permute-start.7
  9.2 3.6 collective-permute-start.2
  13.6 3.1 collective-permute-done.2.d
  16.7 3.3 collective-permute-done.1.c
  23.1 2.6 collective-permute-start.5
  27.4 6.1 %collective-permute-done.5.d = bf16[96,1152]{1,0:T(8,128)(2,1)S(1)} collective-permute-done((bf16[96,1152]{1,0:T(8,128)(2,1)}, bf16[96,1152]{1,0:T(8,128)(2,1)S(1)}, u32[]{:S(2)}, u32[]{:S(2)}) %collective-permute-start.5) | collective-permute-done | bytes 221216 | tf_op jit(solution)/shard_map/ppermute | solution.py:55
  35.0 8.1 %collective-permute-done.4.c = bf16[96,1152]{1,0:T(8,128)(2,1)S(1)} collective-permute-done((bf16[96,1152]{1,0:T(8,128)(2,1)}, bf16[96,1152]{1,0:T(8,128)(2,1)S(1)}, u32[]{:S(2)}, u32[]{:S(2)}) %collective-permute-start.4) | collective-permute-done | bytes 221216 | tf_op jit(solution)/shard_map/ppermute | solution.py:55
  50.3 7.7 %collective-permute-done.14.d = bf16[2,96,768]{2,1,0:T(8,128)(2,1)S(1)} collective-permute-done((bf16[2,96,768]{2,1,0:T(8,128)(2,1)}, bf16[2,96,768]{2,1,0:T(8,128)(2,1)S(1)}, u32[]{:S(2)}, u32[]{:S(2)}) %collective-permute-start.14) | collective-permute-done | bytes 294944 | tf_op jit(solution)/shard_map/ppermute | solution.py:55
  58.0 10.7 %collective-permute-start.12 = (bf16[2,96,768]{2,1,0:T(8,128)(2,1)}, bf16[2,96,768]{2,1,0:T(8,128)(2,1)S(1)}, u32[]{:S(2)}, u32[]{:S(2)}) collective-permute-start(bf16[2,96,768]{2,1,0:T(8,128)(2,1)} %get-tuple-element.150.a), channel_id=1, source_target_pairs={{0,8},{4,12},{8,0},{12,4},{16,24},{20,28},{24,16},{28,20},{1,9},{5... | collective-permute-start | bytes 884744 | tf_op jit(solution)/shard_map/ppermute | solution.py:55
  68.7 2.9 collective-permute-done.13.c
  71.6 3.0 collective-permute-done.12.b
  75.4 2.3 join_f.1.rest_0_
  81.5 4.5 %turn.1.xt_ref = bf16[2,768,1024]{2,1,0:T(8,128)(2,1)} custom-call(s32[3]{0:T(128)} %pad_add_fusion.scal, bf16[2,272,768]{2,1,0:T(8,128)(2,1)} %get-tuple-element.146.t0, bf16[2,272,768]{2,1,0:T(8,128)(2,1)} %copy-done.2, bf16[2,272,768]{2,1,0:T(8,128)(2,1)} %copy-done.1, bf16[2,272,768]{2,1,0:T(8,128)(2,1)} %copy-done.3), custom_call_target="tpu_custom_call" | custom-call | bytes 12000000 | tf_op jit(solution)/shard_map/turn/pallas_call | solution.py:602
  87.2 8.8 %attend00.1 = (bf16[2,12,256,1024]{3,2,1,0:T(8,128)(2,1)}, bf16[4,256,1024]{2,1,0:T(8,128)(2,1)}, bf16[256,256]{1,0:T(8,128)(2,1)}, bf16[1024,256]{1,0:T(8,128)(...) custom-call(s32[3]{0:T(128)} %pad_add_fusion.scal, ...), custom_call_target="tpu_custom_call" | custom-call | flops 5000000000 | bytes 10000000 | tf_op jit(solution)/shard_map/attend00/pallas_call | solution.py:602
  96.0 8.4 %attend01.1 = (bf16[2,12,256,1024]{3,2,1,0:T(8,128)(2,1)}, bf16[4,256,1024]{2,1,0:T(8,128)(2,1)}, bf16[256,256]{1,0:T(8,128)(2,1)}, bf16[1024,256]{1,0:T(8,128)(...) custom-call(s32[3]{0:T(128)} %pad_add_fusion.scal, ...), custom_call_target="tpu_custom_call", output_to_operand_aliasing={{0}: (12, {})} | custom-call | flops 5000000000 | bytes 10000000 | tf_op jit(solution)/shard_map/attend01/pallas_call | solution.py:602
  109.8 5.5 %collective-permute-done.18.rest_1_ = bf16[2,4,96,768]{3,2,1,0:T(8,128)(2,1)S(1)} collective-permute-done((bf16[2,4,96,768]{3,2,1,0:T(8,128)(2,1)}, bf16[2,4,96,768]{3,2,1,0:T(8,128)(2,1)S(1)}, u32[]{:S(2)}, u32[]{:S(2)}) %collective-permute-start.18) | collective-permute-done | bytes 1179680 | tf_op jit(solution)/shard_map/ppermute | solution.py:55
  118.1 8.4 %attend10.1 = (bf16[2,12,256,1024]{3,2,1,0:T(8,128)(2,1)}, bf16[4,256,1024]{2,1,0:T(8,128)(2,1)}, bf16[256,256]{1,0:T(8,128)(2,1)}, bf16[1024,256]{1,0:T(8,128)(...) custom-call(s32[3]{0:T(128)} %pad_add_fusion.scal, ...), custom_call_target="tpu_custom_call", output_to_operand_aliasing={{0}: (12, {})} | custom-call | flops 5000000000 | bytes 10000000 | tf_op jit(solution)/shard_map/attend10/pallas_call | solution.py:602
  126.6 8.4 %attend11.1 = (bf16[2,12,256,1024]{3,2,1,0:T(8,128)(2,1)}, bf16[4,256,1024]{2,1,0:T(8,128)(2,1)}, bf16[256,256]{1,0:T(8,128)(2,1)}, bf16[1024,256]{1,0:T(8,128)(...) custom-call(s32[3]{0:T(128)} %pad_add_fusion.scal, ...), custom_call_target="tpu_custom_call", output_to_operand_aliasing={{0}: (12, {})} | custom-call | flops 5000000000 | bytes 10000000 | tf_op jit(solution)/shard_map/attend11/pallas_call | solution.py:602
  135.7 8.4 %attend20.1 = (bf16[2,12,256,1024]{3,2,1,0:T(8,128)(2,1)}, bf16[4,256,1024]{2,1,0:T(8,128)(2,1)}, bf16[256,256]{1,0:T(8,128)(2,1)}, bf16[1024,256]{1,0:T(8,128)(...) custom-call(s32[3]{0:T(128)} %pad_add_fusion.scal, ...), custom_call_target="tpu_custom_call", output_to_operand_aliasing={{0}: (12, {})} | custom-call | flops 5000000000 | bytes 10000000 | tf_op jit(solution)/shard_map/attend20/pallas_call | solution.py:602
  144.1 8.9 %attend21.1 = (bf16[2,12,256,1024]{3,2,1,0:T(8,128)(2,1)}, bf16[4,256,1024]{2,1,0:T(8,128)(2,1)}, bf16[256,256]{1,0:T(8,128)(2,1)}, bf16[1024,256]{1,0:T(8,128)(...) custom-call(s32[3]{0:T(128)} %pad_add_fusion.scal, ...), custom_call_target="tpu_custom_call", output_to_operand_aliasing={{0}: (12, {})} | custom-call | flops 5000000000 | bytes 10000000 | tf_op jit(solution)/shard_map/attend21/pallas_call | solution.py:602
  154.4 20.0 %ff_fwd.1 = (bf16[2,256,768]{2,1,0:T(8,128)(2,1)}, bf16[512,768]{1,0:T(8,128)(2,1)}, f32[512,768]{1,0:T(8,128)}, f32[512,1]{1,0:T(8,128)}, bf16[512,768]{1,0:T(8...) custom-call(s32[3]{0:T(128)} %pad_add_fusion.scal, ...), custom_call_target="tpu_custom_call" | custom-call | flops 6000000000 | bytes 25000000 | tf_op jit(solution)/shard_map/ff_fwd/pallas_call | solution.py:602
  174.4 6.2 %down_grad.1 = (bf16[2,8,96,768]{3,2,1,0:T(8,128)(2,1)}, bf16[2,8,96,768]{3,2,1,0:T(8,128)(2,1)}) custom-call(s32[3]{0:T(128)} %pad_add_fusion.scal, bf16[4,512,768]{2,1,0:T(8,128)(2,1)} %get-tuple-element.168.hid, bf16[512,768]{1,0:T(8,128)(2,1)} %get-tuple-element.169.dsec), custom_call_target="tpu_custom_call" | custom-call | flops 3000000000 | bytes 8000000 | tf_op jit(solution)/shard_map/down_grad/pallas_call | solution.py:602
  180.5 12.3 %in_grad.1 = (bf16[2,8,96,768]{3,2,1,0:T(8,128)(2,1)}, bf16[2,8,96,768]{3,2,1,0:T(8,128)(2,1)}, bf16[4,512,768]{2,1,0:T(8,128)(2,1)}, f32[4,1,768]{2,1,0:T(1,128)}) custom-call(s32[3]{0:T(128)} %pad_add_fusion.scal, bf16[512,768]{1,0:T(8,128)(2,1)} %get-tuple-element.172.inner, bf16[4,512,768]{2,1,0:T(8,128)(2,1)} %get-tuple-element.173.dg, ...), custom_call_target="tpu_custom_call" | custom-call | flops 6000000000 | bytes 20000000 | tf_op jit(solution)/shard_map/in_grad/pallas_call | solution.py:602
  193.4 12.8 %first_grad.1 = (bf16[8,96,384]{2,1,0:T(8,128)(2,1)}, bf16[8,96,384]{2,1,0:T(8,128)(2,1)}, f32[512,768]{1,0:T(8,128)}, bf16[512,768]{1,0:T(8,128)(2,1)}, f32[8,768]{1,0:T(8,128)}) custom-call(s32[3]{0:T(128)} %pad_add_fusion.scal, bf16[512,768]{1,0:T(8,128)(2,1)} %get-tuple-element.181.mix_ref, f32[512,768]{1,0:T(8,128)} %get-tuple-element.182.first_n, ...), custom_call_target="tpu_custom_call" | custom-call | flops 4000000000 | bytes 15000000 | tf_op jit(solution)/shard_map/first_grad/pallas_call | solution.py:602
  207.7 2.8 fusion.2
  214.3 7.3 %back00.1 = (bf16[2,12,256,1024]{3,2,1,0:T(8,128)(2,1)}, bf16[256,256]{1,0:T(8,128)(2,1)}, bf16[1024,512]{1,0:T(8,128)(2,1)}) custom-call(s32[3]{0:T(128)} %pad_add_fusion.scal, bf16[4,256,1024]{2,1,0:T(8,128)(2,1)} %get-tuple-element.180.e_ref, bf16[512,768]{1,0:T(8,128)(2,1)} %get-tuple-element.186.dm_ref, bf16[256,256]{1,0:T(8,128)(2,1)} %get-tuple-element.187.q_ref, ...), custom_call_target="tpu_custom_call" | custom-call | flops 5000000000 | bytes 10000000 | tf_op jit(solution)/shard_map/back00/pallas_call | solution.py:602
  221.7 4.8 %collective-permute-done.28 = bf16[4,96,768]{2,1,0:T(8,128)(2,1)} collective-permute-done((bf16[4,96,768]{2,1,0:T(8,128)(2,1)}, bf16[4,96,768]{2,1,0:T(8,128)(2,1)}, u32[]{:S(2)}, u32[]{:S(2)}) %collective-permute-start.28) | collective-permute-done | bytes 589856 | tf_op jit(solution)/shard_map/ppermute | solution.py:55
  232.9 7.3 %back01.1 = (bf16[2,12,256,1024]{3,2,1,0:T(8,128)(2,1)}, bf16[256,256]{1,0:T(8,128)(2,1)}, bf16[1024,512]{1,0:T(8,128)(2,1)}) custom-call(s32[3]{0:T(128)} %pad_add_fusion.scal, bf16[4,256,1024]{2,1,0:T(8,128)(2,1)} %get-tuple-element.192.e_ref, bf16[512,768]{1,0:T(8,128)(2,1)} %get-tuple-element.186.dm_ref, ...), custom_call_target="tpu_custom_call", output_to_operand_aliasing={{0}: (8, {})} | custom-call | flops 5000000000 | bytes 10000000 | tf_op jit(solution)/shard_map/back01/pallas_call | solution.py:602
  240.2 6.6 %weight_grad0.1 = (bf16[8,96,768]{2,1,0:T(8,128)(2,1)}, bf16[8,96,768]{2,1,0:T(8,128)(2,1)}, f32[8,256]{1,0:T(8,128)}) custom-call(s32[3]{0:T(128)} %pad_add_fusion.scal, bf16[2,768,1024]{2,1,0:T(8,128)(2,1)} %turn.1.xt_ref, bf16[256,256]{1,0:T(8,128)(2,1)} %get-tuple-element.191.dq0.dq00, bf16[256,256]{1,0:T(8,128)(2,1)} %get-tuple-element.198.dq1.dq01, ...), custom_call_target="tpu_custom_call" | custom-call | flops 2000000000 | bytes 8000000 | tf_op jit(solution)/shard_map/weight_grad0/pallas_call | solution.py:602
  246.8 7.4 %back10.1 = (bf16[2,12,256,1024]{3,2,1,0:T(8,128)(2,1)}, bf16[256,256]{1,0:T(8,128)(2,1)}, bf16[1024,512]{1,0:T(8,128)(2,1)}) custom-call(s32[3]{0:T(128)} %pad_add_fusion.scal, bf16[4,256,1024]{2,1,0:T(8,128)(2,1)} %get-tuple-element.205.e_ref, bf16[512,768]{1,0:T(8,128)(2,1)} %get-tuple-element.186.dm_ref, ...), custom_call_target="tpu_custom_call", output_to_operand_aliasing={{0}: (8, {})} | custom-call | flops 5000000000 | bytes 10000000 | tf_op jit(solution)/shard_map/back10/pallas_call | solution.py:602
  254.1 2.9 collective-permute-done.30
  257.1 2.6 collective-permute-done.32
  259.6 2.7 fusion.5
  267.6 7.4 %back11.1 = (bf16[2,12,256,1024]{3,2,1,0:T(8,128)(2,1)}, bf16[256,256]{1,0:T(8,128)(2,1)}, bf16[1024,512]{1,0:T(8,128)(2,1)}) custom-call(s32[3]{0:T(128)} %pad_add_fusion.scal, bf16[4,256,1024]{2,1,0:T(8,128)(2,1)} %get-tuple-element.214.e_ref, bf16[512,768]{1,0:T(8,128)(2,1)} %get-tuple-element.186.dm_ref, ...), custom_call_target="tpu_custom_call", output_to_operand_aliasing={{0}: (8, {})} | custom-call | flops 5000000000 | bytes 10000000 | tf_op jit(solution)/shard_map/back11/pallas_call | solution.py:602
  277.0 5.8 %weight_grad1.1 = (bf16[8,96,384]{2,1,0:T(8,128)(2,1)}, bf16[8,96,384]{2,1,0:T(8,128)(2,1)}, f32[8,256]{1,0:T(8,128)}) custom-call(s32[3]{0:T(128)} %pad_add_fusion.scal, bf16[2,768,1024]{2,1,0:T(8,128)(2,1)} %turn.1.xt_ref, bf16[256,256]{1,0:T(8,128)(2,1)} %get-tuple-element.211.dq0.dq10, bf16[256,256]{1,0:T(8,128)(2,1)} %get-tuple-element.220.dq1.dq11, ...), custom_call_target="tpu_custom_call" | custom-call | flops 2000000000 | bytes 8000000 | tf_op jit(solution)/shard_map/weight_grad1/pallas_call | solution.py:602
  282.8 5.0 %collective-permute-done.34 = bf16[2,96,768]{2,1,0:T(8,128)(2,1)S(1)} collective-permute-done((bf16[2,96,768]{2,1,0:T(8,128)(2,1)}, bf16[2,96,768]{2,1,0:T(8,128)(2,1)S(1)}, u32[]{:S(2)}, u32[]{:S(2)}) %collective-permute-start.34) | collective-permute-done | bytes 294944 | tf_op jit(solution)/shard_map/ppermute | solution.py:55
  288.6 7.6 %back20.1 = (bf16[2,12,256,1024]{3,2,1,0:T(8,128)(2,1)}, bf16[256,256]{1,0:T(8,128)(2,1)}, bf16[1024,512]{1,0:T(8,128)(2,1)}) custom-call(s32[3]{0:T(128)} %pad_add_fusion.scal, bf16[4,256,1024]{2,1,0:T(8,128)(2,1)} %get-tuple-element.225.e_ref, bf16[512,768]{1,0:T(8,128)(2,1)} %get-tuple-element.186.dm_ref, ...), custom_call_target="tpu_custom_call", output_to_operand_aliasing={{0}: (8, {})} | custom-call | flops 5000000000 | bytes 10000000 | tf_op jit(solution)/shard_map/back20/pallas_call | solution.py:602
  298.0 4.1 %collective-permute-start.42 = (bf16[96,768]{1,0:T(8,128)(2,1)S(1)}, bf16[96,768]{1,0:T(8,128)(2,1)S(1)}, u32[]{:S(2)}, u32[]{:S(2)}) collective-permute-start(bf16[96,768]{1,0:T(8,128)(2,1)S(1)} %get-tuple-element.278), channel_id=1, source_target_pairs={{0,8},{4,12},{8,0},{12,4},{16,24},{20,28},{24,16},{28,20},{1,9},{5... | collective-permute-start | bytes 442376 | tf_op jit(solution)/shard_map/ppermute | solution.py:55
  304.4 7.4 %back21.1 = (bf16[2,12,256,1024]{3,2,1,0:T(8,128)(2,1)}, bf16[256,256]{1,0:T(8,128)(2,1)}, bf16[1024,512]{1,0:T(8,128)(2,1)}) custom-call(s32[3]{0:T(128)} %pad_add_fusion.scal, bf16[4,256,1024]{2,1,0:T(8,128)(2,1)} %get-tuple-element.235.e_ref, bf16[512,768]{1,0:T(8,128)(2,1)} %get-tuple-element.186.dm_ref, ...), custom_call_target="tpu_custom_call", output_to_operand_aliasing={{0}: (8, {})} | custom-call | flops 5000000000 | bytes 10000000 | tf_op jit(solution)/shard_map/back21/pallas_call | solution.py:602
  311.7 6.0 %weight_grad2.1 = (bf16[8,112,384]{2,1,0:T(8,128)(2,1)}, bf16[8,112,384]{2,1,0:T(8,128)(2,1)}, f32[8,256]{1,0:T(8,128)}) custom-call(s32[3]{0:T(128)} %pad_add_fusion.scal, bf16[2,768,1024]{2,1,0:T(8,128)(2,1)} %turn.1.xt_ref, bf16[256,256]{1,0:T(8,128)(2,1)} %get-tuple-element.231.dq0.dq20, bf16[256,256]{1,0:T(8,128)(2,1)} %get-tuple-element.241.dq1.dq21, ...), custom_call_target="tpu_custom_call" | custom-call | flops 2000000000 | bytes 8000000 | tf_op jit(solution)/shard_map/weight_grad2/pallas_call | solution.py:602
  322.0 7.0 %collective-permute-done.43 = bf16[96,768]{1,0:T(8,128)(2,1)S(1)} collective-permute-done((bf16[96,768]{1,0:T(8,128)(2,1)S(1)}, bf16[96,768]{1,0:T(8,128)(2,1)S(1)}, u32[]{:S(2)}, u32[]{:S(2)}) %collective-permute-start.43) | collective-permute-done | bytes 147488 | tf_op jit(solution)/shard_map/ppermute | solution.py:55
  332.9 11.6 %token_grad.1 = (f32[2,256,768]{2,1,0:T(8,128)}, bf16[2,256,768]{2,1,0:T(8,128)(2,1)}, bf16[2,256,768]{2,1,0:T(8,128)(2,1)}, bf16[2,256,768]{2,1,0:T(8,128)(2,1)}) custom-call(s32[3]{0:T(128)} %pad_add_fusion.scal, bf16[256,256]{1,0:T(8,128)(2,1)} %get-tuple-element.191.dq0.dq00, bf16[256,256]{1,0:T(8,128)(2,1)} %get-tuple-element.198.dq1.dq01, ...), custom_call_target="tpu_custom_call" | custom-call | flops 10000000000 | bytes 15000000 | tf_op jit(solution)/shard_map/token_grad/pallas_call | solution.py:602
  345.8 2.4 collective-permute-start.51
  353.1 2.4 collective-permute-start.57
  357.6 2.8 collective-permute-done.57
  378.9 3.7 finish.1
  385.3 3.6 collective-permute-done.41
  (213 shorter events, 94.9 us)
Async XLA Ops:
  6.3 43.9 %collective-permute-start.7 = (bf16[2,272,768]{2,1,0:T(8,128)(2,1)}, bf16[2,272,768]{2,1,0:T(8,128)(2,1)S(1)}, u32[]{:S(2)}, u32[]{:S(2)}) collective-permute-start(bf16[2,272,768]{2,1,0:T(8,128)(2,1)} %get-tuple-element.146.t0), channel_id=1, source_target_pairs={{0,2},{1,3},{2,0},{3,1},{4,6},{5,7},{6,4},{7,5},{8,10},{9,11},{10,... | collective-permute-start | bytes 2506760 | tf_op jit(solution)/shard_map/ppermute | solution.py:55
  23.1 10.5 %collective-permute-start.5 = (bf16[96,1152]{1,0:T(8,128)(2,1)}, bf16[96,1152]{1,0:T(8,128)(2,1)S(1)}, u32[]{:S(2)}, u32[]{:S(2)}) collective-permute-start(bf16[96,1152]{1,0:T(8,128)(2,1)} %get-tuple-element.144.a), channel_id=1, source_target_pairs={{0,24},{4,28},{8,16},{12,20},{16,8},{20,12},{24,0},{28,4},{1,25},{... | collective-permute-start | bytes 663560 | tf_op jit(solution)/shard_map/ppermute | solution.py:55
  25.6 17.5 %collective-permute-start.4 = (bf16[96,1152]{1,0:T(8,128)(2,1)}, bf16[96,1152]{1,0:T(8,128)(2,1)S(1)}, u32[]{:S(2)}, u32[]{:S(2)}) collective-permute-start(bf16[96,1152]{1,0:T(8,128)(2,1)} %get-tuple-element.144.a), channel_id=1, source_target_pairs={{0,16},{4,20},{8,24},{12,28},{16,0},{20,4},{24,8},{28,12},{1,17},{... | collective-permute-start | bytes 663560 | tf_op jit(solution)/shard_map/ppermute | solution.py:55
  25.6 17.5 %collective-permute-start.3 = (bf16[96,1152]{1,0:T(8,128)(2,1)}, bf16[96,1152]{1,0:T(8,128)(2,1)S(1)}, u32[]{:S(2)}, u32[]{:S(2)}) collective-permute-start(bf16[96,1152]{1,0:T(8,128)(2,1)} %get-tuple-element.144.a), channel_id=1, source_target_pairs={{0,8},{4,12},{8,0},{12,4},{16,24},{20,28},{24,16},{28,20},{1,9},{5... | collective-permute-start | bytes 663560 | tf_op jit(solution)/shard_map/ppermute | solution.py:55
  27.4 50.3 %collective-permute-start.6 = (bf16[2,272,768]{2,1,0:T(8,128)(2,1)}, bf16[2,272,768]{2,1,0:T(8,128)(2,1)S(1)}, u32[]{:S(2)}, u32[]{:S(2)}) collective-permute-start(bf16[2,272,768]{2,1,0:T(8,128)(2,1)} %get-tuple-element.146.t0), channel_id=1, source_target_pairs={{0,1},{1,0},{2,3},{3,2},{4,5},{5,4},{6,7},{7,6},{8,9},{9,8},{10,11... | collective-permute-start | bytes 2506760 | tf_op jit(solution)/shard_map/ppermute | solution.py:55
  33.5 16.7 %collective-permute-start.9 = (bf16[4,112,384]{2,1,0:T(8,128)(2,1)}, bf16[4,112,384]{2,1,0:T(8,128)(2,1)S(1)}, u32[]{:S(2)}, u32[]{:S(2)}) collective-permute-start(bf16[4,112,384]{2,1,0:T(8,128)(2,1)} %join_a.1.lo.own_lo.a_lo), channel_id=1, source_target_pairs={{0,4},{4,0},{8,12},{12,8},{16,20},{20,16},{24,28},{28,24},{1,5},{5... | collective-permute-start | bytes 1032200 | tf_op jit(solution)/shard_map/ppermute | solution.py:55
  46.8 11.2 %collective-permute-start.14 = (bf16[2,96,768]{2,1,0:T(8,128)(2,1)}, bf16[2,96,768]{2,1,0:T(8,128)(2,1)S(1)}, u32[]{:S(2)}, u32[]{:S(2)}) collective-permute-start(bf16[2,96,768]{2,1,0:T(8,128)(2,1)} %get-tuple-element.150.a), channel_id=1, source_target_pairs={{0,24},{4,28},{8,16},{12,20},{16,8},{20,12},{24,0},{28,4},{1,25},{... | collective-permute-start | bytes 884744 | tf_op jit(solution)/shard_map/ppermute | solution.py:55
  48.7 38.5 %collective-permute-start.15 = (bf16[4,96,1152]{2,1,0:T(8,128)(2,1)}, bf16[4,96,1152]{2,1,0:T(8,128)(2,1)}, u32[]{:S(2)}, u32[]{:S(2)}) collective-permute-start(bf16[4,96,1152]{2,1,0:T(8,128)(2,1)} %join_b.1.own_lo.wl.b_lo), channel_id=1, source_target_pairs={{0,4},{4,0},{8,12},{12,8},{16,20},{20,16},{24,28},{28,24},{1,5},{5... | collective-permute-start | bytes 2654216 | tf_op jit(solution)/shard_map/ppermute | solution.py:55
  50.2 30.4 %collective-permute-start.8 = (bf16[2,272,768]{2,1,0:T(8,128)(2,1)S(1)}, bf16[2,272,768]{2,1,0:T(8,128)(2,1)S(1)}, u32[]{:S(2)}, u32[]{:S(2)}) collective-permute-start(bf16[2,272,768]{2,1,0:T(8,128)(2,1)S(1)} %collective-permute-done.7.t2), channel_id=1, source_target_pairs={{0,1},{1,0},{2,3},{3,2},{4,5},{5,4},{6,7},{7,6},{8,9},{9,8},{10,11... | collective-permute-start | bytes 2506760 | tf_op jit(solution)/shard_map/ppermute | solution.py:55
  50.2 21.4 %collective-permute-start.13 = (bf16[2,96,768]{2,1,0:T(8,128)(2,1)}, bf16[2,96,768]{2,1,0:T(8,128)(2,1)S(1)}, u32[]{:S(2)}, u32[]{:S(2)}) collective-permute-start(bf16[2,96,768]{2,1,0:T(8,128)(2,1)} %get-tuple-element.150.a), channel_id=1, source_target_pairs={{0,16},{4,20},{8,24},{12,28},{16,0},{20,4},{24,8},{28,12},{1,17},{... | collective-permute-start | bytes 884744 | tf_op jit(solution)/shard_map/ppermute | solution.py:55
  58.0 16.7 %collective-permute-start.12 = (bf16[2,96,768]{2,1,0:T(8,128)(2,1)}, bf16[2,96,768]{2,1,0:T(8,128)(2,1)S(1)}, u32[]{:S(2)}, u32[]{:S(2)}) collective-permute-start(bf16[2,96,768]{2,1,0:T(8,128)(2,1)} %get-tuple-element.150.a), channel_id=1, source_target_pairs={{0,8},{4,12},{8,0},{12,4},{16,24},{20,28},{24,16},{28,20},{1,9},{5... | collective-permute-start | bytes 884744 | tf_op jit(solution)/shard_map/ppermute | solution.py:55
  71.6 14.5 %collective-permute-start.10 = (bf16[4,112,384]{2,1,0:T(8,128)(2,1)S(1)}, bf16[4,112,384]{2,1,0:T(8,128)(2,1)}, u32[]{:S(2)}, u32[]{:S(2)}) collective-permute-start(bf16[4,112,384]{2,1,0:T(8,128)(2,1)S(1)} %copy-done.5), channel_id=1, source_target_pairs={{0,1},{1,0},{2,3},{3,2},{4,5},{5,4},{6,7},{7,6},{8,9},{9,8},{10,11... | collective-permute-start | bytes 1032200 | tf_op jit(solution)/shard_map/ppermute | solution.py:55
  75.4 10.9 %collective-permute-start.11 = (bf16[4,112,384]{2,1,0:T(8,128)(2,1)S(1)}, bf16[4,112,384]{2,1,0:T(8,128)(2,1)}, u32[]{:S(2)}, u32[]{:S(2)}) collective-permute-start(bf16[4,112,384]{2,1,0:T(8,128)(2,1)S(1)} %collective-permute-done.9.hi.own_hi.a_hi), channel_id=1, source_target_pairs={{0,1},{1,0},{2,3},{3,2},{4,5},{5,4},{6,7},{7,6},{8,9},{9,8},{10,11... | collective-permute-start | bytes 1032200 | tf_op jit(solution)/shard_map/ppermute | solution.py:55
  77.7 28.7 %collective-permute-start.19 = (bf16[2,4,96,768]{3,2,1,0:T(8,128)(2,1)}, bf16[2,4,96,768]{3,2,1,0:T(8,128)(2,1)}, u32[]{:S(2)}, u32[]{:S(2)}) collective-permute-start(bf16[2,4,96,768]{3,2,1,0:T(8,128)(2,1)} %join_f.1.rest_0_), channel_id=1, source_target_pairs={{0,2},{1,3},{2,0},{3,1},{4,6},{5,7},{6,4},{7,5},{8,10},{9,11},{10,... | collective-permute-start | bytes 3538952 | tf_op jit(solution)/shard_map/ppermute | solution.py:55
  80.6 36.6 %collective-permute-start.16 = (bf16[4,96,1152]{2,1,0:T(8,128)(2,1)S(1)}, bf16[4,96,1152]{2,1,0:T(8,128)(2,1)}, u32[]{:S(2)}, u32[]{:S(2)}) collective-permute-start(bf16[4,96,1152]{2,1,0:T(8,128)(2,1)S(1)} %copy-done), channel_id=1, source_target_pairs={{0,1},{1,0},{2,3},{3,2},{4,5},{5,4},{6,7},{7,6},{8,9},{9,8},{10,11... | collective-permute-start | bytes 2654216 | tf_op jit(solution)/shard_map/ppermute | solution.py:55
  86.1 66.9 %collective-permute-start.22 = (bf16[2,4,96,768]{3,2,1,0:T(8,128)(2,1)}, bf16[2,4,96,768]{3,2,1,0:T(8,128)(2,1)}, u32[]{:S(2)}, u32[]{:S(2)}) collective-permute-start(bf16[2,4,96,768]{3,2,1,0:T(8,128)(2,1)} %join_f.1.rest_0_), channel_id=1, source_target_pairs={{0,1},{1,0},{2,3},{3,2},{4,5},{5,4},{6,7},{7,6},{8,9},{9,8},{10,11... | collective-permute-start | bytes 3538952 | tf_op jit(solution)/shard_map/ppermute | solution.py:55
  86.3 29.0 %collective-permute-start.18 = (bf16[2,4,96,768]{3,2,1,0:T(8,128)(2,1)}, bf16[2,4,96,768]{3,2,1,0:T(8,128)(2,1)S(1)}, u32[]{:S(2)}, u32[]{:S(2)}) collective-permute-start(bf16[2,4,96,768]{3,2,1,0:T(8,128)(2,1)} %join_f.1.rest_0_), channel_id=1, source_target_pairs={{0,4},{4,0},{8,12},{12,8},{16,20},{20,16},{24,28},{28,24},{1,5},{5... | collective-permute-start | bytes 3538952 | tf_op jit(solution)/shard_map/ppermute | solution.py:55
  87.2 30.0 %collective-permute-start.17 = (bf16[4,96,1152]{2,1,0:T(8,128)(2,1)}, bf16[4,96,1152]{2,1,0:T(8,128)(2,1)S(1)}, u32[]{:S(2)}, u32[]{:S(2)}) collective-permute-start(bf16[4,96,1152]{2,1,0:T(8,128)(2,1)} %collective-permute-done.15.own_hi.wh.b_hi), channel_id=1, source_target_pairs={{0,1},{1,0},{2,3},{3,2},{4,5},{5,4},{6,7},{7,6},{8,9},{9,8},{10,11... | collective-permute-start | bytes 2654216 | tf_op jit(solution)/shard_map/ppermute | solution.py:55
  108.3 26.6 %collective-permute-start.21 = (bf16[4,96,768]{2,1,0:T(8,128)(2,1)}, bf16[4,96,768]{2,1,0:T(8,128)(2,1)}, u32[]{:S(2)}, u32[]{:S(2)}) collective-permute-start(bf16[4,96,768]{2,1,0:T(8,128)(2,1)} %slice_bitcast_fusion), channel_id=1, source_target_pairs={{0,4},{4,0},{8,12},{12,8},{16,20},{20,16},{24,28},{28,24},{1,5},{5... | collective-permute-start | bytes 1769480 | tf_op jit(solution)/shard_map/ppermute | solution.py:55
  116.3 19.3 %collective-permute-start.20 = (bf16[4,96,768]{2,1,0:T(8,128)(2,1)}, bf16[4,96,768]{2,1,0:T(8,128)(2,1)}, u32[]{:S(2)}, u32[]{:S(2)}) collective-permute-start(bf16[4,96,768]{2,1,0:T(8,128)(2,1)} %slice_bitcast_fusion.1), channel_id=1, source_target_pairs={{0,2},{1,3},{2,0},{3,1},{4,6},{5,7},{6,4},{7,5},{8,10},{9,11},{10,... | collective-permute-start | bytes 1769480 | tf_op jit(solution)/shard_map/ppermute | solution.py:55
  117.2 35.8 %collective-permute-start.24 = (bf16[2,4,96,768]{3,2,1,0:T(8,128)(2,1)}, bf16[2,4,96,768]{3,2,1,0:T(8,128)(2,1)S(1)}, u32[]{:S(2)}, u32[]{:S(2)}) collective-permute-start(bf16[2,4,96,768]{3,2,1,0:T(8,128)(2,1)} %collective-permute-done.19.rest_2_), channel_id=1, source_target_pairs={{0,1},{1,0},{2,3},{3,2},{4,5},{5,4},{6,7},{7,6},{8,9},{9,8},{10,11... | collective-permute-start | bytes 3538952 | tf_op jit(solution)/shard_map/ppermute | solution.py:55
  117.2 35.8 %collective-permute-start.23 = (bf16[2,4,96,768]{3,2,1,0:T(8,128)(2,1)S(1)}, bf16[2,4,96,768]{3,2,1,0:T(8,128)(2,1)}, u32[]{:S(2)}, u32[]{:S(2)}) collective-permute-start(bf16[2,4,96,768]{3,2,1,0:T(8,128)(2,1)S(1)} %collective-permute-done.18.rest_1_), channel_id=1, source_target_pairs={{0,1},{1,0},{2,3},{3,2},{4,5},{5,4},{6,7},{7,6},{8,9},{9,8},{10,11... | collective-permute-start | bytes 3538952 | tf_op jit(solution)/shard_map/ppermute | solution.py:55
  135.0 18.0 %collective-permute-start.26 = (bf16[4,96,768]{2,1,0:T(8,128)(2,1)}, bf16[4,96,768]{2,1,0:T(8,128)(2,1)S(1)}, u32[]{:S(2)}, u32[]{:S(2)}) collective-permute-start(bf16[4,96,768]{2,1,0:T(8,128)(2,1)} %collective-permute-done.21.rest_4_), channel_id=1, source_target_pairs={{0,1},{1,0},{2,3},{3,2},{4,5},{5,4},{6,7},{7,6},{8,9},{9,8},{10,11... | collective-permute-start | bytes 1769480 | tf_op jit(solution)/shard_map/ppermute | solution.py:55
  135.6 17.4 %collective-permute-start.25 = (bf16[4,96,768]{2,1,0:T(8,128)(2,1)}, bf16[4,96,768]{2,1,0:T(8,128)(2,1)S(1)}, u32[]{:S(2)}, u32[]{:S(2)}) collective-permute-start(bf16[4,96,768]{2,1,0:T(8,128)(2,1)} %collective-permute-done.20.rest_3_), channel_id=1, source_target_pairs={{0,1},{1,0},{2,3},{3,2},{4,5},{5,4},{6,7},{7,6},{8,9},{9,8},{10,11... | collective-permute-start | bytes 1769480 | tf_op jit(solution)/shard_map/ppermute | solution.py:55
  192.8 13.4 %collective-permute-start.27 = (bf16[2,8,96,768]{3,2,1,0:T(8,128)(2,1)}, bf16[2,8,96,768]{3,2,1,0:T(8,128)(2,1)S(1)}, u32[]{:S(2)}, u32[]{:S(2)}) collective-permute-start(bf16[2,8,96,768]{3,2,1,0:T(8,128)(2,1)} %get-tuple-element.175), channel_id=1, source_target_pairs={{0,1},{1,0},{2,3},{3,2},{4,5},{5,4},{6,7},{7,6},{8,9},{9,8},{10,11... | collective-permute-start | bytes 7077896 | tf_op jit(solution)/shard_map/ppermute | solution.py:55
  193.3 18.3 %collective-permute-start.29 = (bf16[2,8,96,768]{3,2,1,0:T(8,128)(2,1)}, bf16[2,8,96,768]{3,2,1,0:T(8,128)(2,1)}, u32[]{:S(2)}, u32[]{:S(2)}) collective-permute-start(bf16[2,8,96,768]{3,2,1,0:T(8,128)(2,1)} %get-tuple-element.176), channel_id=1, source_target_pairs={{0,1},{1,0},{2,3},{3,2},{4,5},{5,4},{6,7},{7,6},{8,9},{9,8},{10,11... | collective-permute-start | bytes 7077896 | tf_op jit(solution)/shard_map/ppermute | solution.py:55
  210.5 16.0 %collective-permute-start.28 = (bf16[4,96,768]{2,1,0:T(8,128)(2,1)}, bf16[4,96,768]{2,1,0:T(8,128)(2,1)}, u32[]{:S(2)}, u32[]{:S(2)}) collective-permute-start(bf16[4,96,768]{2,1,0:T(8,128)(2,1)} %get-tuple-element.265), channel_id=1, source_target_pairs={{0,2},{1,3},{2,0},{3,1},{4,6},{5,7},{6,4},{7,5},{8,10},{9,11},{10,... | collective-permute-start | bytes 1769480 | tf_op jit(solution)/shard_map/ppermute | solution.py:55
  213.3 17.3 %collective-permute-start.31 = (bf16[4,96,768]{2,1,0:T(8,128)(2,1)S(1)}, bf16[4,96,768]{2,1,0:T(8,128)(2,1)}, u32[]{:S(2)}, u32[]{:S(2)}) collective-permute-start(bf16[4,96,768]{2,1,0:T(8,128)(2,1)S(1)} %get-tuple-element.268), channel_id=1, source_target_pairs={{0,4},{4,0},{8,12},{12,8},{16,20},{20,16},{24,28},{28,24},{1,5},{5... | collective-permute-start | bytes 1769480 | tf_op jit(solution)/shard_map/ppermute | solution.py:55
  229.2 27.8 %collective-permute-start.30 = (bf16[2,4,96,768]{3,2,1,0:T(8,128)(2,1)}, bf16[2,4,96,768]{3,2,1,0:T(8,128)(2,1)}, u32[]{:S(2)}, u32[]{:S(2)}) collective-permute-start(bf16[2,4,96,768]{3,2,1,0:T(8,128)(2,1)} %pad_maximum_fusion.1), channel_id=1, source_target_pairs={{0,4},{4,0},{8,12},{12,8},{16,20},{20,16},{24,28},{28,24},{1,5},{5... | collective-permute-start | bytes 3538952 | tf_op jit(solution)/shard_map/ppermute | solution.py:55
  232.2 27.4 %collective-permute-start.32 = (bf16[2,4,96,768]{3,2,1,0:T(8,128)(2,1)S(1)}, bf16[2,4,96,768]{3,2,1,0:T(8,128)(2,1)}, u32[]{:S(2)}, u32[]{:S(2)}) collective-permute-start(bf16[2,4,96,768]{3,2,1,0:T(8,128)(2,1)S(1)} %pad_maximum_fusion.2), channel_id=1, source_target_pairs={{0,2},{1,3},{2,0},{3,1},{4,6},{5,7},{6,4},{7,5},{8,10},{9,11},{10,... | collective-permute-start | bytes 3538952 | tf_op jit(solution)/shard_map/ppermute | solution.py:55
  246.8 20.9 %collective-permute-start.36 = (bf16[8,96,768]{2,1,0:T(8,128)(2,1)}, bf16[8,96,768]{2,1,0:T(8,128)(2,1)}, u32[]{:S(2)}, u32[]{:S(2)}) collective-permute-start(bf16[8,96,768]{2,1,0:T(8,128)(2,1)} %get-tuple-element.212), channel_id=1, source_target_pairs={{0,1},{1,0},{2,3},{3,2},{4,5},{5,4},{6,7},{7,6},{8,9},{9,8},{10,11... | collective-permute-start | bytes 3538952 | tf_op jit(solution)/shard_map/ppermute | solution.py:55
  263.3 19.5 %collective-permute-start.33 = (bf16[2,96,768]{2,1,0:T(8,128)(2,1)}, bf16[2,96,768]{2,1,0:T(8,128)(2,1)S(1)}, u32[]{:S(2)}, u32[]{:S(2)}) collective-permute-start(bf16[2,96,768]{2,1,0:T(8,128)(2,1)} %get-tuple-element.271), channel_id=1, source_target_pairs={{0,8},{4,12},{8,0},{12,4},{16,24},{20,28},{24,16},{28,20},{1,9},{5... | collective-permute-start | bytes 884744 | tf_op jit(solution)/shard_map/ppermute | solution.py:55
  264.1 23.7 %collective-permute-start.34 = (bf16[2,96,768]{2,1,0:T(8,128)(2,1)}, bf16[2,96,768]{2,1,0:T(8,128)(2,1)S(1)}, u32[]{:S(2)}, u32[]{:S(2)}) collective-permute-start(bf16[2,96,768]{2,1,0:T(8,128)(2,1)} %get-tuple-element.272), channel_id=1, source_target_pairs={{0,16},{4,20},{8,24},{12,28},{16,0},{20,4},{24,8},{28,12},{1,17},{... | collective-permute-start | bytes 884744 | tf_op jit(solution)/shard_map/ppermute | solution.py:55
  265.9 21.9 %collective-permute-start.35 = (bf16[2,96,768]{2,1,0:T(8,128)(2,1)S(1)}, bf16[2,96,768]{2,1,0:T(8,128)(2,1)S(1)}, u32[]{:S(2)}, u32[]{:S(2)}) collective-permute-start(bf16[2,96,768]{2,1,0:T(8,128)(2,1)S(1)} %get-tuple-element.273), channel_id=1, source_target_pairs={{0,24},{4,28},{8,16},{12,20},{16,8},{20,12},{24,0},{28,4},{1,25},{... | collective-permute-start | bytes 884744 | tf_op jit(solution)/shard_map/ppermute | solution.py:55
  276.3 20.1 %collective-permute-start.37 = (bf16[4,96,768]{2,1,0:T(8,128)(2,1)S(1)}, bf16[4,96,768]{2,1,0:T(8,128)(2,1)}, u32[]{:S(2)}, u32[]{:S(2)}) collective-permute-start(bf16[4,96,768]{2,1,0:T(8,128)(2,1)S(1)} %add_convert_fusion.2), channel_id=1, source_target_pairs={{0,4},{4,0},{8,12},{12,8},{16,20},{20,16},{24,28},{28,24},{1,5},{5... | collective-permute-start | bytes 1769480 | tf_op jit(solution)/shard_map/ppermute | solution.py:55
  282.8 37.0 %collective-permute-start.47 = (bf16[8,96,384]{2,1,0:T(8,128)(2,1)}, bf16[8,96,384]{2,1,0:T(8,128)(2,1)}, u32[]{:S(2)}, u32[]{:S(2)}) collective-permute-start(bf16[8,96,384]{2,1,0:T(8,128)(2,1)} %get-tuple-element.256), channel_id=1, source_target_pairs={{0,1},{1,0},{2,3},{3,2},{4,5},{5,4},{6,7},{7,6},{8,9},{9,8},{10,11... | collective-permute-start | bytes 1769480 | tf_op jit(solution)/shard_map/ppermute | solution.py:55
  296.3 81.4 %collective-permute-start.61 = (bf16[2,2,96,768]{3,2,1,0:T(8,128)(2,1)S(1)}, bf16[2,2,96,768]{3,2,1,0:T(8,128)(2,1)}, u32[]{:S(2)}, u32[]{:S(2)}) collective-permute-start(bf16[2,2,96,768]{3,2,1,0:T(8,128)(2,1)S(1)} %pad_maximum_fusion.3.ff), channel_id=1, source_target_pairs={{0,1},{1,0},{2,3},{3,2},{4,5},{5,4},{6,7},{7,6},{8,9},{9,8},{10,11... | collective-permute-start | bytes 1769480 | tf_op jit(solution)/shard_map/ppermute | solution.py:55
  298.0 22.8 %collective-permute-start.42 = (bf16[96,768]{1,0:T(8,128)(2,1)S(1)}, bf16[96,768]{1,0:T(8,128)(2,1)S(1)}, u32[]{:S(2)}, u32[]{:S(2)}) collective-permute-start(bf16[96,768]{1,0:T(8,128)(2,1)S(1)} %get-tuple-element.278), channel_id=1, source_target_pairs={{0,8},{4,12},{8,0},{12,4},{16,24},{20,28},{24,16},{28,20},{1,9},{5... | collective-permute-start | bytes 442376 | tf_op jit(solution)/shard_map/ppermute | solution.py:55
  302.1 19.9 %collective-permute-start.44 = (bf16[96,768]{1,0:T(8,128)(2,1)S(1)}, bf16[96,768]{1,0:T(8,128)(2,1)S(1)}, u32[]{:S(2)}, u32[]{:S(2)}) collective-permute-start(bf16[96,768]{1,0:T(8,128)(2,1)S(1)} %get-tuple-element.279), channel_id=1, source_target_pairs={{0,24},{4,28},{8,16},{12,20},{16,8},{20,12},{24,0},{28,4},{1,25},{... | collective-permute-start | bytes 442376 | tf_op jit(solution)/shard_map/ppermute | solution.py:55
  317.7 11.4 %collective-permute-start.38 = (bf16[8,112,384]{2,1,0:T(8,128)(2,1)}, bf16[8,112,384]{2,1,0:T(8,128)(2,1)S(1)}, u32[]{:S(2)}, u32[]{:S(2)}) collective-permute-start(bf16[8,112,384]{2,1,0:T(8,128)(2,1)} %get-tuple-element.247), channel_id=1, source_target_pairs={{0,1},{1,0},{2,3},{3,2},{4,5},{5,4},{6,7},{7,6},{8,9},{9,8},{10,11... | collective-permute-start | bytes 2064392 | tf_op jit(solution)/shard_map/ppermute | solution.py:55
  319.8 9.2 %collective-permute-start.43 = (bf16[96,768]{1,0:T(8,128)(2,1)S(1)}, bf16[96,768]{1,0:T(8,128)(2,1)S(1)}, u32[]{:S(2)}, u32[]{:S(2)}) collective-permute-start(bf16[96,768]{1,0:T(8,128)(2,1)S(1)} %get-tuple-element.280), channel_id=1, source_target_pairs={{0,16},{4,20},{8,24},{12,28},{16,0},{20,4},{24,8},{28,12},{1,17},{... | collective-permute-start | bytes 442376 | tf_op jit(solution)/shard_map/ppermute | solution.py:55
  320.9 23.8 %collective-permute-start.48 = (bf16[4,96,384]{2,1,0:T(8,128)(2,1)S(1)}, bf16[4,96,384]{2,1,0:T(8,128)(2,1)S(1)}, u32[]{:S(2)}, u32[]{:S(2)}) collective-permute-start(bf16[4,96,384]{2,1,0:T(8,128)(2,1)S(1)} %add_convert_fusion.10), channel_id=1, source_target_pairs={{0,4},{4,0},{8,12},{12,8},{16,20},{20,16},{24,28},{28,24},{1,5},{5... | collective-permute-start | bytes 884744 | tf_op jit(solution)/shard_map/ppermute | solution.py:55
  332.0 16.3 %collective-permute-start.54 = (bf16[4,112,384]{2,1,0:T(8,128)(2,1)}, bf16[4,112,384]{2,1,0:T(8,128)(2,1)S(1)}, u32[]{:S(2)}, u32[]{:S(2)}) collective-permute-start(bf16[4,112,384]{2,1,0:T(8,128)(2,1)} %sum_table.4), channel_id=1, source_target_pairs={{0,4},{4,0},{8,12},{12,8},{16,20},{20,16},{24,28},{28,24},{1,5},{5... | collective-permute-start | bytes 1032200 | tf_op jit(solution)/shard_map/ppermute | solution.py:55
  344.6 22.7 %collective-permute-start.40 = (bf16[2,256,768]{2,1,0:T(8,128)(2,1)}, bf16[2,256,768]{2,1,0:T(8,128)(2,1)S(1)}, u32[]{:S(2)}, u32[]{:S(2)}) collective-permute-start(bf16[2,256,768]{2,1,0:T(8,128)(2,1)} %get-tuple-element.253), channel_id=1, source_target_pairs={{0,1},{1,0},{2,3},{3,2},{4,5},{5,4},{6,7},{7,6},{8,9},{9,8},{10,11... | collective-permute-start | bytes 2359304 | tf_op jit(solution)/shard_map/ppermute | solution.py:55
  345.8 9.7 %collective-permute-start.51 = (bf16[96,384]{1,0:T(8,128)(2,1)S(1)}, bf16[96,384]{1,0:T(8,128)(2,1)S(1)}, u32[]{:S(2)}, u32[]{:S(2)}) collective-permute-start(bf16[96,384]{1,0:T(8,128)(2,1)S(1)} %get-tuple-element.286), channel_id=1, source_target_pairs={{0,24},{4,28},{8,16},{12,20},{16,8},{20,12},{24,0},{28,4},{1,25},{... | collective-permute-start | bytes 221192 | tf_op jit(solution)/shard_map/ppermute | solution.py:55
  363.8 10.8 %collective-permute-start.52 = (bf16[96,384]{1,0:T(8,128)(2,1)S(1)}, bf16[96,384]{1,0:T(8,128)(2,1)S(1)}, u32[]{:S(2)}, u32[]{:S(2)}) collective-permute-start(bf16[96,384]{1,0:T(8,128)(2,1)S(1)} %fusion.24), channel_id=1, source_target_pairs={{0,2},{1,3},{2,0},{3,1},{4,6},{5,7},{6,4},{7,5},{8,10},{9,11},{10,... | collective-permute-start | bytes 221192 | tf_op jit(solution)/shard_map/ppermute | solution.py:55
  364.9 20.3 %collective-permute-start.39 = (bf16[2,256,768]{2,1,0:T(8,128)(2,1)}, bf16[2,256,768]{2,1,0:T(8,128)(2,1)S(1)}, u32[]{:S(2)}, u32[]{:S(2)}) collective-permute-start(bf16[2,256,768]{2,1,0:T(8,128)(2,1)} %get-tuple-element.251), channel_id=1, source_target_pairs={{0,1},{1,0},{2,3},{3,2},{4,5},{5,4},{6,7},{7,6},{8,9},{9,8},{10,11... | collective-permute-start | bytes 2359304 | tf_op jit(solution)/shard_map/ppermute | solution.py:55
  369.2 19.6 %collective-permute-start.41 = (bf16[2,256,768]{2,1,0:T(8,128)(2,1)}, bf16[2,256,768]{2,1,0:T(8,128)(2,1)S(1)}, u32[]{:S(2)}, u32[]{:S(2)}) collective-permute-start(bf16[2,256,768]{2,1,0:T(8,128)(2,1)} %add_convert_fusion), channel_id=1, source_target_pairs={{0,2},{1,3},{2,0},{3,1},{4,6},{5,7},{6,4},{7,5},{8,10},{9,11},{10,... | collective-permute-start | bytes 2359304 | tf_op jit(solution)/shard_map/ppermute | solution.py:55
  (51 other events, 357.8 us)
